TPU v7x, 512 devices: a whole 4x8x8 slice. The times are simulated.
512 devices in a mesh: node: 32 (over x, y_lo, core), local: 16 (over z, y_hi).
Axes of the slice: x: 4, y: 8 (y_hi: 2, y_lo: 4; y = y_hi * 4 + y_lo), z: 8, core: 2. Of those that a mesh axis runs over, the one named last changes fastest.
Arguments:
- hidden: bfloat16 [65536, 5120], P(('node', 'local')), may hold values from -6 to 6
- gain: float32 [5120], replicated, may hold values from 0.1 to 1.9
- cotangent: bfloat16 [65536, 128], P(('node', 'local')), may hold values from -6 to 6
- weight: bfloat16 [5120, 128], P('local'), may hold values from -0.078125 to 0.078125
- momentum: float32 [32, 5120, 128], P('node', 'local'), may hold values from -1536 to 1536
- indices: int32 [160, 32], P('local'), may hold values from 0 to 4095, as said below
Outputs:
- new_weight: bfloat16 [5120, 128], replicated
- new_momentum: float32 [32, 5120, 128], P('node', 'local')
- input_grad: bfloat16 [65536, 5120], P(('node', 'local'))
Inputs may be any that keep to these rules, and one draw needn't show every extreme that they name: `indices`: each row lists 32 different positions in a block, as row * 64 + column.
All inputs are finite; a program needn't handle non-finite values.
Results may differ from a plain program's by a relative error of at most 0.0006.
Values may be sent and summed in bfloat16 or wider, within the bound.
No kernel may reach another device: no remote copies, remote signals or barrier semaphores. Data moves between devices by JAX's collectives and lax.ppermute only.
A program may use at most 64 MiB of HBM per device.

v0:
```python
import jax
import jax.numpy as jnp
from jax import lax
from jax.sharding import PartitionSpec as P

epsilon = 1e-06
decay_rate = 0.9
learn_rate = 0.01


def dct_table(side):
    freq = jnp.arange(side, dtype=jnp.float32)[:, None]
    place = jnp.arange(side, dtype=jnp.float32)[None, :]
    wave = jnp.cos(jnp.pi * (2.0 * place + 1.0) * freq / (2.0 * side))
    norm_row = jnp.where(freq == 0.0, jnp.sqrt(1.0 / side), jnp.sqrt(2.0 / side))
    return wave * norm_row


def forward(field, table):
    side = table.shape[0]
    blocks = field.reshape(field.shape[0] // side, side, field.shape[1] // side, side)
    spec = jnp.einsum("kn,rncm,lm->rckl", table, blocks, table, precision=lax.Precision.HIGHEST)
    return spec.reshape(-1, side * side)


def inverse(flat, height, breadth, table):
    side = table.shape[0]
    spec = flat.reshape(height // side, breadth // side, side, side)
    field = jnp.einsum("kn,rckl,lm->rncm", table, spec, table, precision=lax.Precision.HIGHEST)
    return field.reshape(height, breadth)


def spread(values, indices, side):
    empty = jnp.zeros((indices.shape[0], side * side), jnp.float32)
    rows_at = jnp.arange(indices.shape[0], dtype=jnp.int32)[:, None]
    return empty.at[rows_at, indices].set(values)


def on_device(hidden, gain, cotangent, weight, momentum, indices):
    side = 64
    table = dct_table(side)
    head = cotangent.shape[1]
    own_rows = weight.shape[0]
    nodes = lax.axis_size("node")
    wide = hidden.astype(jnp.float32)
    scale = lax.rsqrt(jnp.mean(wide * wide, axis=1, keepdims=True) + epsilon)
    normed = (wide * scale * gain).astype(jnp.bfloat16)
    dnormed = lax.dot_general(
        cotangent,
        lax.all_gather(weight, "local", axis=0, tiled=True),
        (((1,), (1,)), ((), ())),
        preferred_element_type=jnp.float32,
    )
    gained = gain * dnormed
    back = scale * gained - wide * scale**3 * jnp.mean(wide * gained, axis=1, keepdims=True)
    input_grad = back.astype(jnp.bfloat16)
    grad_rows = lax.psum_scatter(
        lax.dot_general(
            normed, cotangent, (((0,), (0,)), ((), ())), preferred_element_type=jnp.float32
        ),
        "local",
        scatter_dimension=0,
        tiled=True,
    )
    middle = decay_rate * momentum[0] + grad_rows
    spectrum = forward(middle, table)
    picked = jnp.take_along_axis(spectrum, indices, axis=1)
    sent = inverse(spread(picked, indices, side), own_rows, head, table)
    new_momentum = (middle - sent)[None]
    every = lax.all_gather(picked[None], "node", axis=0, tiled=True)
    total = jnp.sum(every, axis=0) / nodes
    field = inverse(spread(total, indices, side), own_rows, head, table)
    fresh = (weight.astype(jnp.float32) - learn_rate * jnp.tanh(field)).astype(jnp.bfloat16)
    new_weight = lax.all_gather(fresh, "local", axis=0, tiled=True)
    return (new_weight, new_momentum, input_grad)


def solution(mesh):
    return jax.shard_map(
        on_device,
        mesh=mesh,
        in_specs=(
            P(("node", "local"), None),
            P(),
            P(("node", "local"), None),
            P("local", None),
            P("node", "local", None),
            P("local", None),
        ),
        out_specs=(P(), P("node", "local", None), P(("node", "local"), None)),
        check_vma=False,
    )
```

profile of v0, /device:TPU:6, one launch (start us, length us, event | category | flops | bytes accessed | tf_op | source)
XLA Modules:
  0.0 505.7 jit_solution(3284075454267154719)
XLA Ops:
  7.2 0.7 all-gather.7.cloned.1.call-update
  8.0 101.0 %all-gather.7.cloned.1.call-done = bf16[5120,128]{1,0:T(8,128)(2,1)} async-done(((bf16[320,128]{1,0:T(8,128)(2,1)}), bf16[5120,128]{1,0:T(8,128)(2,1)}) %all-gather.7.cloned.1.call-update) | async-done | bytes 1310736 | tf_op jit(solution)/shard_map/all_gather | solution.py:50
  109.0 3.9 fusion.6
  113.0 2.1 fusion.7
  115.4 227.2 %reduce-scatter.2.cloned.1.call-done = f32[320,128]{1,0:T(8,128)} async-done(((f32[5120,128]{1,0:T(8,128)}), f32[320,128]{1,0:T(8,128)}) %reduce-scatter.2.cloned.1.call-update) | async-done | bytes 163856 | tf_op jit(solution)/shard_map/reduce_scatter | solution.py:57
  342.6 0.9 bitcast_add_fusion
  343.5 0.2 reshape.75
  343.7 0.6 fusion.13
  344.3 0.5 fusion.21
  345.0 3.0 gather_fusion
  348.1 36.4 %all-gather.1 = f32[32,10,32]{2,1,0:T(8,128)S(1)} all-gather(f32[1,10,32]{2,1,0:T(8,128)S(1)} %bitcast.49), channel_id=2, replica_groups=mesh['node'=32,'local'=16] {'node'}, dimensions={0}, use_global_device_ids=true | all-gather | bytes 42240 | tf_op jit(solution)/shard_map/all_gather | solution.py:70
  384.6 16.8 %scatter_fusion = f32[10,4096]{1,0:T(8,128)S(1)} fusion(f32[10,4096]{1,0:T(8,128)S(1)} %broadcast.82.clone, s32[320]{0:T(512)S(1)} %reshape.86, f32[320]{0:T(512)S(1)} %reshape.88), kind=kCustom, calls=%fused_computation.1 | custom fusion | bytes 6400 | tf_op jit(solution)/shard_map/scatter | solution.py:36
  401.6 0.6 fusion.19
  402.2 0.5 fusion.12
  402.7 0.3 copy.16
  403.2 0.7 subtract_convert_fusion
  403.9 3.5 fusion.5
  407.5 16.8 %scatter_fusion.1 = f32[10,4096]{1,0:T(8,128)S(1)} fusion(f32[10,4096]{1,0:T(8,128)S(1)} %broadcast.82.clone.1, s32[320]{0:T(512)S(1)} %reshape.86, f32[320]{0:T(512)S(1)} %reshape.94), kind=kCustom, calls=%fused_computation.2 | custom fusion | bytes 6400 | tf_op jit(solution)/shard_map/scatter | solution.py:36
  424.5 0.6 fusion.16
  425.1 0.5 convolution_bitcast_fusion
  425.6 0.3 copy.19
  426.1 0.7 subtract_bitcast_fusion
  426.8 69.9 %all-gather.5.cloned.1.call-done = bf16[5120,128]{1,0:T(8,128)(2,1)} async-done(((bf16[320,128]{1,0:T(8,128)(2,1)}), bf16[5120,128]{1,0:T(8,128)(2,1)}) %all-gather.5.cloned.1.call-update) | async-done | bytes 1310736 | tf_op jit(solution)/shard_map/all_gather | solution.py:74
  496.7 2.5 copy.32
  (36 shorter events, 1.5 us)
Async XLA Ops:
  7.2 101.9 %copy-start = (bf16[128,128]{1,0:T(8,128)(2,1)S(1)}, bf16[128,128]{1,0:T(8,128)(2,1)}, u32[]{:S(2)}) copy-start(bf16[128,128]{1,0:T(8,128)(2,1)} %param.8) | copy-start | bytes 98308
  7.2 101.8 %all-gather.7.cloned.1.call-start = ((), (), s32[]{:S(2)}) async-start(), calls=%async_computation.3 | async-start | bytes 1392640 | tf_op jit(solution)/shard_map/all_gather | solution.py:50
  7.9 105.0 %copy-start.1 = (bf16[128,5120]{1,0:T(8,128)(2,1)S(1)}, bf16[128,5120]{1,0:T(8,128)(2,1)}, u32[]{:S(2)}) copy-start(bf16[128,5120]{1,0:T(8,128)(2,1)} %param.6) | copy-start | bytes 3932164
  7.9 105.0 %copy-start.4 = (f32[5120]{0:T(1024)S(1)}, f32[5120]{0:T(1024)}, u32[]{:S(2)}) copy-start(f32[5120]{0:T(1024)} %param.7) | copy-start | bytes 61444
  7.9 334.6 %reduce-scatter.2.cloned.1.call-start = ((), (), s32[]{:S(2)}) async-start(), calls=%async_computation.1 | async-start | bytes 2785280 | tf_op jit(solution)/shard_map/reduce_scatter | solution.py:57
  112.9 2.2 copy-start.5
  113.0 229.6 %copy-start.3 = (f32[1,320,128]{2,1,0:T(8,128)S(1)}, f32[1,320,128]{2,1,0:T(8,128)}, u32[]{:S(2)}) copy-start(f32[1,320,128]{2,1,0:T(8,128)} %param.10) | copy-start | bytes 491524
  115.1 381.6 %all-gather.5.cloned.1.call-start = ((), (), s32[]{:S(2)}) async-start(), calls=%async_computation.2 | async-start | bytes 1392640 | tf_op jit(solution)/shard_map/all_gather | solution.py:74
  401.4 1.8 copy-start.2
Sparse Core Ops, SparseCore 0:
  11.2 97.7 all-gather.6
  115.2 227.2 reduce-scatter.1
  404.0 92.6 all-gather.4
where the time goes:
time: 508 us; the launch traced here: 506 us
  waiting for transfers between devices  399 us (79%)
  local copies, waits for them, and re-layouts  41.1 us (8%)
  blocking collectives  36.4 us (7%)
  between operations  14 us (3%)
  matrix products  9.43 us (2%)
  other arithmetic  5.82 us (1%)
    reduce_scatter x1, waiting for transfers between devices, on_device(): lax.psum_scatter(lax.dot_general(normed, cotangent, (((0,), (0,)), ((), (...  227 us
    all_gather x1, waiting for transfers between devices, on_device(): lax.all_gather(weight, 'local', axis=0, tiled=True)  101 us
    all_gather x1, waiting for transfers between devices, on_device(): new_weight = lax.all_gather(fresh, 'local', axis=0, tiled=True)  69.9 us
    all_gather x1, blocking collectives, on_device(): every = lax.all_gather(picked[None], 'node', axis=0, tiled=True)  36.4 us
    scatter x2, local copies, waits for them, and re-layouts, spread(): return empty.at[rows_at, indices].set(values)  33.7 us
  transfers between devices with their start and end apart: 3, of which 3 were waited for; matrix products, arithmetic and copies ran while one was open for 5% of the time, Pallas kernels for 0%

commit v1 on v0

v1 whole, which is shorter than its diff:
```python
import functools

import jax
import jax.numpy as jnp
from jax import lax
from jax.experimental import pallas as pl
from jax.experimental.pallas import tpu as pltpu
from jax.sharding import PartitionSpec as P

epsilon = 1e-06
decay_rate = 0.9
learn_rate = 0.01
side = 64
pair = 128
f32 = jnp.float32
bf16 = jnp.bfloat16

z_groups = [[2 * z + h for z in range(8)] for h in range(2)]
x_groups = [[8 * x + r for x in range(4)] for r in range(8)]
core_groups = [[2 * i, 2 * i + 1] for i in range(16)]


def whole_mesh(move):
    def index(x, y, z, core):
        return ((x * 4 + y % 4) * 2 + core) * 16 + z * 2 + y // 4

    places = [(x, y, z, c) for x in range(4) for y in range(8) for z in range(8) for c in range(2)]
    return [(index(*place), index(*move(*place))) for place in places]


def hop(value, move):
    return lax.ppermute(value, ("node", "local"), whole_mesh(move))


def dct_table():
    freq = jnp.arange(side, dtype=f32)[:, None]
    place = jnp.arange(side, dtype=f32)[None, :]
    wave = jnp.cos(jnp.pi * (2.0 * place + 1.0) * freq / (2.0 * side))
    norm_row = jnp.where(freq == 0.0, jnp.sqrt(1.0 / side), jnp.sqrt(2.0 / side))
    return wave * norm_row


def split2(value):
    high = value.astype(bf16)
    return high, (value - high.astype(f32)).astype(bf16)


def pair_table():
    turned = dct_table().T
    empty = jnp.zeros_like(turned)
    wide = jnp.block([[turned, empty], [empty, turned]])
    high = lax.reduce_precision(wide, exponent_bits=8, mantissa_bits=7)
    return jnp.concatenate([high, wide - high], axis=0).astype(bf16)


def dot(a, b, dims):
    return lax.dot_general(a, b, (dims, ((), ())), preferred_element_type=f32)


def waves(table, spots):
    at = lax.broadcasted_iota(jnp.int32, (pair, pair), 0)
    chosen = jnp.where(at == spots, 1.0, 0.0).astype(bf16)
    both = dot(table, chosen, ((1,), (0,)))
    return both[:pair].astype(bf16), both[pair:].astype(bf16)


def front_kernel(hidden_ref, gain_ref, cot_ref, message_ref, high_ref, low_ref):
    wide = hidden_ref[...].astype(f32)
    features = wide.shape[1]
    owners, tall, _ = message_ref.shape
    rows = features // owners
    scale = lax.rsqrt(jnp.sum(wide * wide, axis=1, keepdims=True) * (1.0 / features) + epsilon)
    cot = cot_ref[...]
    for piece in range(owners // 2):
        at = slice(piece * 2 * rows, (piece + 1) * 2 * rows)
        normed = (hidden_ref[:, at].astype(f32) * scale * gain_ref[:, at]).astype(bf16)
        turned = dot(cot, normed, ((0,), (0,)))
        high, low = split2(turned)
        high_ref[:, at] = high
        low_ref[:, at] = low
        term = dot(normed, cot, ((0,), (0,)))
        for half in range(2):
            own = term[half * rows : (half + 1) * rows]
            top = jnp.max(jnp.abs(own), axis=0, keepdims=True)
            power = jnp.ceil(jnp.log2(top * (1.0 / 32000.0)))
            power = jnp.clip(power, -120.0, 120.0)
            whole = jnp.round(own * jnp.exp2(-power)).astype(jnp.int32)
            message_ref[2 * piece + half, 0:rows, :] = whole.astype(jnp.int16)
            message_ref[2 * piece + half, rows:tall, :] = jnp.broadcast_to(
                power.astype(jnp.int32), (tall - rows, pair)
            ).astype(jnp.int16)


def front(hidden, gain, cot, owners):
    tokens, features = hidden.shape
    rows = features // owners
    return pl.pallas_call(
        front_kernel,
        out_shape=(
            jax.ShapeDtypeStruct((owners, rows + 16, pair), jnp.int16),
            jax.ShapeDtypeStruct((pair, features), bf16),
            jax.ShapeDtypeStruct((pair, features), bf16),
        ),
        compiler_params=pltpu.CompilerParams(vmem_limit_bytes=40 * 2**20),
        name="front",
    )(hidden, gain, cot)


def own_kernel(table_ref, row_ref, col_ref, momentum_ref, row_waves_ref, col_waves_ref, picked_ref):
    for q in range(row_ref.shape[0]):
        row_high, row_low = waves(table_ref[...], row_ref[q : q + 1, :])
        col_high, col_low = waves(table_ref[...], col_ref[q : q + 1, :])
        row_waves = row_high.astype(f32) + row_low.astype(f32)
        col_waves = col_high.astype(f32) + col_low.astype(f32)
        row_waves_ref[q] = row_waves
        col_waves_ref[q] = col_waves
        tile = decay_rate * momentum_ref[q * pair : (q + 1) * pair, :]
        half = lax.dot_general(
            tile, row_waves, (((0,), (0,)), ((), ())), precision=lax.Precision.HIGHEST, preferred_element_type=f32
        )
        picked_ref[q : q + 1, :] = jnp.sum(half * col_waves, axis=0, keepdims=True)


def own_waves(table, rows, cols, momentum):
    tiles = rows.shape[0]
    return pl.pallas_call(
        own_kernel,
        out_shape=(
            jax.ShapeDtypeStruct((tiles, pair, pair), f32),
            jax.ShapeDtypeStruct((tiles, pair, pair), f32),
            jax.ShapeDtypeStruct((tiles, pair), f32),
        ),
        name="own_waves",
    )(table, rows, cols, momentum)


def pick_kernel(table_ref, row_ref, col_ref, high_ref, low_ref, row_waves_ref, col_waves_ref, picked_ref):
    for q in range(row_ref.shape[0]):
        row_high, row_low = waves(table_ref[...], row_ref[q : q + 1, :])
        col_high, col_low = waves(table_ref[...], col_ref[q : q + 1, :])
        row_waves_ref[q, 0:pair, :] = row_high
        row_waves_ref[q, pair:, :] = row_low
        col_waves_ref[q, 0:pair, :] = col_high
        col_waves_ref[q, pair:, :] = col_low
        at = slice(q * pair, (q + 1) * pair)
        high = high_ref[:, at]
        both = jnp.concatenate([high, low_ref[:, at]], axis=1)
        half = dot(both, jnp.concatenate([row_high, row_high], axis=0), ((1,), (0,)))
        half += dot(high, row_low, ((1,), (0,)))
        picked_ref[q : q + 1, :] = jnp.sum(
            half * (col_high.astype(f32) + col_low.astype(f32)), axis=0, keepdims=True
        )


def pick(table, rows, cols, high, low):
    tiles = rows.shape[0]
    return pl.pallas_call(
        pick_kernel,
        out_shape=(
            jax.ShapeDtypeStruct((tiles, 2 * pair, pair), bf16),
            jax.ShapeDtypeStruct((tiles, 2 * pair, pair), bf16),
            jax.ShapeDtypeStruct((tiles, pair), f32),
        ),
        compiler_params=pltpu.CompilerParams(vmem_limit_bytes=40 * 2**20),
        name="pick",
    )(table, rows, cols, high, low)


def momentum_kernel(message_ref, momentum_ref, row_waves_ref, col_waves_ref, out_ref, mid_ref):
    owners, tall, _ = message_ref.shape
    rows = out_ref.shape[0]
    total = decay_rate * momentum_ref[...]
    for source in range(owners):
        power = message_ref[source, rows:tall, :].astype(jnp.int32)[0:1, :].astype(f32)
        total += message_ref[source, 0:rows, :].astype(jnp.int32).astype(f32) * jnp.exp2(power)
    mid_ref[0:rows, :] = total
    mid_ref[rows:, :] = jnp.zeros((mid_ref.shape[0] - rows, pair), f32)
    highest = functools.partial(lax.dot_general, precision=lax.Precision.HIGHEST, preferred_element_type=f32)
    for q in range(row_waves_ref.shape[0]):
        tile = mid_ref[q * pair : (q + 1) * pair, :]
        half = highest(tile, row_waves_ref[q], (((0,), (0,)), ((), ())))
        picked = jnp.sum(half * col_waves_ref[q], axis=0, keepdims=True)
        sent = highest(row_waves_ref[q], picked * col_waves_ref[q], (((1,), (1,)), ((), ())))
        left = min(pair, rows - q * pair)
        out_ref[q * pair : q * pair + left, :] = (tile - sent)[:left]


def new_momentum_of(message, momentum, row_waves, col_waves):
    tiles = row_waves.shape[0]
    return pl.pallas_call(
        momentum_kernel,
        out_shape=jax.ShapeDtypeStruct(momentum.shape, f32),
        scratch_shapes=[pltpu.VMEM((tiles * pair, pair), f32)],
        compiler_params=pltpu.CompilerParams(vmem_limit_bytes=40 * 2**20),
        name="momentum_step",
    )(message, momentum, row_waves, col_waves)


def weight_kernel(nodes, total_ref, row_waves_ref, col_waves_ref, weight_ref, out_ref):
    for q in range(total_ref.shape[0]):
        at = slice(q * pair, (q + 1) * pair)
        mean = total_ref[q : q + 1, :] / nodes
        col_waves = col_waves_ref[q, 0:pair, :].astype(f32) + col_waves_ref[q, pair:, :].astype(f32)
        high, low = split2(mean * col_waves)
        row_high, row_low = row_waves_ref[q, 0:pair, :], row_waves_ref[q, pair:, :]
        field = dot(
            jnp.concatenate([row_high, row_low], axis=1), jnp.concatenate([high, high], axis=1), ((1,), (1,))
        )
        field += dot(row_high, low, ((1,), (1,)))
        out_ref[at, :] = (weight_ref[at, :].astype(f32) - learn_rate * jnp.tanh(field)).astype(bf16)


def new_weight_of(total, row_waves, col_waves, weight, nodes):
    return pl.pallas_call(
        functools.partial(weight_kernel, nodes),
        out_shape=jax.ShapeDtypeStruct(weight.shape, bf16),
        compiler_params=pltpu.CompilerParams(vmem_limit_bytes=40 * 2**20),
        name="weight_step",
    )(total, row_waves, col_waves, weight)


def on_device(hidden, gain, cotangent, weight, momentum, indices):
    nodes, owners = lax.axis_size("node"), lax.axis_size("local")
    node, local = lax.axis_index("node"), lax.axis_index("local")
    features = hidden.shape[1]
    own_rows, head = weight.shape
    table = pair_table()
    blocks = indices.size
    row_of, col_of = indices // side, indices % side

    eighth = own_rows // 8
    part = (node // 8) * 2 + node % 2
    with jax.named_scope("weight_part"):
        piece = lax.dynamic_slice_in_dim(weight, part * eighth, eighth, axis=0)
        spots = jnp.concatenate([row_of.reshape(-1), col_of.reshape(-1)]).astype(bf16).reshape(-1, head)
        spots = jnp.pad(spots, ((0, 8 - spots.shape[0]), (0, 0)))
        piece = jnp.concatenate([piece, spots], axis=0)
    with jax.named_scope("weight_over_y"):
        other = hop(piece, lambda x, y, z, c: (x, (y + 4) % 8, z, c))
        upper = local % 2
        two = jnp.where(upper == 0, jnp.stack([piece, other]), jnp.stack([other, piece]))
    with jax.named_scope("weight_over_z"):
        gathered = lax.all_to_all(
            jnp.broadcast_to(two[None], (8,) + two.shape), "local", 0, 0, axis_index_groups=z_groups
        )
        gathered = gathered.reshape(owners, eighth + 8, head)

    message, high, low = front(hidden, gain[None, :], cotangent, owners)
    with jax.named_scope("gradient_exchange"):
        arrived = lax.all_to_all(message, "local", 0, 0)

    spare = (-blocks) % pair
    tiles = (blocks + spare) // pair
    own_at = jnp.pad(indices.reshape(-1), (0, spare)).reshape(tiles, pair)
    quarter = 2 * side * (jnp.arange(pair, dtype=jnp.int32) // side)[None, :]
    block_in = (jnp.arange(pair, dtype=jnp.int32) // 32)[None, :]
    place = lambda rows, cols: (rows + side * (block_in // 2), cols + side * (block_in % 2))
    own_row, own_col = place(own_at // side, own_at % side)
    own_momentum = momentum[0]
    padded = jnp.pad(own_momentum, ((0, tiles * pair - own_rows), (0, 0)))
    row_waves, col_waves, decayed = own_waves(table, own_row, own_col, padded)
    decayed = lax.dynamic_update_slice(
        jnp.zeros((owners * blocks,), f32), decayed.reshape(-1)[:blocks], (local * blocks,)
    ).reshape(-1, pair)

    spots = gathered[:, eighth:, :].reshape(owners, -1)[:, : 2 * blocks].astype(jnp.int32)
    all_row, all_col = place(spots[:, :blocks].reshape(-1, pair), spots[:, blocks:].reshape(-1, pair))
    all_row_waves, all_col_waves, picked = pick(table, all_row, all_col, high, low)
    with jax.named_scope("coefficients"):
        total = picked + decayed
        total = jnp.sum(lax.all_gather(total, "node", axis_index_groups=core_groups), axis=0)
        total = total + hop(total, lambda x, y, z, c: (x, y ^ 1, z, c))
        total = total + hop(total, lambda x, y, z, c: (x, y ^ 2, z, c))
        total = total + hop(total, lambda x, y, z, c: (x, y ^ 4, z, c))
        spread = lambda v, n: jnp.broadcast_to(v[None], (n,) + v.shape)
        total = jnp.sum(lax.all_to_all(spread(total, 8), "local", 0, 0, axis_index_groups=z_groups), axis=0)
        total = jnp.sum(lax.all_to_all(spread(total, 4), "node", 0, 0, axis_index_groups=x_groups), axis=0)

    with jax.named_scope("weight_over_x"):
        quarter = gathered[:, :eighth, :]
        half = lax.all_to_all(spread(quarter, 4), "node", 0, 0, axis_index_groups=x_groups)
    with jax.named_scope("weight_over_core"):
        full = lax.all_gather(half, "node", axis_index_groups=core_groups)
        full = jnp.transpose(full, (2, 1, 0, 3, 4)).reshape(features, head)

    wide = hidden.astype(f32)
    scale = lax.rsqrt(jnp.mean(wide * wide, axis=1, keepdims=True) + epsilon)
    gained = gain * dot(cotangent, full, ((1,), (1,)))
    back = scale * gained - wide * scale**3 * jnp.mean(wide * gained, axis=1, keepdims=True)
    input_grad = back.astype(bf16)

    new_momentum = new_momentum_of(arrived, own_momentum, row_waves, col_waves)[None]
    new_weight = new_weight_of(total, all_row_waves, all_col_waves, full, nodes)
    return (new_weight, new_momentum, input_grad)


def solution(mesh):
    return jax.shard_map(
        on_device,
        mesh=mesh,
        in_specs=(
            P(("node", "local"), None),
            P(),
            P(("node", "local"), None),
            P("local", None),
            P("node", "local", None),
            P("local", None),
        ),
        out_specs=(P(), P("node", "local", None), P(("node", "local"), None)),
        check_vma=False,
    )
```

time: 508 us -> 164 us (0.32)
  the two profiles are of different devices: /device:TPU:6 before, /device:TPU:40 now
where the time goes in v1:
time: 164 us; the launch traced here: 163 us
  waiting for transfers between devices  45.5 us (28%)
  starting transfers between devices  33.5 us (20%)
  blocking collectives  27.6 us (17%)
  local copies, waits for them, and re-layouts  22 us (13%)
  between operations  14.3 us (9%)
  Pallas kernels  13.7 us (8%)
  other arithmetic  4.02 us (2%)
  matrix products  2.39 us (1%)
    all_to_all x1, waiting for transfers between devices, on_device(): arrived = lax.all_to_all(message, 'local', 0, 0)  26.3 us
    ppermute x4, waiting for transfers between devices, hop(): return lax.ppermute(value, ('node', 'local'), whole_mesh(move))  18.1 us
    all_to_all x1, blocking collectives, on_device(): lax.all_to_all(spread(total, 8), 'local', 0, 0, axis_index_groups=z_groups)  16.2 us
    unnamed x39, local copies, waits for them, and re-layouts  15.2 us
    ppermute x4, starting transfers between devices, hop(): return lax.ppermute(value, ('node', 'local'), whole_mesh(move))  11.7 us
    all_to_all x1, starting transfers between devices, on_device(): lax.all_to_all(jnp.broadcast_to(two[None], (8,) + two.shape), 'local', 0,...  10.3 us
    all_to_all x1, blocking collectives, on_device(): lax.all_to_all(spread(total, 4), 'node', 0, 0, axis_index_groups=x_groups)  9.58 us
    all_to_all x1, starting transfers between devices, on_device(): arrived = lax.all_to_all(message, 'local', 0, 0)  7.22 us
  transfers between devices with their start and end apart: 8, of which 6 were waited for; matrix products, arithmetic and copies ran while one was open for 9% of the time, Pallas kernels for 7%

profile of v1, /device:TPU:40, one launch (start us, length us, event | category | flops | bytes accessed | tf_op | source)
XLA Modules:
  0.0 163.1 jit_solution(8440613263187306671)
XLA Ops:
  8.2 2.9 %collective-permute-start = (bf16[48,128]{1,0:T(8,128)(2,1)S(1)}, bf16[48,128]{1,0:T(8,128)(2,1)S(1)}, u32[]{:S(2)}, u32[]{:S(2)}) collective-permute-start(bf16[48,128]{1,0:T(8,128)(2,1)S(1)} %get-tuple-element.40), channel_id=1, source_target_pairs={{0,1},{16,17},{2,3},{18,19},{4,5},{20,21},{6,7},{22,23},{8,9},{24,... | collective-permute-start | bytes 36872 | tf_op jit(solution)/shard_map/weight_over_y/ppermute | solution.py:32
  12.7 5.0 %collective-permute-done = bf16[48,128]{1,0:T(8,128)(2,1)S(1)} collective-permute-done((bf16[48,128]{1,0:T(8,128)(2,1)S(1)}, bf16[48,128]{1,0:T(8,128)(2,1)S(1)}, u32[]{:S(2)}, u32[]{:S(2)}) %collective-permute-start) | collective-permute-done | bytes 12320 | tf_op jit(solution)/shard_map/weight_over_y/ppermute | solution.py:32
  18.4 10.3 %all-to-all-start = ((bf16[8,2,48,128]{3,2,1,0:T(8,128)(2,1)}), bf16[8,2,48,128]{3,2,1,0:T(8,128)(2,1)S(1)}, u32[]{:S(2)}, u32[]{:S(2)}) async-start(bf16[8,2,48,128]{3,2,1,0:T(8,128)(2,1)} %broadcast_in_dim.24), calls=%async_computation | async-start | bytes 393216 | tf_op jit(solution)/shard_map/weight_over_z/all_to_all | solution.py:243
  28.8 1.6 pad.16.momentum_ref
  36.4 2.3 %own_waves.1 = (f32[3,128,128]{2,1,0:T(8,128)}, f32[3,128,128]{2,1,0:T(8,128)}, f32[3,128]{1,0:T(4,128)}) custom-call(bf16[256,128]{1,0:T(8,128)(2,1)} %pad_maximum_fusion.table_ref, s32[3,128]{1,0:T(4,128)} %get-tuple-element.44.row_ref, s32[3,128]{1,0:T(4,128)} %get-tuple-element.43.col_ref, f32[384,128]{1,0:T(8,128)} %pad.16.momentum_ref), custom_call_target="tpu_custom_call" | custom-call | tf_op jit(solution)/shard_map/own_waves/pallas_call | solution.py:126
  40.4 4.3 %all-to-all-start.3 = ((bf16[4,16,40,128]{3,2,1,0:T(8,128)(2,1)}), bf16[4,16,40,128]{3,2,1,0:T(8,128)(2,1)S(1)}, u32[]{:S(2)}, u32[]{:S(2)}) async-start(bf16[4,16,40,128]{3,2,1,0:T(8,128)(2,1)} %broadcast_in_dim.29), calls=%async_computation.3 | async-start | bytes 1310720 | tf_op jit(solution)/shard_map/weight_over_x/all_to_all | solution.py:281
  45.0 5.1 %pick.1 = (bf16[40,256,128]{2,1,0:T(8,128)(2,1)S(1)}, bf16[40,256,128]{2,1,0:T(8,128)(2,1)S(1)}, f32[40,128]{1,0:T(8,128)S(1)}) custom-call(bf16[256,128]{1,0:T(8,128)(2,1)S(1)} %copy-done.9, s32[40,128]{1,0:T(8,128)S(1)} %get-tuple-element.51.row_ref, s32[40,128]{1,0:T(8,128)S(1)} %get-tuple-element.50.col_ref, ...), custom_call_target="tpu_custom_call" | custom-call | tf_op jit(solution)/shard_map/pick/pallas_call | solution.py:157
  55.0 1.8 %all-gather = f32[80,128]{1,0:T(8,128)S(1)} all-gather(f32[40,128]{1,0:T(8,128)S(1)} %bitcast_add_fusion), channel_id=2, replica_groups={{0,16},{32,48},{64,80},{96,112},{128,144},{160,176},{192,208},{224,240}..., dimensions={0}, use_global_device_ids=true | all-gather | bytes 61440 | tf_op jit(solution)/shard_map/coefficients/all_gather | solution.py:271
  56.9 3.3 %collective-permute-start.1 = (f32[40,128]{1,0:T(8,128)S(1)}, f32[40,128]{1,0:T(8,128)S(1)}, u32[]{:S(2)}, u32[]{:S(2)}) collective-permute-start(f32[40,128]{1,0:T(8,128)S(1)} %reduce_sum.45), channel_id=1, source_target_pairs={{0,32},{16,48},{2,34},{18,50},{4,36},{20,52},{6,38},{22,54},{8,40}... | collective-permute-start | bytes 61448 | tf_op jit(solution)/shard_map/coefficients/ppermute | solution.py:32
  60.1 2.4 %collective-permute-done.1 = f32[40,128]{1,0:T(8,128)S(1)} collective-permute-done((f32[40,128]{1,0:T(8,128)S(1)}, f32[40,128]{1,0:T(8,128)S(1)}, u32[]{:S(2)}, u32[]{:S(2)}) %collective-permute-start.1) | collective-permute-done | bytes 20512 | tf_op jit(solution)/shard_map/coefficients/ppermute | solution.py:32
  62.6 2.7 %collective-permute-start.2 = (f32[40,128]{1,0:T(8,128)S(1)}, f32[40,128]{1,0:T(8,128)S(1)}, u32[]{:S(2)}, u32[]{:S(2)}) collective-permute-start(f32[40,128]{1,0:T(8,128)S(1)} %add.160), channel_id=1, source_target_pairs={{0,64},{16,80},{2,66},{18,82},{4,68},{20,84},{6,70},{22,86},{8,72}... | collective-permute-start | bytes 61448 | tf_op jit(solution)/shard_map/coefficients/ppermute | solution.py:32
  65.3 4.0 %collective-permute-done.2 = f32[40,128]{1,0:T(8,128)S(1)} collective-permute-done((f32[40,128]{1,0:T(8,128)S(1)}, f32[40,128]{1,0:T(8,128)S(1)}, u32[]{:S(2)}, u32[]{:S(2)}) %collective-permute-start.2) | collective-permute-done | bytes 20512 | tf_op jit(solution)/shard_map/coefficients/ppermute | solution.py:32
  69.2 2.8 %collective-permute-start.3 = (f32[40,128]{1,0:T(8,128)S(1)}, f32[40,128]{1,0:T(8,128)S(1)}, u32[]{:S(2)}, u32[]{:S(2)}) collective-permute-start(f32[40,128]{1,0:T(8,128)S(1)} %add.161), channel_id=1, source_target_pairs={{0,1},{16,17},{2,3},{18,19},{4,5},{20,21},{6,7},{22,23},{8,9},{24,... | collective-permute-start | bytes 61448 | tf_op jit(solution)/shard_map/coefficients/ppermute | solution.py:32
  72.0 6.8 %collective-permute-done.3 = f32[40,128]{1,0:T(8,128)S(1)} collective-permute-done((f32[40,128]{1,0:T(8,128)S(1)}, f32[40,128]{1,0:T(8,128)S(1)}, u32[]{:S(2)}, u32[]{:S(2)}) %collective-permute-start.3) | collective-permute-done | bytes 20512 | tf_op jit(solution)/shard_map/coefficients/ppermute | solution.py:32
  78.8 16.2 %all_to_all.25 = f32[8,40,128]{2,1,0:T(8,128)S(1)} all-to-all(f32[8,40,128]{2,1,0:T(8,128)S(1)} %broadcast_in_dim.27), channel_id=1, replica_groups={{0,2,4,6,8,10,12,14},{1,3,5,7,9,11,13,15},{16,18,20,22,24,26,28,30},{17..., dimensions={0} | all-to-all | bytes 327680 | tf_op jit(solution)/shard_map/coefficients/all_to_all | solution.py:276
  95.0 9.6 %all_to_all.26 = f32[4,40,128]{2,1,0:T(8,128)S(1)} all-to-all(f32[4,40,128]{2,1,0:T(8,128)S(1)} %broadcast_in_dim.28), channel_id=1, replica_groups={{0,128,256,384},{16,144,272,400},{32,160,288,416},{48,176,304,432},{64,..., dimensions={0} | all-to-all | bytes 163840 | tf_op jit(solution)/shard_map/coefficients/all_to_all | solution.py:277
  104.6 7.2 %all-to-all-start.4 = ((s16[16,336,128]{2,1,0:T(8,128)(2,1)}), s16[16,336,128]{2,1,0:T(8,128)(2,1)S(1)}, u32[]{:S(2)}, u32[]{:S(2)}) async-start(s16[16,336,128]{2,1,0:T(8,128)(2,1)} %copy-done.7), calls=%async_computation.4 | async-start | bytes 2752512 | tf_op jit(solution)/shard_map/gradient_exchange/all_to_all | solution.py:250
  115.1 2.4 %fusion.1 = (f32[128]{0:T(128)S(1)}, f32[128]{0:T(128)S(1)}, f32[128,5120]{0,1:T(8,128)S(1)}) fusion(bf16[128,5120]{0,1:T(8,128)(2,1)S(1)} %copy-done.16, bf16[5120,128]{1,0:T(8,128)(2,1)S(1)} %bitcast.47, bf16[128,128]{1,0:T(8,128)(2,1)S(1)} %copy-done.13, f32[5120]{0:T(1024)S(1)} %copy-done.15), kind=kOutput, calls=%fused_computation.5 | convolution fusion | flops 171704064 | bytes 5297152 | tf_op jit(solution)/shard_map/dot_general | solution.py:57
  119.0 2.4 %copy.19 = bf16[128,5120]{1,0:T(8,128)(2,1)} copy(bf16[128,5120]{0,1:T(8,128)(2,1)} %fusion.4) | data formatting | bytes 2621440
  121.5 1.7 %copy-done.4 = bf16[40,256,128]{2,1,0:T(8,128)(2,1)S(1)} copy-done((bf16[40,256,128]{2,1,0:T(8,128)(2,1)S(1)}, bf16[40,256,128]{2,1,0:T(8,128)(2,1)}, u32[]{:S(2)}) %copy-start.4) | copy-done | bytes 2621464
  123.2 1.7 %copy-done.6 = bf16[40,256,128]{2,1,0:T(8,128)(2,1)S(1)} copy-done((bf16[40,256,128]{2,1,0:T(8,128)(2,1)S(1)}, bf16[40,256,128]{2,1,0:T(8,128)(2,1)}, u32[]{:S(2)}) %copy-start.6) | copy-done | bytes 2621464
  124.9 2.8 %weight_step.1 = bf16[5120,128]{1,0:T(8,128)(2,1)} custom-call(f32[40,128]{1,0:T(8,128)S(1)} %reduce_sum.47.total_ref, bf16[40,256,128]{2,1,0:T(8,128)(2,1)S(1)} %copy-done.4, bf16[40,256,128]{2,1,0:T(8,128)(2,1)S(1)} %copy-done.6, bf16[5120,128]{1,0:T(8,128)(2,1)S(1)} %bitcast.48), custom_call_target="tpu_custom_call" | custom-call | tf_op jit(solution)/shard_map/weight_step/pallas_call | solution.py:214
  127.8 26.3 %all-to-all-done.4.message_ref = s16[16,336,128]{2,1,0:T(8,128)(2,1)S(1)} async-done(((s16[16,336,128]{2,1,0:T(8,128)(2,1)}), s16[16,336,128]{2,1,0:T(8,128)(2,1)S(1)}, u32[]{:S(2)}, u32[]{:S(2)}) %all-to-all-start.4) | async-done | bytes 1376288 | tf_op jit(solution)/shard_map/gradient_exchange/all_to_all | solution.py:250
  154.1 2.1 %momentum_step.1 = f32[320,128]{1,0:T(8,128)} custom-call(s16[16,336,128]{2,1,0:T(8,128)(2,1)S(1)} %all-to-all-done.4.message_ref, f32[320,128]{1,0:T(8,128)S(1)} %bitcast.50, f32[3,128,128]{2,1,0:T(8,128)S(1)} %copy-done.10, f32[3,128,128]{2,1,0:T(8,128)S(1)} %copy-done.11), custom_call_target="tpu_custom_call" | custom-call | tf_op jit(solution)/shard_map/momentum_step/pallas_call | solution.py:190
  (80 shorter events, 21.1 us)
Async XLA Ops:
  7.2 1.0 copy-start
  8.2 9.5 %collective-permute-start = (bf16[48,128]{1,0:T(8,128)(2,1)S(1)}, bf16[48,128]{1,0:T(8,128)(2,1)S(1)}, u32[]{:S(2)}, u32[]{:S(2)}) collective-permute-start(bf16[48,128]{1,0:T(8,128)(2,1)S(1)} %get-tuple-element.40), channel_id=1, source_target_pairs={{0,1},{16,17},{2,3},{18,19},{4,5},{20,21},{6,7},{22,23},{8,9},{24,... | collective-permute-start | bytes 36872 | tf_op jit(solution)/shard_map/weight_over_y/ppermute | solution.py:32
  18.4 21.0 %all-to-all-start = ((bf16[8,2,48,128]{3,2,1,0:T(8,128)(2,1)}), bf16[8,2,48,128]{3,2,1,0:T(8,128)(2,1)S(1)}, u32[]{:S(2)}, u32[]{:S(2)}) async-start(bf16[8,2,48,128]{3,2,1,0:T(8,128)(2,1)} %broadcast_in_dim.24), calls=%async_computation | async-start | bytes 393216 | tf_op jit(solution)/shard_map/weight_over_z/all_to_all | solution.py:243
  30.4 1.3 copy-start.1
  34.7 1.1 copy-start.7
  36.4 8.6 %copy-start.9 = (bf16[256,128]{1,0:T(8,128)(2,1)S(1)}, bf16[256,128]{1,0:T(8,128)(2,1)}, u32[]{:S(2)}) copy-start(bf16[256,128]{1,0:T(8,128)(2,1)} %pad_maximum_fusion.table_ref) | copy-start | bytes 196612
  40.4 13.7 %all-to-all-start.3 = ((bf16[4,16,40,128]{3,2,1,0:T(8,128)(2,1)}), bf16[4,16,40,128]{3,2,1,0:T(8,128)(2,1)S(1)}, u32[]{:S(2)}, u32[]{:S(2)}) async-start(bf16[4,16,40,128]{3,2,1,0:T(8,128)(2,1)} %broadcast_in_dim.29), calls=%async_computation.3 | async-start | bytes 1310720 | tf_op jit(solution)/shard_map/weight_over_x/all_to_all | solution.py:281
  44.7 68.6 %all-gather.4.cloned.1.call-start = ((), (), s32[]{:S(2)}) async-start(), calls=%async_computation.5 | async-start | bytes 1966080 | tf_op jit(solution)/shard_map/weight_over_core/all_gather | solution.py:283
  50.1 1.5 copy-start.3
  51.6 1.5 copy-start.5
  53.2 58.7 %copy-start.2 = (bf16[128,5120]{1,0:T(8,128)(2,1)S(1)}, bf16[128,5120]{1,0:T(8,128)(2,1)}, u32[]{:S(2)}) copy-start(bf16[128,5120]{1,0:T(8,128)(2,1)} %hidden_ref.1) | copy-start | bytes 3932164
  54.2 0.8 copy-start.17
  56.9 5.7 %collective-permute-start.1 = (f32[40,128]{1,0:T(8,128)S(1)}, f32[40,128]{1,0:T(8,128)S(1)}, u32[]{:S(2)}, u32[]{:S(2)}) collective-permute-start(f32[40,128]{1,0:T(8,128)S(1)} %reduce_sum.45), channel_id=1, source_target_pairs={{0,32},{16,48},{2,34},{18,50},{4,36},{20,52},{6,38},{22,54},{8,40}... | collective-permute-start | bytes 61448 | tf_op jit(solution)/shard_map/coefficients/ppermute | solution.py:32
  62.6 6.7 %collective-permute-start.2 = (f32[40,128]{1,0:T(8,128)S(1)}, f32[40,128]{1,0:T(8,128)S(1)}, u32[]{:S(2)}, u32[]{:S(2)}) collective-permute-start(f32[40,128]{1,0:T(8,128)S(1)} %add.160), channel_id=1, source_target_pairs={{0,64},{16,80},{2,66},{18,82},{4,68},{20,84},{6,70},{22,86},{8,72}... | collective-permute-start | bytes 61448 | tf_op jit(solution)/shard_map/coefficients/ppermute | solution.py:32
  69.2 9.6 %collective-permute-start.3 = (f32[40,128]{1,0:T(8,128)S(1)}, f32[40,128]{1,0:T(8,128)S(1)}, u32[]{:S(2)}, u32[]{:S(2)}) collective-permute-start(f32[40,128]{1,0:T(8,128)S(1)} %add.161), channel_id=1, source_target_pairs={{0,1},{16,17},{2,3},{18,19},{4,5},{20,21},{6,7},{22,23},{8,9},{24,... | collective-permute-start | bytes 61448 | tf_op jit(solution)/shard_map/coefficients/ppermute | solution.py:32
  104.6 49.5 %all-to-all-start.4 = ((s16[16,336,128]{2,1,0:T(8,128)(2,1)}), s16[16,336,128]{2,1,0:T(8,128)(2,1)S(1)}, u32[]{:S(2)}, u32[]{:S(2)}) async-start(s16[16,336,128]{2,1,0:T(8,128)(2,1)} %copy-done.7), calls=%async_computation.4 | async-start | bytes 2752512 | tf_op jit(solution)/shard_map/gradient_exchange/all_to_all | solution.py:250
  111.8 3.1 %copy-start.13 = (bf16[128,128]{1,0:T(8,128)(2,1)S(1)}, bf16[128,128]{1,0:T(8,128)(2,1)}, u32[]{:S(2)}) copy-start(bf16[128,128]{1,0:T(8,128)(2,1)} %cot_ref.1) | copy-start | bytes 98308
  111.8 3.1 %copy-start.15 = (f32[5120]{0:T(1024)S(1)}, f32[5120]{0:T(1024)}, u32[]{:S(2)}) copy-start(f32[5120]{0:T(1024)} %param.7) | copy-start | bytes 61444
  113.3 1.7 %copy-start.16 = (bf16[128,5120]{0,1:T(8,128)(2,1)S(1)}, bf16[128,5120]{0,1:T(8,128)(2,1)}, u32[]{:S(2)}) copy-start(bf16[128,5120]{0,1:T(8,128)(2,1)} %copy.18) | copy-start | bytes 3932164
  121.5 1.7 %copy-start.4 = (bf16[40,256,128]{2,1,0:T(8,128)(2,1)S(1)}, bf16[40,256,128]{2,1,0:T(8,128)(2,1)}, u32[]{:S(2)}) copy-start(bf16[40,256,128]{2,1,0:T(8,128)(2,1)} %copy-done.3) | copy-start | bytes 7864324
  123.2 1.7 %copy-start.6 = (bf16[40,256,128]{2,1,0:T(8,128)(2,1)S(1)}, bf16[40,256,128]{2,1,0:T(8,128)(2,1)}, u32[]{:S(2)}) copy-start(bf16[40,256,128]{2,1,0:T(8,128)(2,1)} %copy-done.5) | copy-start | bytes 7864324
  124.9 29.2 %copy-start.8 = (f32[1,320,128]{2,1,0:T(8,128)S(1)}, f32[1,320,128]{2,1,0:T(8,128)}, u32[]{:S(2)}) copy-start(f32[1,320,128]{2,1,0:T(8,128)} %param.10) | copy-start | bytes 491524
  124.9 29.2 %copy-start.10 = (f32[3,128,128]{2,1,0:T(8,128)S(1)}, f32[3,128,128]{2,1,0:T(8,128)}, u32[]{:S(2)}) copy-start(f32[3,128,128]{2,1,0:T(8,128)} %get-tuple-element.19.row_waves_ref) | copy-start | bytes 589828
  124.9 29.2 %copy-start.11 = (f32[3,128,128]{2,1,0:T(8,128)S(1)}, f32[3,128,128]{2,1,0:T(8,128)}, u32[]{:S(2)}) copy-start(f32[3,128,128]{2,1,0:T(8,128)} %get-tuple-element.20.col_waves_ref) | copy-start | bytes 589828
  (2 other events, 1.5 us)
Sparse Core Ops, SparseCore 0:
  55.1 18.1 all-gather.3

commit v2 on v1

v2 whole, which is shorter than its diff:
```python
import functools

import jax
import jax.numpy as jnp
from jax import lax
from jax.experimental import pallas as pl
from jax.experimental.pallas import tpu as pltpu
from jax.sharding import PartitionSpec as P

epsilon = 1e-06
decay_rate = 0.9
learn_rate = 0.01
side = 64
pair = 128
f32 = jnp.float32
bf16 = jnp.bfloat16
kernel_room = pltpu.CompilerParams(vmem_limit_bytes=24 * 2**20)
small = pl.CostEstimate(flops=1, bytes_accessed=1, transcendentals=0)

z_groups = [[2 * z + h for z in range(8)] for h in range(2)]
x_groups = [[8 * x + r for x in range(4)] for r in range(8)]
x_core_groups = [[8 * x + 2 * r + c for x in range(4) for c in range(2)] for r in range(4)]


def whole_mesh(move):
    def index(x, y, z, core):
        return ((x * 4 + y % 4) * 2 + core) * 16 + z * 2 + y // 4

    places = [(x, y, z, c) for x in range(4) for y in range(8) for z in range(8) for c in range(2)]
    sizes = (4, 8, 8, 2)
    wrap = lambda place: [at % size for at, size in zip(place, sizes)]
    return [(index(*place), index(*wrap(move(*place)))) for place in places]


def hop(value, move):
    return lax.ppermute(value, ("node", "local"), whole_mesh(move))


def over_z(value):
    return lax.all_to_all(value, "local", 0, 0, axis_index_groups=z_groups)


def dct_table():
    freq = jnp.arange(side, dtype=f32)[:, None]
    place = jnp.arange(side, dtype=f32)[None, :]
    wave = jnp.cos(jnp.pi * (2.0 * place + 1.0) * freq / (2.0 * side))
    norm_row = jnp.where(freq == 0.0, jnp.sqrt(1.0 / side), jnp.sqrt(2.0 / side))
    return wave * norm_row


def split2(value):
    high = value.astype(bf16)
    return high, (value - high.astype(f32)).astype(bf16)


def pair_tables():
    table = dct_table()
    empty = jnp.zeros_like(table)
    wide = jnp.block([[table, empty], [empty, table]])
    high = lax.reduce_precision(wide, exponent_bits=8, mantissa_bits=7)
    low = wide - high
    turned = jnp.concatenate([high.T, low.T], axis=0).astype(bf16)
    return turned, jnp.concatenate([high, low], axis=1).astype(bf16)


def dot(a, b, dims):
    return lax.dot_general(a, b, (dims, ((), ())), preferred_element_type=f32)


def from_hbm(value):
    return pltpu.with_memory_space_constraint(value, pltpu.HBM)


in_hbm = pl.BlockSpec(memory_space=pltpu.HBM)
in_vmem = pl.BlockSpec(memory_space=pltpu.VMEM)
in_smem = pl.BlockSpec(memory_space=pltpu.SMEM)


def waves(table, spots):
    at = lax.broadcasted_iota(jnp.int32, (pair, pair), 0)
    chosen = jnp.where(at == spots, 1.0, 0.0).astype(bf16)
    both = dot(table, chosen, ((1,), (0,)))
    return both[:pair].astype(bf16), both[pair:].astype(bf16)


def coded(value):
    top = jnp.max(jnp.abs(value), axis=0, keepdims=True)
    power = jnp.clip(jnp.ceil(jnp.log2(top * (1.0 / 32000.0))), -120.0, 120.0)
    whole = jnp.round(value * jnp.exp2(-power)).astype(jnp.int32).astype(jnp.int16)
    return whole, jnp.broadcast_to(power.astype(jnp.int32), (16, pair)).astype(jnp.int16)


def decoded(whole, power):
    return whole.astype(jnp.int32).astype(f32) * jnp.exp2(power.astype(jnp.int32)[0:1, :].astype(f32))


def front_kernel(
    hidden_ref, gain_ref, cot_ref, message_out_ref, high_out_ref, low_out_ref,
    message_ref, high_ref, low_ref, message_done, high_done, low_done,
):
    wide = hidden_ref[...].astype(f32)
    features = wide.shape[1]
    lines, _, tall, _ = message_ref.shape
    rows = tall - 16
    scale = lax.rsqrt(jnp.sum(wide * wide, axis=1, keepdims=True) * (1.0 / features) + epsilon)
    cot = cot_ref[...]
    copies = []
    for line in range(lines):
        at = slice(line * 2 * rows, (line + 1) * 2 * rows)
        normed = (hidden_ref[:, at].astype(f32) * scale * gain_ref[:, at]).astype(bf16)
        term = dot(normed, cot, ((0,), (0,)))
        high_ref[line], low_ref[line] = split2(term)
        for half in range(2):
            own = term[half * rows : (half + 1) * rows]
            message_ref[line, half, 0:rows, :], message_ref[line, half, rows:tall, :] = coded(own)
        for source, target, done in (
            (message_ref, message_out_ref, message_done),
            (high_ref, high_out_ref, high_done),
            (low_ref, low_out_ref, low_done),
        ):
            copies.append(pltpu.make_async_copy(source.at[line], target.at[line], done.at[line]))
            copies[-1].start()
    for copy in copies:
        copy.wait()


def front(hidden, gain, cot, owners):
    tokens, features = hidden.shape
    lines, rows = owners // 2, features // owners
    outs = (
        pltpu.HBM((lines, 2, rows + 16, pair), jnp.int16),
        pltpu.HBM((lines, 2 * rows, pair), bf16),
        pltpu.HBM((lines, 2 * rows, pair), bf16),
    )
    return pl.pallas_call(
        front_kernel,
        out_shape=outs,
        in_specs=[in_vmem] * 3,
        out_specs=(in_hbm,) * 3,
        scratch_shapes=[pltpu.VMEM(out.shape, out.dtype) for out in outs]
        + [pltpu.SemaphoreType.DMA((lines,))] * 3,
        compiler_params=kernel_room,
        cost_estimate=small,
        name="front",
    )(hidden, gain, cot)


def own_kernel(table_ref, row_ref, col_ref, momentum_ref, row_waves_ref, col_waves_ref, picked_ref):
    for q in range(row_ref.shape[0]):
        row_high, row_low = waves(table_ref[...], row_ref[q : q + 1, :])
        col_high, col_low = waves(table_ref[...], col_ref[q : q + 1, :])
        row_waves = row_high.astype(f32) + row_low.astype(f32)
        col_waves = col_high.astype(f32) + col_low.astype(f32)
        row_waves_ref[q] = row_waves
        col_waves_ref[q] = col_waves
        tile = decay_rate * momentum_ref[q * pair : min((q + 1) * pair, momentum_ref.shape[0]), :]
        short = pair - tile.shape[0]
        if short:
            tile = jnp.concatenate([tile, jnp.zeros((short, pair), f32)], axis=0)
        half = lax.dot_general(
            tile, row_waves, (((0,), (0,)), ((), ())), precision=lax.Precision.HIGHEST, preferred_element_type=f32
        )
        picked_ref[q : q + 1, :] = jnp.sum(half * col_waves, axis=0, keepdims=True)


def own_waves(table, rows, cols, momentum):
    tiles = rows.shape[0]
    return pl.pallas_call(
        own_kernel,
        out_shape=(
            jax.ShapeDtypeStruct((tiles, pair, pair), f32),
            jax.ShapeDtypeStruct((tiles, pair, pair), f32),
            jax.ShapeDtypeStruct((tiles, pair), f32),
        ),
        cost_estimate=small,
        name="own_waves",
    )(table, rows, cols, momentum)


def pack_kernel(upper_ref, mine_ref, other_ref, _, out_ref):
    eighth = mine_ref.shape[0] - 16
    mine, other = mine_ref[...].astype(f32), other_ref[...].astype(f32)
    first = upper_ref[0] == 0
    low = jnp.where(first, mine[:eighth], other[:eighth])
    high = jnp.where(first, other[:eighth], mine[:eighth])
    packed = jnp.concatenate([low, high, mine[eighth:] + other[eighth:]], axis=0).astype(bf16)
    for target in range(out_ref.shape[0]):
        out_ref[target] = packed


def pack(upper, mine, other, after):
    return pl.pallas_call(
        pack_kernel,
        out_shape=jax.ShapeDtypeStruct((8, 2 * mine.shape[0] - 16, pair), bf16),
        in_specs=[in_smem, in_vmem, in_vmem, pl.BlockSpec(memory_space=pl.ANY)],
        cost_estimate=small,
        name="pack",
    )(upper[None], mine, other, after)


def block_offsets(spots):
    block_in = lax.broadcasted_iota(jnp.int32, spots.shape, 1) // 32
    is_row = lax.broadcasted_iota(jnp.int32, spots.shape, 0) % 16 < 8
    return spots + side * jnp.where(is_row, block_in // 2, block_in % 2).astype(spots.dtype)


def pick_kernel(
    table_ref, spots_ref, high_in_ref, low_in_ref, decayed_ref, picked_ref, high_ref, low_ref, high_done, low_done
):
    lines, tall, _ = spots_ref.shape
    tiles = picked_ref.shape[0]
    each = tiles // lines
    arrivals = []
    for line in range(lines):
        arrivals.append(pltpu.make_async_copy(high_in_ref.at[line], high_ref.at[line], high_done.at[line]))
        arrivals.append(pltpu.make_async_copy(low_in_ref.at[line], low_ref.at[line], low_done.at[line]))
        arrivals[-2].start()
        arrivals[-1].start()
    spots = [spots_ref[line, tall - 16 : tall, :].astype(f32) for line in range(lines)]
    spots = jnp.transpose(block_offsets(jnp.concatenate(spots, axis=0)))
    across = lax.broadcasted_iota(jnp.int32, (pair, pair), 1)
    lane = across.astype(f32)
    table = table_ref[...]
    picked = jnp.zeros((pair, pair), f32)
    for line in range(lines):
        arrivals[2 * line].wait()
        arrivals[2 * line + 1].wait()
        for tile in range(each):
            chosen = []
            for at in (line * 16 + tile, line * 16 + 8 + tile):
                chosen.append(jnp.where(lane == spots[:, at : at + 1], 1.0, 0.0).astype(bf16))
            rows = dot(chosen[0], table, ((1,), (0,))).astype(bf16)
            cols = dot(chosen[1], table, ((1,), (0,)))
            at = slice(tile * pair, (tile + 1) * pair)
            high = high_ref[line, at, :]
            half = dot(rows, jnp.concatenate([high, high], axis=0), ((1,), (0,)))
            half += dot(rows[:, :pair], low_ref[line, at, :], ((1,), (0,)))
            found = jnp.sum(half * (cols[:, :pair] + cols[:, pair:]), axis=1, keepdims=True)
            picked = jnp.where(across == line * each + tile, found, picked)
    picked_ref[...] = jnp.transpose(picked)[:tiles] + decayed_ref[...]


def pick(table, spots, high, low, decayed):
    lines = spots.shape[0]
    return pl.pallas_call(
        pick_kernel,
        out_shape=jax.ShapeDtypeStruct(decayed.shape, f32),
        in_specs=[in_vmem, in_vmem, in_hbm, in_hbm, in_vmem],
        scratch_shapes=[pltpu.VMEM(high.shape, bf16)] * 2 + [pltpu.SemaphoreType.DMA((lines,))] * 2,
        compiler_params=kernel_room,
        cost_estimate=small,
        name="pick",
    )(table, spots, from_hbm(high), from_hbm(low), decayed)


def middle_kernel(upper_ref, message_ref, total_ref, own_ref, rest_out_ref, spread_ref, rest_ref, rest_done):
    sources, halves, tall, _ = message_ref.shape
    rows = own_ref.shape[0]
    sums = []
    for half in range(halves):
        term = jnp.zeros(own_ref.shape, f32)
        for source in range(sources):
            term += decoded(message_ref[source, half, 0:rows, :], message_ref[source, half, rows:tall, :])
        sums.append(term)
    first = upper_ref[0] == 0
    own_ref[...] = jnp.where(first, sums[0], sums[1])
    rest_ref[0:rows, :], rest_ref[rows:tall, :] = coded(jnp.where(first, sums[1], sums[0]))
    copy = pltpu.make_async_copy(rest_ref, rest_out_ref, rest_done)
    copy.start()
    for source in range(sources):
        spread_ref[source] = total_ref[...]
    copy.wait()


def middle(message, upper, total):
    sources, _, tall, _ = message.shape
    return pl.pallas_call(
        middle_kernel,
        out_shape=(
            jax.ShapeDtypeStruct((tall - 16, pair), f32),
            pltpu.HBM((tall, pair), jnp.int16),
            jax.ShapeDtypeStruct((sources,) + total.shape, f32),
        ),
        out_specs=(in_vmem, in_hbm, in_vmem),
        scratch_shapes=[pltpu.VMEM((tall, pair), jnp.int16), pltpu.SemaphoreType.DMA],
        in_specs=[in_smem, in_vmem, in_vmem],
        compiler_params=kernel_room,
        cost_estimate=small,
        name="middle",
    )(upper[None], message, total)


def momentum_kernel(sum_ref, rest_ref, momentum_ref, row_waves_ref, col_waves_ref, out_ref, mid_ref):
    rows = out_ref.shape[0]
    total = decay_rate * momentum_ref[...] + sum_ref[...]
    mid_ref[0:rows, :] = total + decoded(rest_ref[0:rows, :], rest_ref[rows:, :])
    mid_ref[rows:, :] = jnp.zeros((mid_ref.shape[0] - rows, pair), f32)
    highest = functools.partial(lax.dot_general, precision=lax.Precision.HIGHEST, preferred_element_type=f32)
    for q in range(row_waves_ref.shape[0]):
        tile = mid_ref[q * pair : (q + 1) * pair, :]
        half = highest(tile, row_waves_ref[q], (((0,), (0,)), ((), ())))
        picked = jnp.sum(half * col_waves_ref[q], axis=0, keepdims=True)
        sent = highest(row_waves_ref[q], picked * col_waves_ref[q], (((1,), (1,)), ((), ())))
        left = min(pair, rows - q * pair)
        out_ref[q * pair : q * pair + left, :] = (tile - sent)[:left]


def new_momentum_of(own_sum, rest, momentum, row_waves, col_waves):
    tiles = row_waves.shape[0]
    return pl.pallas_call(
        momentum_kernel,
        out_shape=jax.ShapeDtypeStruct(momentum.shape, f32),
        scratch_shapes=[pltpu.VMEM((tiles * pair, pair), f32)],
        compiler_params=kernel_room,
        cost_estimate=small,
        name="momentum_step",
    )(own_sum, rest, momentum, row_waves, col_waves)


def weight_rows(parts_ref, line):
    parts = [parts_ref[part, line].astype(f32) for part in range(parts_ref.shape[0])]
    eighth = parts[0].shape[0] // 2
    return jnp.concatenate([p[:eighth] for p in parts] + [p[eighth:] for p in parts], axis=0)


def weight_kernel(nodes, table_ref, spots_ref, total_ref, parts_ref, out_ref):
    lines, tall, _ = spots_ref.shape
    total = total_ref[0]
    for part in range(1, total_ref.shape[0]):
        total += total_ref[part]
    total = total / nodes
    each = total.shape[0] // lines
    table = table_ref[...]
    for line in range(lines):
        weight = weight_rows(parts_ref, line)
        spots = block_offsets(spots_ref[line, tall - 16 : tall, :].astype(f32).astype(jnp.int32))
        for tile in range(each):
            q = line * each + tile
            row_high, row_low = waves(table, spots[tile : tile + 1])
            col_high, col_low = waves(table, spots[8 + tile : 9 + tile])
            high, low = split2(total[q : q + 1, :] * (col_high.astype(f32) + col_low.astype(f32)))
            field = dot(
                jnp.concatenate([row_high, row_low], axis=1), jnp.concatenate([high, high], axis=1), ((1,), (1,))
            )
            field += dot(row_high, low, ((1,), (1,)))
            fresh = weight[tile * pair : (tile + 1) * pair] - learn_rate * jnp.tanh(field)
            out_ref[q * pair : (q + 1) * pair, :] = fresh.astype(bf16)


def new_weight_of(table, spots, total, parts, nodes):
    return pl.pallas_call(
        functools.partial(weight_kernel, nodes),
        out_shape=jax.ShapeDtypeStruct((total.shape[1] * pair, pair), bf16),
        compiler_params=kernel_room,
        cost_estimate=small,
        name="weight_step",
    )(table, spots, total, parts)


def input_kernel(hidden_ref, gain_ref, cot_ref, parts_ref, out_ref, gained_ref):
    features = hidden_ref.shape[1]
    wide = hidden_ref[...].astype(f32)
    scale = lax.rsqrt(jnp.sum(wide * wide, axis=1, keepdims=True) * (1.0 / features) + epsilon)
    cot = cot_ref[...]
    lines = parts_ref.shape[1]
    step = features // lines
    along = jnp.zeros(scale.shape, f32)
    for piece in range(lines):
        at = slice(piece * step, (piece + 1) * step)
        weight = weight_rows(parts_ref, piece).astype(bf16)
        gained = gain_ref[:, at] * dot(cot, weight, ((1,), (1,)))
        gained_ref[:, at] = gained
        along += jnp.sum(hidden_ref[:, at].astype(f32) * gained, axis=1, keepdims=True)
    factor = scale**3 * (along * (1.0 / features))
    for piece in range(lines):
        at = slice(piece * step, (piece + 1) * step)
        out_ref[:, at] = (scale * gained_ref[:, at] - hidden_ref[:, at].astype(f32) * factor).astype(bf16)


def input_grad_of(hidden, gain, cot, parts):
    return pl.pallas_call(
        input_kernel,
        out_shape=jax.ShapeDtypeStruct(hidden.shape, bf16),
        scratch_shapes=[pltpu.VMEM(hidden.shape, f32)],
        compiler_params=kernel_room,
        cost_estimate=small,
        name="input_gradient",
    )(hidden, gain, cot, parts)


def on_device(hidden, gain, cotangent, weight, momentum, indices):
    nodes, owners = lax.axis_size("node"), lax.axis_size("local")
    node, local = lax.axis_index("node"), lax.axis_index("local")
    features = hidden.shape[1]
    own_rows, head = weight.shape
    turned, table = pair_tables()
    blocks = indices.size
    row_of, col_of = indices // side, indices % side

    upper = local % 2
    eighth = own_rows // 8
    part = (node // 8) * 2 + node % 2
    with jax.named_scope("weight_part"):
        piece = lax.dynamic_slice_in_dim(weight, part * eighth, eighth, axis=0)
        at_half = lambda spots: lax.dynamic_update_slice(
            jnp.zeros((8 * pair,), jnp.int32), spots.reshape(-1), (upper * blocks,)
        ).reshape(8, pair)
        piece = jnp.concatenate([piece, at_half(row_of).astype(bf16), at_half(col_of).astype(bf16)], axis=0)
    with jax.named_scope("weight_over_y"):
        other = hop(piece, lambda x, y, z, c: (x, (y + (2 if y in (2, 3, 6, 7) else 6)) % 8, z, c))

    spare = (-blocks) % pair
    tiles = (blocks + spare) // pair
    own_at = jnp.pad(indices.reshape(-1), (0, spare)).reshape(tiles, pair)
    block_in = (jnp.arange(pair, dtype=jnp.int32) // 32)[None, :]
    place = lambda rows, cols: (rows + side * (block_in // 2), cols + side * (block_in % 2))
    own_row, own_col = place(own_at // side, own_at % side)
    own_momentum = momentum[0]
    row_waves, col_waves, decayed = own_waves(turned, own_row, own_col, own_momentum)
    decayed = lax.dynamic_update_slice(
        jnp.zeros((owners * blocks,), f32), decayed.reshape(-1)[:blocks], (local * blocks,)
    ).reshape(-1, pair)

    with jax.named_scope("weight_over_z"):
        gathered = over_z(pack(upper, piece, other, decayed))

    message, high, low = front(hidden, gain[None, :], cotangent, owners)
    with jax.named_scope("gradient_exchange"):
        arrived = over_z(message)

    total = pick(table, gathered, high, low, decayed)
    with jax.named_scope("coefficients"):
        total = total + hop(total, lambda x, y, z, c: (x, y, z, 1 - c))
        total = total + hop(total, lambda x, y, z, c: (x, y ^ 1, z, c))
        total = total + hop(total, lambda x, y, z, c: (x, ((y + 1) ^ 1) - 1, z, c))
        total = total + hop(total, lambda x, y, z, c: (x, y ^ 3 if y in (0, 3, 4, 7) else 7 - y, z, c))
    own_sum, rest, spread = middle(arrived, upper, total)
    with jax.named_scope("coefficients_over_z"):
        totals = jnp.sum(over_z(spread), axis=0)
    with jax.named_scope("coefficients_over_x"):
        totals = jnp.broadcast_to(totals[None], (4,) + totals.shape)
        totals = lax.all_to_all(totals, "node", 0, 0, axis_index_groups=x_groups)
    with jax.named_scope("gradient_over_y"):
        rest = hop(rest, lambda x, y, z, c: (x, (y + 4) % 8, z, c))

    with jax.named_scope("weight_over_x_and_core"):
        parts = lax.all_gather(gathered[:, : 2 * eighth, :], "node", axis_index_groups=x_core_groups)

    input_grad = input_grad_of(hidden, gain[None, :], cotangent, parts)
    new_momentum = new_momentum_of(own_sum, rest, own_momentum, row_waves, col_waves)[None]
    new_weight = new_weight_of(turned, gathered, totals, parts, nodes)
    return (new_weight, new_momentum, input_grad)


def solution(mesh):
    return jax.shard_map(
        on_device,
        mesh=mesh,
        in_specs=(
            P(("node", "local"), None),
            P(),
            P(("node", "local"), None),
            P("local", None),
            P("node", "local", None),
            P("local", None),
        ),
        out_specs=(P(), P("node", "local", None), P(("node", "local"), None)),
        check_vma=False,
    )
```

time: 164 us -> 129 us (0.79)
  the two profiles are of different devices: /device:TPU:40 before, /device:TPU:6 now
where the time goes in v2:
time: 129 us; the launch traced here: 128 us
  starting transfers between devices  45.9 us (36%)
  Pallas kernels  31.8 us (25%)
  waiting for transfers between devices  26.1 us (20%)
  between operations  14.3 us (11%)
  local copies, waits for them, and re-layouts  7.17 us (6%)
  other arithmetic  2.97 us (2%)
    ppermute x6, starting transfers between devices, hop(): return lax.ppermute(value, ('node', 'local'), whole_mesh(move))  20.6 us
    all_to_all x3, starting transfers between devices, over_z(): return lax.all_to_all(value, 'local', 0, 0, axis_index_groups=z_groups)  20.5 us
    all_to_all x3, waiting for transfers between devices, over_z(): return lax.all_to_all(value, 'local', 0, 0, axis_index_groups=z_groups)  13.5 us
    ppermute x6, waiting for transfers between devices, hop(): return lax.ppermute(value, ('node', 'local'), whole_mesh(move))  12.5 us
    pallas_call x1, Pallas kernels, new_weight_of(): pl.pallas_call(functools.partial(weight_kernel, nodes), out_shape=jax.Sha...  10.8 us
    pallas_call x1, Pallas kernels, pick(): pl.pallas_call(pick_kernel, out_shape=jax.ShapeDtypeStruct(decayed.shape,...  8.3 us
    all_to_all x1, starting transfers between devices, on_device(): totals = lax.all_to_all(totals, 'node', 0, 0, axis_index_groups=x_groups)  4.77 us
    unnamed x30, local copies, waits for them, and re-layouts  3.6 us
  transfers between devices with their start and end apart: 11, of which 7 were waited for; matrix products, arithmetic and copies ran while one was open for 4% of the time, Pallas kernels for 15%

profile of v2, /device:TPU:6, one launch (start us, length us, event | category | flops | bytes accessed | tf_op | source)
XLA Modules:
  0.0 128.3 jit_solution(7642586204559964458)
XLA Ops:
  8.7 6.2 %collective-permute-start = (bf16[56,128]{1,0:T(8,128)(2,1)S(1)}, bf16[56,128]{1,0:T(8,128)(2,1)S(1)}, u32[]{:S(2)}, u32[]{:S(2)}) collective-permute-start(bf16[56,128]{1,0:T(8,128)(2,1)S(1)} %pad_maximum_fusion.2.mine_ref), channel_id=1, source_target_pairs={{0,65},{16,81},{2,67},{18,83},{4,69},{20,85},{6,71},{22,87},{8,73}... | collective-permute-start | bytes 43016 | tf_op jit(solution)/shard_map/weight_over_y/ppermute | solution.py:36
  17.2 2.2 %own_waves.1 = (f32[3,128,128]{2,1,0:T(8,128)}, f32[3,128,128]{2,1,0:T(8,128)}, f32[3,128]{1,0:T(4,128)}) custom-call(bf16[256,128]{1,0:T(8,128)(2,1)} %pad_maximum_fusion.table_ref, s32[3,128]{1,0:T(4,128)} %get-tuple-element.27.row_ref, s32[3,128]{1,0:T(4,128)} %get-tuple-element.26.col_ref, f32[320,128]{1,0:T(8,128)} %bitcast.38), custom_call_target="tpu_custom_call" | custom-call | flops 1 | bytes 1 | tf_op jit(solution)/shard_map/own_waves/pallas_call | solution.py:168
  20.8 1.4 %pack.1 = bf16[8,96,128]{2,1,0:T(8,128)(2,1)} custom-call(s32[1]{0:T(128)} %bitcast.2.upper_ref, bf16[56,128]{1,0:T(8,128)(2,1)} %copy-done.13, bf16[56,128]{1,0:T(8,128)(2,1)} %copy-done.14, f32[40,128]{1,0:T(8,128)} %bitcast.40), custom_call_target="tpu_custom_call" | custom-call | flops 1 | bytes 1 | tf_op jit(solution)/shard_map/weight_over_z/pack/pallas_call | solution.py:192
  22.2 10.3 %all-to-all-start = ((bf16[8,96,128]{2,1,0:T(8,128)(2,1)}), bf16[8,96,128]{2,1,0:T(8,128)(2,1)S(1)}, u32[]{:S(2)}, u32[]{:S(2)}) async-start(bf16[8,96,128]{2,1,0:T(8,128)(2,1)} %pack.1), calls=%async_computation | async-start | bytes 393216 | tf_op jit(solution)/shard_map/weight_over_z/all_to_all | solution.py:40
  32.5 2.9 %front.1 = (s16[8,2,336,128]{3,2,1,0:T(8,128)(2,1)}, bf16[8,640,128]{2,1,0:T(8,128)(2,1)}, bf16[8,640,128]{2,1,0:T(8,128)(2,1)}) custom-call(bf16[128,5120]{1,0:T(8,128)(2,1)S(1)} %copy-done.1, f32[1,5120]{1,0:T(1,128)S(1)} %bitcast.42, bf16[128,128]{1,0:T(8,128)(2,1)S(1)} %copy-done.10), custom_call_target="tpu_custom_call" | custom-call | flops 1 | bytes 1 | tf_op jit(solution)/shard_map/front/pallas_call | solution.py:135
  35.4 7.3 %all-to-all-done.spots_ref = bf16[8,96,128]{2,1,0:T(8,128)(2,1)S(1)} async-done(((bf16[8,96,128]{2,1,0:T(8,128)(2,1)}), bf16[8,96,128]{2,1,0:T(8,128)(2,1)S(1)}, u32[]{:S(2)}, u32[]{:S(2)}) %all-to-all-start) | async-done | bytes 196640 | tf_op jit(solution)/shard_map/weight_over_z/all_to_all | solution.py:40
  42.7 3.7 %all-to-all-start.1 = ((s16[8,2,336,128]{3,2,1,0:T(8,128)(2,1)}), s16[8,2,336,128]{3,2,1,0:T(8,128)(2,1)S(1)}, u32[]{:S(2)}, u32[]{:S(2)}) async-start(s16[8,2,336,128]{3,2,1,0:T(8,128)(2,1)} %get-tuple-element.13), calls=%async_computation.1 | async-start | bytes 2752512 | tf_op jit(solution)/shard_map/gradient_exchange/all_to_all | solution.py:40
  47.3 8.3 %pick.1 = f32[40,128]{1,0:T(8,128)S(1)} custom-call(bf16[128,256]{1,0:T(8,128)(2,1)S(1)} %copy.10.table_ref, bf16[8,96,128]{2,1,0:T(8,128)(2,1)S(1)} %all-to-all-done.spots_ref, bf16[8,640,128]{2,1,0:T(8,128)(2,1)} %get-tuple-element.14.high_in_ref, bf16[8,640,128]{2,1,0:T(8,128)(2,1)} %get-tuple-element.15.low_in_ref, f32[40,128]{1,0:T(8,128)S(1)} %bitcast.41), custom_call_target="tpu_custom_call" | custom-call | flops 1 | bytes 1 | tf_op jit(solution)/shard_map/pick/pallas_call | solution.py:245
  55.6 2.1 %collective-permute-start.1 = (f32[40,128]{1,0:T(8,128)S(1)}, f32[40,128]{1,0:T(8,128)S(1)}, u32[]{:S(2)}, u32[]{:S(2)}) collective-permute-start(f32[40,128]{1,0:T(8,128)S(1)} %pick.1), channel_id=1, source_target_pairs={{0,16},{16,0},{2,18},{18,2},{4,20},{20,4},{6,22},{22,6},{8,24},{24... | collective-permute-start | bytes 61448 | tf_op jit(solution)/shard_map/coefficients/ppermute | solution.py:36
  58.9 2.6 %collective-permute-start.2 = (f32[40,128]{1,0:T(8,128)S(1)}, f32[40,128]{1,0:T(8,128)S(1)}, u32[]{:S(2)}, u32[]{:S(2)}) collective-permute-start(f32[40,128]{1,0:T(8,128)S(1)} %add.122), channel_id=1, source_target_pairs={{0,32},{16,48},{2,34},{18,50},{4,36},{20,52},{6,38},{22,54},{8,40}... | collective-permute-start | bytes 61448 | tf_op jit(solution)/shard_map/coefficients/ppermute | solution.py:36
  61.4 3.1 %collective-permute-done.2 = f32[40,128]{1,0:T(8,128)S(1)} collective-permute-done((f32[40,128]{1,0:T(8,128)S(1)}, f32[40,128]{1,0:T(8,128)S(1)}, u32[]{:S(2)}, u32[]{:S(2)}) %collective-permute-start.2) | collective-permute-done | bytes 20512 | tf_op jit(solution)/shard_map/coefficients/ppermute | solution.py:36
  64.5 1.9 %collective-permute-start.3 = (f32[40,128]{1,0:T(8,128)S(1)}, f32[40,128]{1,0:T(8,128)S(1)}, u32[]{:S(2)}, u32[]{:S(2)}) collective-permute-start(f32[40,128]{1,0:T(8,128)S(1)} %add.123), channel_id=1, source_target_pairs={{0,97},{16,113},{2,99},{18,115},{4,101},{20,117},{6,103},{22,119},... | collective-permute-start | bytes 61448 | tf_op jit(solution)/shard_map/coefficients/ppermute | solution.py:36
  66.5 5.0 %collective-permute-done.3 = f32[40,128]{1,0:T(8,128)S(1)} collective-permute-done((f32[40,128]{1,0:T(8,128)S(1)}, f32[40,128]{1,0:T(8,128)S(1)}, u32[]{:S(2)}, u32[]{:S(2)}) %collective-permute-start.3) | collective-permute-done | bytes 20512 | tf_op jit(solution)/shard_map/coefficients/ppermute | solution.py:36
  71.4 4.1 %collective-permute-start.4 = (f32[40,128]{1,0:T(8,128)S(1)}, f32[40,128]{1,0:T(8,128)S(1)}, u32[]{:S(2)}, u32[]{:S(2)}) collective-permute-start(f32[40,128]{1,0:T(8,128)S(1)} %add.124), channel_id=1, source_target_pairs={{0,96},{16,112},{2,98},{18,114},{4,100},{20,116},{6,102},{22,118},... | collective-permute-start | bytes 61448 | tf_op jit(solution)/shard_map/coefficients/ppermute | solution.py:36
  75.6 3.3 %collective-permute-done.4 = f32[40,128]{1,0:T(8,128)S(1)} collective-permute-done((f32[40,128]{1,0:T(8,128)S(1)}, f32[40,128]{1,0:T(8,128)S(1)}, u32[]{:S(2)}, u32[]{:S(2)}) %collective-permute-start.4) | collective-permute-done | bytes 20512 | tf_op jit(solution)/shard_map/coefficients/ppermute | solution.py:36
  80.9 1.8 %middle.1 = (f32[320,128]{1,0:T(8,128)S(1)}, s16[336,128]{1,0:T(8,128)(2,1)}, f32[8,40,128]{2,1,0:T(8,128)}) custom-call(s32[1]{0:T(128)} %bitcast.2.upper_ref, s16[8,2,336,128]{3,2,1,0:T(8,128)(2,1)S(1)} %all-to-all-done.1.message_ref, f32[40,128]{1,0:T(8,128)S(1)} %copy-done.12), custom_call_target="tpu_custom_call" | custom-call | flops 1 | bytes 1 | tf_op jit(solution)/shard_map/middle/pallas_call | solution.py:277
  82.7 6.5 %all-to-all-start.2 = ((f32[8,40,128]{2,1,0:T(8,128)}), f32[8,40,128]{2,1,0:T(8,128)S(1)}, u32[]{:S(2)}, u32[]{:S(2)}) async-start(f32[8,40,128]{2,1,0:T(8,128)} %get-tuple-element.16), calls=%async_computation.2 | async-start | bytes 327680 | tf_op jit(solution)/shard_map/coefficients_over_z/all_to_all | solution.py:40
  89.1 3.8 %collective-permute-start.5 = (s16[336,128]{1,0:T(8,128)(2,1)}, s16[336,128]{1,0:T(8,128)(2,1)S(1)}, u32[]{:S(2)}, u32[]{:S(2)}) collective-permute-start(s16[336,128]{1,0:T(8,128)(2,1)} %get-tuple-element.18), channel_id=1, source_target_pairs={{0,1},{16,17},{2,3},{18,19},{4,5},{20,21},{6,7},{22,23},{8,9},{24,... | collective-permute-start | bytes 258056 | tf_op jit(solution)/shard_map/gradient_over_y/ppermute | solution.py:36
  92.9 5.6 %all-to-all-done.2 = f32[8,40,128]{2,1,0:T(8,128)S(1)} async-done(((f32[8,40,128]{2,1,0:T(8,128)}), f32[8,40,128]{2,1,0:T(8,128)S(1)}, u32[]{:S(2)}, u32[]{:S(2)}) %all-to-all-start.2) | async-done | bytes 163872 | tf_op jit(solution)/shard_map/coefficients_over_z/all_to_all | solution.py:40
  99.2 4.8 %all-to-all-start.3 = ((f32[4,40,128]{2,1,0:T(8,128)}), f32[4,40,128]{2,1,0:T(8,128)S(1)}, u32[]{:S(2)}, u32[]{:S(2)}) async-start(f32[4,40,128]{2,1,0:T(8,128)} %broadcast_in_dim.37), calls=%async_computation.3 | async-start | bytes 163840 | tf_op jit(solution)/shard_map/coefficients_over_x/all_to_all | solution.py:442
  104.9 2.0 %momentum_step.1 = f32[320,128]{1,0:T(8,128)} custom-call(f32[320,128]{1,0:T(8,128)S(1)} %get-tuple-element.17.sum_ref, s16[336,128]{1,0:T(8,128)(2,1)S(1)} %collective-permute-done.5.rest_ref, f32[320,128]{1,0:T(8,128)S(1)} %bitcast.39, f32[3,128,128]{2,1,0:T(8,128)S(1)} %copy-done.6, f32[3,128,128]{2,1,0:T(8,128)S(1)} %copy-done.7), custom_call_target="tpu_custom_call" | custom-call | flops 1 | bytes 1 | tf_op jit(solution)/shard_map/momentum_step/pallas_call | solution.py:310
  106.9 1.3 %copy-done.2 = bf16[64,80,128]{2,1,0:T(8,128)(2,1)S(1)} copy-done((bf16[64,80,128]{2,1,0:T(8,128)(2,1)S(1)}, bf16[64,80,128]{2,1,0:T(8,128)(2,1)}, u32[]{:S(2)}) %copy-start.2) | copy-done | bytes 1310744
  108.2 2.4 %input_gradient.1 = bf16[128,5120]{1,0:T(8,128)(2,1)} custom-call(bf16[128,5120]{1,0:T(8,128)(2,1)S(1)} %copy-done.1, f32[1,5120]{1,0:T(1,128)S(1)} %bitcast.43, bf16[128,128]{1,0:T(8,128)(2,1)S(1)} %copy-done.10, bf16[8,8,80,128]{3,2,1,0:T(8,128)(2,1)S(1)} %bitcast.36), custom_call_target="tpu_custom_call" | custom-call | flops 1 | bytes 1 | tf_op jit(solution)/shard_map/input_gradient/pallas_call | solution.py:381
  110.7 10.8 %weight_step.1 = bf16[5120,128]{1,0:T(8,128)(2,1)} custom-call(bf16[256,128]{1,0:T(8,128)(2,1)S(1)} %copy-done.5, bf16[8,96,128]{2,1,0:T(8,128)(2,1)S(1)} %all-to-all-done.spots_ref, f32[4,40,128]{2,1,0:T(8,128)S(1)} %all-to-all-done.3.total_ref, bf16[8,8,80,128]{3,2,1,0:T(8,128)(2,1)S(1)} %bitcast.37), custom_call_target="tpu_custom_call" | custom-call | flops 1 | bytes 1 | tf_op jit(solution)/shard_map/weight_step/pallas_call | solution.py:351
  (65 shorter events, 10.7 us)
Async XLA Ops:
  7.2 1.1 copy-start
  7.2 25.3 %copy-start.11 = (f32[5120]{0:T(1024)S(1)}, f32[5120]{0:T(1024)}, u32[]{:S(2)}) copy-start(f32[5120]{0:T(1024)} %param.7) | copy-start | bytes 61444
  7.2 25.3 %copy-start.1 = (bf16[128,5120]{1,0:T(8,128)(2,1)S(1)}, bf16[128,5120]{1,0:T(8,128)(2,1)}, u32[]{:S(2)}) copy-start(bf16[128,5120]{1,0:T(8,128)(2,1)} %hidden_ref.3) | copy-start | bytes 3932164
  7.2 25.3 %copy-start.10 = (bf16[128,128]{1,0:T(8,128)(2,1)S(1)}, bf16[128,128]{1,0:T(8,128)(2,1)}, u32[]{:S(2)}) copy-start(bf16[128,128]{1,0:T(8,128)(2,1)} %cot_ref.3) | copy-start | bytes 98308
  8.7 11.5 %copy-start.13 = (bf16[56,128]{1,0:T(8,128)(2,1)}, bf16[56,128]{1,0:T(8,128)(2,1)S(1)}, u32[]{:S(2)}) copy-start(bf16[56,128]{1,0:T(8,128)(2,1)S(1)} %pad_maximum_fusion.2.mine_ref) | copy-start | bytes 43012
  8.7 11.5 %collective-permute-start = (bf16[56,128]{1,0:T(8,128)(2,1)S(1)}, bf16[56,128]{1,0:T(8,128)(2,1)S(1)}, u32[]{:S(2)}, u32[]{:S(2)}) collective-permute-start(bf16[56,128]{1,0:T(8,128)(2,1)S(1)} %pad_maximum_fusion.2.mine_ref), channel_id=1, source_target_pairs={{0,65},{16,81},{2,67},{18,83},{4,69},{20,85},{6,71},{22,87},{8,73}... | collective-permute-start | bytes 43016 | tf_op jit(solution)/shard_map/weight_over_y/ppermute | solution.py:36
  22.2 20.5 %all-to-all-start = ((bf16[8,96,128]{2,1,0:T(8,128)(2,1)}), bf16[8,96,128]{2,1,0:T(8,128)(2,1)S(1)}, u32[]{:S(2)}, u32[]{:S(2)}) async-start(bf16[8,96,128]{2,1,0:T(8,128)(2,1)} %pack.1), calls=%async_computation | async-start | bytes 393216 | tf_op jit(solution)/shard_map/weight_over_z/all_to_all | solution.py:40
  42.7 4.6 %copy-start.9 = (f32[5120]{0:T(1024)S(1)}, f32[5120]{0:T(1024)}, u32[]{:S(2)}) copy-start(f32[5120]{0:T(1024)} %copy-done.8) | copy-start | bytes 61444
  42.7 37.4 %all-to-all-start.1 = ((s16[8,2,336,128]{3,2,1,0:T(8,128)(2,1)}), s16[8,2,336,128]{3,2,1,0:T(8,128)(2,1)S(1)}, u32[]{:S(2)}, u32[]{:S(2)}) async-start(s16[8,2,336,128]{3,2,1,0:T(8,128)(2,1)} %get-tuple-element.13), calls=%async_computation.1 | async-start | bytes 2752512 | tf_op jit(solution)/shard_map/gradient_exchange/all_to_all | solution.py:40
  46.4 60.5 %all-gather.3.cloned.1.call-start = ((), (), s32[]{:S(2)}) async-start(), calls=%async_computation.4 | async-start | bytes 1474560 | tf_op jit(solution)/shard_map/weight_over_x_and_core/all_gather | solution.py:447
  55.6 48.4 %copy-start.4 = (f32[1,320,128]{2,1,0:T(8,128)S(1)}, f32[1,320,128]{2,1,0:T(8,128)}, u32[]{:S(2)}) copy-start(f32[1,320,128]{2,1,0:T(8,128)} %param.10) | copy-start | bytes 491524
  55.6 48.4 %copy-start.6 = (f32[3,128,128]{2,1,0:T(8,128)S(1)}, f32[3,128,128]{2,1,0:T(8,128)}, u32[]{:S(2)}) copy-start(f32[3,128,128]{2,1,0:T(8,128)} %get-tuple-element.19.row_waves_ref) | copy-start | bytes 589828
  55.6 3.2 %collective-permute-start.1 = (f32[40,128]{1,0:T(8,128)S(1)}, f32[40,128]{1,0:T(8,128)S(1)}, u32[]{:S(2)}, u32[]{:S(2)}) collective-permute-start(f32[40,128]{1,0:T(8,128)S(1)} %pick.1), channel_id=1, source_target_pairs={{0,16},{16,0},{2,18},{18,2},{4,20},{20,4},{6,22},{22,6},{8,24},{24... | collective-permute-start | bytes 61448 | tf_op jit(solution)/shard_map/coefficients/ppermute | solution.py:36
  58.9 5.7 %collective-permute-start.2 = (f32[40,128]{1,0:T(8,128)S(1)}, f32[40,128]{1,0:T(8,128)S(1)}, u32[]{:S(2)}, u32[]{:S(2)}) collective-permute-start(f32[40,128]{1,0:T(8,128)S(1)} %add.122), channel_id=1, source_target_pairs={{0,32},{16,48},{2,34},{18,50},{4,36},{20,52},{6,38},{22,54},{8,40}... | collective-permute-start | bytes 61448 | tf_op jit(solution)/shard_map/coefficients/ppermute | solution.py:36
  64.5 6.9 %collective-permute-start.3 = (f32[40,128]{1,0:T(8,128)S(1)}, f32[40,128]{1,0:T(8,128)S(1)}, u32[]{:S(2)}, u32[]{:S(2)}) collective-permute-start(f32[40,128]{1,0:T(8,128)S(1)} %add.123), channel_id=1, source_target_pairs={{0,97},{16,113},{2,99},{18,115},{4,101},{20,117},{6,103},{22,119},... | collective-permute-start | bytes 61448 | tf_op jit(solution)/shard_map/coefficients/ppermute | solution.py:36
  71.4 7.5 %collective-permute-start.4 = (f32[40,128]{1,0:T(8,128)S(1)}, f32[40,128]{1,0:T(8,128)S(1)}, u32[]{:S(2)}, u32[]{:S(2)}) collective-permute-start(f32[40,128]{1,0:T(8,128)S(1)} %add.124), channel_id=1, source_target_pairs={{0,96},{16,112},{2,98},{18,114},{4,100},{20,116},{6,102},{22,118},... | collective-permute-start | bytes 61448 | tf_op jit(solution)/shard_map/coefficients/ppermute | solution.py:36
  80.1 0.7 copy-start.12
  82.7 15.9 %all-to-all-start.2 = ((f32[8,40,128]{2,1,0:T(8,128)}), f32[8,40,128]{2,1,0:T(8,128)S(1)}, u32[]{:S(2)}, u32[]{:S(2)}) async-start(f32[8,40,128]{2,1,0:T(8,128)} %get-tuple-element.16), calls=%async_computation.2 | async-start | bytes 327680 | tf_op jit(solution)/shard_map/coefficients_over_z/all_to_all | solution.py:40
  89.1 14.9 %collective-permute-start.5 = (s16[336,128]{1,0:T(8,128)(2,1)}, s16[336,128]{1,0:T(8,128)(2,1)S(1)}, u32[]{:S(2)}, u32[]{:S(2)}) collective-permute-start(s16[336,128]{1,0:T(8,128)(2,1)} %get-tuple-element.18), channel_id=1, source_target_pairs={{0,1},{16,17},{2,3},{18,19},{4,5},{20,21},{6,7},{22,23},{8,9},{24,... | collective-permute-start | bytes 258056 | tf_op jit(solution)/shard_map/gradient_over_y/ppermute | solution.py:36
  99.2 11.5 %all-to-all-start.3 = ((f32[4,40,128]{2,1,0:T(8,128)}), f32[4,40,128]{2,1,0:T(8,128)S(1)}, u32[]{:S(2)}, u32[]{:S(2)}) async-start(f32[4,40,128]{2,1,0:T(8,128)} %broadcast_in_dim.37), calls=%async_computation.3 | async-start | bytes 163840 | tf_op jit(solution)/shard_map/coefficients_over_x/all_to_all | solution.py:442
  104.0 0.9 copy-start.7
  106.9 1.3 %copy-start.2 = (bf16[64,80,128]{2,1,0:T(8,128)(2,1)S(1)}, bf16[64,80,128]{2,1,0:T(8,128)(2,1)}, u32[]{:S(2)}) copy-start(bf16[64,80,128]{2,1,0:T(8,128)(2,1)} %all-gather.3.cloned.1.call-done) | copy-start | bytes 3932164
  108.2 2.5 %copy-start.3 = (bf16[64,80,128]{2,1,0:T(8,128)(2,1)S(1)}, bf16[64,80,128]{2,1,0:T(8,128)(2,1)}, u32[]{:S(2)}) copy-start(bf16[64,80,128]{2,1,0:T(8,128)(2,1)} %all-gather.3.cloned.1.call-done) | copy-start | bytes 3932164
  108.2 2.5 %copy-start.5 = (bf16[256,128]{1,0:T(8,128)(2,1)S(1)}, bf16[256,128]{1,0:T(8,128)(2,1)}, u32[]{:S(2)}) copy-start(bf16[256,128]{1,0:T(8,128)(2,1)} %pad_maximum_fusion.table_ref) | copy-start | bytes 196612
  (2 other events, 1.2 us)
Sparse Core Ops, SparseCore 0:
  49.4 25.6 all-gather.2

commit v3 on v2

--- a/solution.py
+++ b/solution.py
@@ -53,14 +53,12 @@
     return high, (value - high.astype(f32)).astype(bf16)
 
 
-def pair_tables():
-    table = dct_table()
-    empty = jnp.zeros_like(table)
-    wide = jnp.block([[table, empty], [empty, table]])
-    high = lax.reduce_precision(wide, exponent_bits=8, mantissa_bits=7)
-    low = wide - high
-    turned = jnp.concatenate([high.T, low.T], axis=0).astype(bf16)
-    return turned, jnp.concatenate([high, low], axis=1).astype(bf16)
+def wave_table():
+    turned = dct_table().T
+    high = lax.reduce_precision(turned, exponent_bits=8, mantissa_bits=7)
+    low = turned - high
+    empty = jnp.zeros_like(turned)
+    return jnp.block([[high, empty], [low, empty], [empty, high], [empty, low]]).astype(bf16)
 
 
 def dot(a, b, dims):
@@ -77,10 +75,22 @@
 
 
 def waves(table, spots):
-    at = lax.broadcasted_iota(jnp.int32, (pair, pair), 0)
-    chosen = jnp.where(at == spots, 1.0, 0.0).astype(bf16)
-    both = dot(table, chosen, ((1,), (0,)))
-    return both[:pair].astype(bf16), both[pair:].astype(bf16)
+    tiles = spots.shape[0] // 2
+    rows = jnp.concatenate([spots[at : at + 1] for at in range(tiles)], axis=1)
+    cols = jnp.concatenate([spots[at : at + 1] for at in range(tiles, 2 * tiles)], axis=1)
+    wide = (side, tiles * pair)
+    at = lax.broadcasted_iota(jnp.int32, wide, 0)
+    chosen = jnp.concatenate([jnp.where(at == rows, 1.0, 0.0), jnp.where(at == cols, 1.0, 0.0)], axis=0)
+    found = dot(table, chosen.astype(bf16), ((1,), (0,)))
+    block = lax.broadcasted_iota(jnp.int32, wide, 1) // 32 % 4
+
+    def placed(value, second):
+        return jnp.concatenate([jnp.where(second, 0.0, value), jnp.where(second, value, 0.0)], axis=0)
+
+    below, right = block >= 2, block % 2 == 1
+    row_high = placed(found[:side], below).astype(bf16)
+    row_low = placed(found[side : 2 * side], below).astype(bf16)
+    return row_high, row_low, placed(found[2 * side : 3 * side] + found[3 * side :], right)
 
 
 def coded(value):
@@ -109,7 +119,7 @@
         at = slice(line * 2 * rows, (line + 1) * 2 * rows)
         normed = (hidden_ref[:, at].astype(f32) * scale * gain_ref[:, at]).astype(bf16)
         term = dot(normed, cot, ((0,), (0,)))
-        high_ref[line], low_ref[line] = split2(term)
+        high_ref[line], low_ref[line] = split2(dot(cot, normed, ((0,), (0,))))
         for half in range(2):
             own = term[half * rows : (half + 1) * rows]
             message_ref[line, half, 0:rows, :], message_ref[line, half, rows:tall, :] = coded(own)
@@ -129,8 +139,8 @@
     lines, rows = owners // 2, features // owners
     outs = (
         pltpu.HBM((lines, 2, rows + 16, pair), jnp.int16),
-        pltpu.HBM((lines, 2 * rows, pair), bf16),
-        pltpu.HBM((lines, 2 * rows, pair), bf16),
+        pltpu.HBM((lines, pair, 2 * rows), bf16),
+        pltpu.HBM((lines, pair, 2 * rows), bf16),
     )
     return pl.pallas_call(
         front_kernel,
@@ -145,26 +155,29 @@
     )(hidden, gain, cot)
 
 
-def own_kernel(table_ref, row_ref, col_ref, momentum_ref, row_waves_ref, col_waves_ref, picked_ref):
-    for q in range(row_ref.shape[0]):
-        row_high, row_low = waves(table_ref[...], row_ref[q : q + 1, :])
-        col_high, col_low = waves(table_ref[...], col_ref[q : q + 1, :])
-        row_waves = row_high.astype(f32) + row_low.astype(f32)
-        col_waves = col_high.astype(f32) + col_low.astype(f32)
-        row_waves_ref[q] = row_waves
-        col_waves_ref[q] = col_waves
+def own_kernel(table_ref, spots_ref, momentum_ref, row_waves_ref, col_waves_ref, picked_ref):
+    row_high, row_low, col_waves = waves(table_ref[...], spots_ref[...])
+    row_waves = row_high.astype(f32) + row_low.astype(f32)
+    for q in range(picked_ref.shape[0]):
+        at = slice(q * pair, (q + 1) * pair)
+        row_waves_ref[q] = row_waves[:, at]
+        col_waves_ref[q] = col_waves[:, at]
         tile = decay_rate * momentum_ref[q * pair : min((q + 1) * pair, momentum_ref.shape[0]), :]
         short = pair - tile.shape[0]
         if short:
             tile = jnp.concatenate([tile, jnp.zeros((short, pair), f32)], axis=0)
         half = lax.dot_general(
-            tile, row_waves, (((0,), (0,)), ((), ())), precision=lax.Precision.HIGHEST, preferred_element_type=f32
+            tile,
+            row_waves[:, at],
+            (((0,), (0,)), ((), ())),
+            precision=lax.Precision.HIGHEST,
+            preferred_element_type=f32,
         )
-        picked_ref[q : q + 1, :] = jnp.sum(half * col_waves, axis=0, keepdims=True)
-
-
-def own_waves(table, rows, cols, momentum):
-    tiles = rows.shape[0]
+        picked_ref[q : q + 1, :] = jnp.sum(half * col_waves[:, at], axis=0, keepdims=True)
+
+
+def own_waves(table, spots, momentum):
+    tiles = spots.shape[0] // 2
     return pl.pallas_call(
         own_kernel,
         out_shape=(
@@ -174,7 +187,7 @@
         ),
         cost_estimate=small,
         name="own_waves",
-    )(table, rows, cols, momentum)
+    )(table, spots, momentum)
 
 
 def pack_kernel(upper_ref, mine_ref, other_ref, _, out_ref):
@@ -198,16 +211,16 @@
     )(upper[None], mine, other, after)
 
 
-def block_offsets(spots):
-    block_in = lax.broadcasted_iota(jnp.int32, spots.shape, 1) // 32
-    is_row = lax.broadcasted_iota(jnp.int32, spots.shape, 0) % 16 < 8
-    return spots + side * jnp.where(is_row, block_in // 2, block_in % 2).astype(spots.dtype)
+def line_spots(spots_ref, line, tiles):
+    tall = spots_ref.shape[1]
+    spots = spots_ref[line, tall - 16 : tall, :].astype(f32).astype(jnp.int32)
+    return jnp.concatenate([spots[:tiles], spots[8 : 8 + tiles]], axis=0)
 
 
 def pick_kernel(
     table_ref, spots_ref, high_in_ref, low_in_ref, decayed_ref, picked_ref, high_ref, low_ref, high_done, low_done
 ):
-    lines, tall, _ = spots_ref.shape
+    lines = spots_ref.shape[0]
     tiles = picked_ref.shape[0]
     each = tiles // lines
     arrivals = []
@@ -216,28 +229,21 @@
         arrivals.append(pltpu.make_async_copy(low_in_ref.at[line], low_ref.at[line], low_done.at[line]))
         arrivals[-2].start()
         arrivals[-1].start()
-    spots = [spots_ref[line, tall - 16 : tall, :].astype(f32) for line in range(lines)]
-    spots = jnp.transpose(block_offsets(jnp.concatenate(spots, axis=0)))
-    across = lax.broadcasted_iota(jnp.int32, (pair, pair), 1)
-    lane = across.astype(f32)
     table = table_ref[...]
-    picked = jnp.zeros((pair, pair), f32)
     for line in range(lines):
+        row_high, row_low, col_waves = waves(table, line_spots(spots_ref, line, each))
         arrivals[2 * line].wait()
         arrivals[2 * line + 1].wait()
         for tile in range(each):
-            chosen = []
-            for at in (line * 16 + tile, line * 16 + 8 + tile):
-                chosen.append(jnp.where(lane == spots[:, at : at + 1], 1.0, 0.0).astype(bf16))
-            rows = dot(chosen[0], table, ((1,), (0,))).astype(bf16)
-            cols = dot(chosen[1], table, ((1,), (0,)))
+            q = line * each + tile
             at = slice(tile * pair, (tile + 1) * pair)
-            high = high_ref[line, at, :]
-            half = dot(rows, jnp.concatenate([high, high], axis=0), ((1,), (0,)))
-            half += dot(rows[:, :pair], low_ref[line, at, :], ((1,), (0,)))
-            found = jnp.sum(half * (cols[:, :pair] + cols[:, pair:]), axis=1, keepdims=True)
-            picked = jnp.where(across == line * each + tile, found, picked)
-    picked_ref[...] = jnp.transpose(picked)[:tiles] + decayed_ref[...]
+            high = high_ref[line, :, at]
+            both = jnp.concatenate([high, low_ref[line, :, at]], axis=1)
+            half = dot(both, jnp.concatenate([row_high[:, at], row_high[:, at]], axis=0), ((1,), (0,)))
+            half += dot(high, row_low[:, at], ((1,), (0,)))
+            picked_ref[q : q + 1, :] = decayed_ref[q : q + 1, :] + jnp.sum(
+                half * col_waves[:, at], axis=0, keepdims=True
+            )
 
 
 def pick(table, spots, high, low, decayed):
@@ -317,6 +323,24 @@
     )(own_sum, rest, momentum, row_waves, col_waves)
 
 
+def fold_kernel(parts_ref, _, out_ref):
+    total = parts_ref[0]
+    for part in range(1, parts_ref.shape[0]):
+        total += parts_ref[part]
+    for target in range(out_ref.shape[0]):
+        out_ref[target] = total
+
+
+def fold(parts, after):
+    return pl.pallas_call(
+        fold_kernel,
+        out_shape=jax.ShapeDtypeStruct((4,) + parts.shape[1:], f32),
+        in_specs=[in_vmem, pl.BlockSpec(memory_space=pl.ANY)],
+        cost_estimate=small,
+        name="fold",
+    )(parts, after)
+
+
 def weight_rows(parts_ref, line):
     parts = [parts_ref[part, line].astype(f32) for part in range(parts_ref.shape[0])]
     eighth = parts[0].shape[0] // 2
@@ -324,7 +348,7 @@
 
 
 def weight_kernel(nodes, table_ref, spots_ref, total_ref, parts_ref, out_ref):
-    lines, tall, _ = spots_ref.shape
+    lines = spots_ref.shape[0]
     total = total_ref[0]
     for part in range(1, total_ref.shape[0]):
         total += total_ref[part]
@@ -333,17 +357,19 @@
     table = table_ref[...]
     for line in range(lines):
         weight = weight_rows(parts_ref, line)
-        spots = block_offsets(spots_ref[line, tall - 16 : tall, :].astype(f32).astype(jnp.int32))
+        row_high, row_low, col_waves = waves(table, line_spots(spots_ref, line, each))
+        mean = jnp.concatenate([total[line * each + tile : line * each + tile + 1] for tile in range(each)], axis=1)
+        high, low = split2(mean * col_waves)
         for tile in range(each):
             q = line * each + tile
-            row_high, row_low = waves(table, spots[tile : tile + 1])
-            col_high, col_low = waves(table, spots[8 + tile : 9 + tile])
-            high, low = split2(total[q : q + 1, :] * (col_high.astype(f32) + col_low.astype(f32)))
+            at = slice(tile * pair, (tile + 1) * pair)
             field = dot(
-                jnp.concatenate([row_high, row_low], axis=1), jnp.concatenate([high, high], axis=1), ((1,), (1,))
+                jnp.concatenate([row_high[:, at], row_low[:, at]], axis=1),
+                jnp.concatenate([high[:, at], high[:, at]], axis=1),
+                ((1,), (1,)),
             )
-            field += dot(row_high, low, ((1,), (1,)))
-            fresh = weight[tile * pair : (tile + 1) * pair] - learn_rate * jnp.tanh(field)
+            field += dot(row_high[:, at], low[:, at], ((1,), (1,)))
+            fresh = weight[at] - learn_rate * jnp.tanh(field)
             out_ref[q * pair : (q + 1) * pair, :] = fresh.astype(bf16)
 
 
@@ -393,7 +419,7 @@
     node, local = lax.axis_index("node"), lax.axis_index("local")
     features = hidden.shape[1]
     own_rows, head = weight.shape
-    turned, table = pair_tables()
+    table = wave_table()
     blocks = indices.size
     row_of, col_of = indices // side, indices % side
 
@@ -411,12 +437,10 @@
 
     spare = (-blocks) % pair
     tiles = (blocks + spare) // pair
-    own_at = jnp.pad(indices.reshape(-1), (0, spare)).reshape(tiles, pair)
-    block_in = (jnp.arange(pair, dtype=jnp.int32) // 32)[None, :]
-    place = lambda rows, cols: (rows + side * (block_in // 2), cols + side * (block_in % 2))
-    own_row, own_col = place(own_at // side, own_at % side)
+    own_spots = jnp.stack([row_of.reshape(-1), col_of.reshape(-1)])
+    own_spots = jnp.pad(own_spots, ((0, 0), (0, spare))).reshape(2 * tiles, pair)
     own_momentum = momentum[0]
-    row_waves, col_waves, decayed = own_waves(turned, own_row, own_col, own_momentum)
+    row_waves, col_waves, decayed = own_waves(table, own_spots, own_momentum)
     decayed = lax.dynamic_update_slice(
         jnp.zeros((owners * blocks,), f32), decayed.reshape(-1)[:blocks], (local * blocks,)
     ).reshape(-1, pair)
@@ -436,10 +460,7 @@
         total = total + hop(total, lambda x, y, z, c: (x, y ^ 3 if y in (0, 3, 4, 7) else 7 - y, z, c))
     own_sum, rest, spread = middle(arrived, upper, total)
     with jax.named_scope("coefficients_over_z"):
-        totals = jnp.sum(over_z(spread), axis=0)
-    with jax.named_scope("coefficients_over_x"):
-        totals = jnp.broadcast_to(totals[None], (4,) + totals.shape)
-        totals = lax.all_to_all(totals, "node", 0, 0, axis_index_groups=x_groups)
+        totals = over_z(spread)
     with jax.named_scope("gradient_over_y"):
         rest = hop(rest, lambda x, y, z, c: (x, (y + 4) % 8, z, c))
 
@@ -447,8 +468,10 @@
         parts = lax.all_gather(gathered[:, : 2 * eighth, :], "node", axis_index_groups=x_core_groups)
 
     input_grad = input_grad_of(hidden, gain[None, :], cotangent, parts)
+    with jax.named_scope("coefficients_over_x"):
+        totals = lax.all_to_all(fold(totals, input_grad), "node", 0, 0, axis_index_groups=x_groups)
     new_momentum = new_momentum_of(own_sum, rest, own_momentum, row_waves, col_waves)[None]
-    new_weight = new_weight_of(turned, gathered, totals, parts, nodes)
+    new_weight = new_weight_of(table, gathered, totals, parts, nodes)
     return (new_weight, new_momentum, input_grad)
 
 

time: 129 us -> 119 us (0.922); the launches traced: 128 us -> 117 us
  Pallas kernels: 31.8 us -> 22.6 us
  starting transfers between devices: 45.9 us -> 43 us
  waiting for transfers between devices: 26.1 us -> 28 us
    pallas_call x1, Pallas kernels: 10.8 us -> 4.35 us  [new_weight_of(): pl.pallas_call(functools.partial(weight_kernel, nodes), out_shape=jax.Sha...]
    pallas_call x1, Pallas kernels: 8.3 us -> 4.21 us  [pick(): pl.pallas_call(pick_kernel, out_shape=jax.ShapeDtypeStruct(decayed.shape,...]
    all_to_all x3, starting transfers between devices: 20.5 us -> 17.4 us  [over_z(): return lax.all_to_all(value, 'local', 0, 0, axis_index_groups=z_groups)]
    all_to_all x1, waiting for transfers between devices: 0.01 us -> 1.64 us  [on_device(): lax.all_to_all(fold(totals, input_grad), 'node', 0, 0, axis_index_groups=...]
    pallas_call x0 -> x1, Pallas kernels: none -> 1.56 us  [fold(): pl.pallas_call(fold_kernel, out_shape=jax.ShapeDtypeStruct((4,) + parts.s...]
    unnamed x30 -> x34, local copies, waits for them, and re-layouts: 3.6 us -> 4.1 us
  transfers between devices with their start and end apart: 11 -> 11, of which waited for: 7 -> 8; matrix products, arithmetic and copies ran while one was open for 4% -> 3% of each run, Pallas kernels for 15% -> 14%
where the time goes in v3:
time: 119 us; the launch traced here: 117 us
  starting transfers between devices  43 us (36%)
  waiting for transfers between devices  28 us (24%)
  Pallas kernels  22.6 us (19%)
  between operations  14.3 us (12%)
  local copies, waits for them, and re-layouts  6.9 us (6%)
  other arithmetic  1.77 us (1%)
    ppermute x6, starting transfers between devices, hop(): return lax.ppermute(value, ('node', 'local'), whole_mesh(move))  20.7 us
    all_to_all x3, starting transfers between devices, over_z(): return lax.all_to_all(value, 'local', 0, 0, axis_index_groups=z_groups)  17.4 us
    all_to_all x3, waiting for transfers between devices, over_z(): return lax.all_to_all(value, 'local', 0, 0, axis_index_groups=z_groups)  13.8 us
    ppermute x6, waiting for transfers between devices, hop(): return lax.ppermute(value, ('node', 'local'), whole_mesh(move))  12.5 us
    all_to_all x1, starting transfers between devices, on_device(): lax.all_to_all(fold(totals, input_grad), 'node', 0, 0, axis_index_groups=...  4.76 us
    pallas_call x1, Pallas kernels, new_weight_of(): pl.pallas_call(functools.partial(weight_kernel, nodes), out_shape=jax.Sha...  4.35 us
    pallas_call x1, Pallas kernels, pick(): pl.pallas_call(pick_kernel, out_shape=jax.ShapeDtypeStruct(decayed.shape,...  4.21 us
    unnamed x34, local copies, waits for them, and re-layouts  4.1 us
  transfers between devices with their start and end apart: 11, of which 8 were waited for; matrix products, arithmetic and copies ran while one was open for 3% of the time, Pallas kernels for 14%

profile of v3, /device:TPU:6, one launch (start us, length us, event | category | flops | bytes accessed | tf_op | source)
XLA Modules:
  0.0 116.6 jit_solution(15329420189261982971)
XLA Ops:
  8.7 6.2 %collective-permute-start = (bf16[56,128]{1,0:T(8,128)(2,1)S(1)}, bf16[56,128]{1,0:T(8,128)(2,1)S(1)}, u32[]{:S(2)}, u32[]{:S(2)}) collective-permute-start(bf16[56,128]{1,0:T(8,128)(2,1)S(1)} %pad_maximum_fusion.mine_ref), channel_id=1, source_target_pairs={{0,65},{16,81},{2,67},{18,83},{4,69},{20,85},{6,71},{22,87},{8,73}... | collective-permute-start | bytes 43016 | tf_op jit(solution)/shard_map/weight_over_y/ppermute | solution.py:36
  16.6 2.1 %own_waves.1 = (f32[3,128,128]{2,1,0:T(8,128)}, f32[3,128,128]{2,1,0:T(8,128)}, f32[3,128]{1,0:T(4,128)}) custom-call(bf16[256,128]{1,0:T(8,128)(2,1)} %fusion.7.table_ref, s32[6,128]{1,0:T(8,128)} %reshape.43.spots_ref, f32[320,128]{1,0:T(8,128)} %bitcast.13), custom_call_target="tpu_custom_call" | custom-call | flops 1 | bytes 1 | tf_op jit(solution)/shard_map/own_waves/pallas_call | solution.py:181
  21.5 10.3 %all-to-all-start = ((bf16[8,96,128]{2,1,0:T(8,128)(2,1)}), bf16[8,96,128]{2,1,0:T(8,128)(2,1)S(1)}, u32[]{:S(2)}, u32[]{:S(2)}) async-start(bf16[8,96,128]{2,1,0:T(8,128)(2,1)} %pack.1), calls=%async_computation | async-start | bytes 393216 | tf_op jit(solution)/shard_map/weight_over_z/all_to_all | solution.py:40
  33.3 2.8 %front.1 = (s16[8,2,336,128]{3,2,1,0:T(8,128)(2,1)}, bf16[8,128,640]{2,1,0:T(8,128)(2,1)}, bf16[8,128,640]{2,1,0:T(8,128)(2,1)}) custom-call(bf16[128,5120]{1,0:T(8,128)(2,1)S(1)} %copy-done.1, f32[1,5120]{1,0:T(1,128)S(1)} %bitcast.17, bf16[128,128]{1,0:T(8,128)(2,1)S(1)} %copy-done.10), custom_call_target="tpu_custom_call" | custom-call | flops 1 | bytes 1 | tf_op jit(solution)/shard_map/front/pallas_call | solution.py:145
  36.1 5.9 %all-to-all-done.spots_ref = bf16[8,96,128]{2,1,0:T(8,128)(2,1)S(1)} async-done(((bf16[8,96,128]{2,1,0:T(8,128)(2,1)}), bf16[8,96,128]{2,1,0:T(8,128)(2,1)S(1)}, u32[]{:S(2)}, u32[]{:S(2)}) %all-to-all-start) | async-done | bytes 196640 | tf_op jit(solution)/shard_map/weight_over_z/all_to_all | solution.py:40
  42.0 3.7 %all-to-all-start.1 = ((s16[8,2,336,128]{3,2,1,0:T(8,128)(2,1)}), s16[8,2,336,128]{3,2,1,0:T(8,128)(2,1)S(1)}, u32[]{:S(2)}, u32[]{:S(2)}) async-start(s16[8,2,336,128]{3,2,1,0:T(8,128)(2,1)} %get-tuple-element.13), calls=%async_computation.1 | async-start | bytes 2752512 | tf_op jit(solution)/shard_map/gradient_exchange/all_to_all | solution.py:40
  46.5 4.2 %pick.1 = f32[40,128]{1,0:T(8,128)S(1)} custom-call(bf16[256,128]{1,0:T(8,128)(2,1)S(1)} %copy-done.4, bf16[8,96,128]{2,1,0:T(8,128)(2,1)S(1)} %all-to-all-done.spots_ref, bf16[8,128,640]{2,1,0:T(8,128)(2,1)} %get-tuple-element.14.high_in_ref, bf16[8,128,640]{2,1,0:T(8,128)(2,1)} %get-tuple-element.15.low_in_ref, f32[40,128]{1,0:T(8,128)S(1)} %bitcast.16), custom_call_target="tpu_custom_call" | custom-call | flops 1 | bytes 1 | tf_op jit(solution)/shard_map/pick/pallas_call | solution.py:251
  50.7 1.9 %collective-permute-start.1 = (f32[40,128]{1,0:T(8,128)S(1)}, f32[40,128]{1,0:T(8,128)S(1)}, u32[]{:S(2)}, u32[]{:S(2)}) collective-permute-start(f32[40,128]{1,0:T(8,128)S(1)} %pick.1), channel_id=1, source_target_pairs={{0,16},{16,0},{2,18},{18,2},{4,20},{20,4},{6,22},{22,6},{8,24},{24... | collective-permute-start | bytes 61448 | tf_op jit(solution)/shard_map/coefficients/ppermute | solution.py:36
  53.8 2.6 %collective-permute-start.2 = (f32[40,128]{1,0:T(8,128)S(1)}, f32[40,128]{1,0:T(8,128)S(1)}, u32[]{:S(2)}, u32[]{:S(2)}) collective-permute-start(f32[40,128]{1,0:T(8,128)S(1)} %add.76), channel_id=1, source_target_pairs={{0,32},{16,48},{2,34},{18,50},{4,36},{20,52},{6,38},{22,54},{8,40}... | collective-permute-start | bytes 61448 | tf_op jit(solution)/shard_map/coefficients/ppermute | solution.py:36
  56.4 3.1 %collective-permute-done.2 = f32[40,128]{1,0:T(8,128)S(1)} collective-permute-done((f32[40,128]{1,0:T(8,128)S(1)}, f32[40,128]{1,0:T(8,128)S(1)}, u32[]{:S(2)}, u32[]{:S(2)}) %collective-permute-start.2) | collective-permute-done | bytes 20512 | tf_op jit(solution)/shard_map/coefficients/ppermute | solution.py:36
  59.5 1.9 %collective-permute-start.3 = (f32[40,128]{1,0:T(8,128)S(1)}, f32[40,128]{1,0:T(8,128)S(1)}, u32[]{:S(2)}, u32[]{:S(2)}) collective-permute-start(f32[40,128]{1,0:T(8,128)S(1)} %add.77), channel_id=1, source_target_pairs={{0,97},{16,113},{2,99},{18,115},{4,101},{20,117},{6,103},{22,119},... | collective-permute-start | bytes 61448 | tf_op jit(solution)/shard_map/coefficients/ppermute | solution.py:36
  61.4 4.9 %collective-permute-done.3 = f32[40,128]{1,0:T(8,128)S(1)} collective-permute-done((f32[40,128]{1,0:T(8,128)S(1)}, f32[40,128]{1,0:T(8,128)S(1)}, u32[]{:S(2)}, u32[]{:S(2)}) %collective-permute-start.3) | collective-permute-done | bytes 20512 | tf_op jit(solution)/shard_map/coefficients/ppermute | solution.py:36
  66.3 4.1 %collective-permute-start.4 = (f32[40,128]{1,0:T(8,128)S(1)}, f32[40,128]{1,0:T(8,128)S(1)}, u32[]{:S(2)}, u32[]{:S(2)}) collective-permute-start(f32[40,128]{1,0:T(8,128)S(1)} %add.78), channel_id=1, source_target_pairs={{0,96},{16,112},{2,98},{18,114},{4,100},{20,116},{6,102},{22,118},... | collective-permute-start | bytes 61448 | tf_op jit(solution)/shard_map/coefficients/ppermute | solution.py:36
  70.5 3.3 %collective-permute-done.4 = f32[40,128]{1,0:T(8,128)S(1)} collective-permute-done((f32[40,128]{1,0:T(8,128)S(1)}, f32[40,128]{1,0:T(8,128)S(1)}, u32[]{:S(2)}, u32[]{:S(2)}) %collective-permute-start.4) | collective-permute-done | bytes 20512 | tf_op jit(solution)/shard_map/coefficients/ppermute | solution.py:36
  73.8 5.6 %all-to-all-done.1.message_ref = s16[8,2,336,128]{3,2,1,0:T(8,128)(2,1)S(1)} async-done(((s16[8,2,336,128]{3,2,1,0:T(8,128)(2,1)}), s16[8,2,336,128]{3,2,1,0:T(8,128)(2,1)S(1)}, u32[]{:S(2)}, u32[]{:S(2)}) %all-to-all-start.1) | async-done | bytes 1376288 | tf_op jit(solution)/shard_map/gradient_exchange/all_to_all | solution.py:40
  79.4 1.8 %middle.1 = (f32[320,128]{1,0:T(8,128)S(1)}, s16[336,128]{1,0:T(8,128)(2,1)}, f32[8,40,128]{2,1,0:T(8,128)}) custom-call(s32[1]{0:T(128)} %bitcast.upper_ref, s16[8,2,336,128]{3,2,1,0:T(8,128)(2,1)S(1)} %all-to-all-done.1.message_ref, f32[40,128]{1,0:T(8,128)S(1)} %add.79.total_ref), custom_call_target="tpu_custom_call" | custom-call | flops 1 | bytes 1 | tf_op jit(solution)/shard_map/middle/pallas_call | solution.py:283
  81.2 3.4 %all-to-all-start.2 = ((f32[8,40,128]{2,1,0:T(8,128)}), f32[8,40,128]{2,1,0:T(8,128)S(1)}, u32[]{:S(2)}, u32[]{:S(2)}) async-start(f32[8,40,128]{2,1,0:T(8,128)} %get-tuple-element.16), calls=%async_computation.2 | async-start | bytes 327680 | tf_op jit(solution)/shard_map/coefficients_over_z/all_to_all | solution.py:40
  84.6 4.0 %collective-permute-start.5 = (s16[336,128]{1,0:T(8,128)(2,1)}, s16[336,128]{1,0:T(8,128)(2,1)S(1)}, u32[]{:S(2)}, u32[]{:S(2)}) collective-permute-start(s16[336,128]{1,0:T(8,128)(2,1)} %get-tuple-element.18), channel_id=1, source_target_pairs={{0,1},{16,17},{2,3},{18,19},{4,5},{20,21},{6,7},{22,23},{8,9},{24,... | collective-permute-start | bytes 258056 | tf_op jit(solution)/shard_map/gradient_over_y/ppermute | solution.py:36
  90.0 2.4 %input_gradient.1._ = bf16[128,5120]{1,0:T(8,128)(2,1)} custom-call(bf16[128,5120]{1,0:T(8,128)(2,1)S(1)} %copy-done.1, f32[1,5120]{1,0:T(1,128)S(1)} %bitcast.18, bf16[128,128]{1,0:T(8,128)(2,1)S(1)} %copy-done.11, bf16[8,8,80,128]{3,2,1,0:T(8,128)(2,1)S(1)} %bitcast.11), custom_call_target="tpu_custom_call" | custom-call | flops 1 | bytes 1 | tf_op jit(solution)/shard_map/input_gradient/pallas_call | solution.py:407
  92.4 2.3 %all-to-all-done.2.parts_ref = f32[8,40,128]{2,1,0:T(8,128)S(1)} async-done(((f32[8,40,128]{2,1,0:T(8,128)}), f32[8,40,128]{2,1,0:T(8,128)S(1)}, u32[]{:S(2)}, u32[]{:S(2)}) %all-to-all-start.2) | async-done | bytes 163872 | tf_op jit(solution)/shard_map/coefficients_over_z/all_to_all | solution.py:40
  97.0 4.8 %all-to-all-start.3 = ((f32[4,40,128]{2,1,0:T(8,128)}), f32[4,40,128]{2,1,0:T(8,128)S(1)}, u32[]{:S(2)}, u32[]{:S(2)}) async-start(f32[4,40,128]{2,1,0:T(8,128)} %fold.1), calls=%async_computation.3 | async-start | bytes 163840 | tf_op jit(solution)/shard_map/coefficients_over_x/all_to_all | solution.py:472
  101.7 2.0 %momentum_step.1 = f32[320,128]{1,0:T(8,128)} custom-call(f32[320,128]{1,0:T(8,128)S(1)} %get-tuple-element.17.sum_ref, s16[336,128]{1,0:T(8,128)(2,1)S(1)} %collective-permute-done.5.rest_ref, f32[320,128]{1,0:T(8,128)S(1)} %bitcast.14, f32[3,128,128]{2,1,0:T(8,128)S(1)} %copy-done.6, f32[3,128,128]{2,1,0:T(8,128)S(1)} %copy-done.7), custom_call_target="tpu_custom_call" | custom-call | flops 1 | bytes 1 | tf_op jit(solution)/shard_map/momentum_step/pallas_call | solution.py:316
  103.7 1.6 %all-to-all-done.3.total_ref = f32[4,40,128]{2,1,0:T(8,128)S(1)} async-done(((f32[4,40,128]{2,1,0:T(8,128)}), f32[4,40,128]{2,1,0:T(8,128)S(1)}, u32[]{:S(2)}, u32[]{:S(2)}) %all-to-all-start.3) | async-done | bytes 81952 | tf_op jit(solution)/shard_map/coefficients_over_x/all_to_all | solution.py:472
  105.4 4.4 %weight_step.1 = bf16[5120,128]{1,0:T(8,128)(2,1)} custom-call(bf16[256,128]{1,0:T(8,128)(2,1)S(1)} %copy-done.4, bf16[8,96,128]{2,1,0:T(8,128)(2,1)S(1)} %all-to-all-done.spots_ref, f32[4,40,128]{2,1,0:T(8,128)S(1)} %all-to-all-done.3.total_ref, bf16[8,8,80,128]{3,2,1,0:T(8,128)(2,1)S(1)} %bitcast.12), custom_call_target="tpu_custom_call" | custom-call | flops 1 | bytes 1 | tf_op jit(solution)/shard_map/weight_step/pallas_call | solution.py:377
  (67 shorter events, 12.9 us)
Async XLA Ops:
  7.2 1.0 copy-start
  7.2 24.6 %copy-start.1 = (bf16[128,5120]{1,0:T(8,128)(2,1)S(1)}, bf16[128,5120]{1,0:T(8,128)(2,1)}, u32[]{:S(2)}) copy-start(bf16[128,5120]{1,0:T(8,128)(2,1)} %hidden_ref.3) | copy-start | bytes 3932164
  8.7 10.8 %copy-start.15 = (bf16[56,128]{1,0:T(8,128)(2,1)}, bf16[56,128]{1,0:T(8,128)(2,1)S(1)}, u32[]{:S(2)}) copy-start(bf16[56,128]{1,0:T(8,128)(2,1)S(1)} %pad_maximum_fusion.mine_ref) | copy-start | bytes 43012
  8.7 10.7 %collective-permute-start = (bf16[56,128]{1,0:T(8,128)(2,1)S(1)}, bf16[56,128]{1,0:T(8,128)(2,1)S(1)}, u32[]{:S(2)}, u32[]{:S(2)}) collective-permute-start(bf16[56,128]{1,0:T(8,128)(2,1)S(1)} %pad_maximum_fusion.mine_ref), channel_id=1, source_target_pairs={{0,65},{16,81},{2,67},{18,83},{4,69},{20,85},{6,71},{22,87},{8,73}... | collective-permute-start | bytes 43016 | tf_op jit(solution)/shard_map/weight_over_y/ppermute | solution.py:36
  21.5 20.5 %all-to-all-start = ((bf16[8,96,128]{2,1,0:T(8,128)(2,1)}), bf16[8,96,128]{2,1,0:T(8,128)(2,1)S(1)}, u32[]{:S(2)}, u32[]{:S(2)}) async-start(bf16[8,96,128]{2,1,0:T(8,128)(2,1)} %pack.1), calls=%async_computation | async-start | bytes 393216 | tf_op jit(solution)/shard_map/weight_over_z/all_to_all | solution.py:40
  31.8 0.8 copy-start.10
  42.0 4.5 %copy-start.4 = (bf16[256,128]{1,0:T(8,128)(2,1)S(1)}, bf16[256,128]{1,0:T(8,128)(2,1)}, u32[]{:S(2)}) copy-start(bf16[256,128]{1,0:T(8,128)(2,1)} %fusion.7.table_ref) | copy-start | bytes 196612
  42.0 4.5 %copy-start.9 = (f32[5120]{0:T(1024)S(1)}, f32[5120]{0:T(1024)}, u32[]{:S(2)}) copy-start(f32[5120]{0:T(1024)} %copy-done.8) | copy-start | bytes 61444
  42.0 37.4 %all-to-all-start.1 = ((s16[8,2,336,128]{3,2,1,0:T(8,128)(2,1)}), s16[8,2,336,128]{3,2,1,0:T(8,128)(2,1)S(1)}, u32[]{:S(2)}, u32[]{:S(2)}) async-start(s16[8,2,336,128]{3,2,1,0:T(8,128)(2,1)} %get-tuple-element.13), calls=%async_computation.1 | async-start | bytes 2752512 | tf_op jit(solution)/shard_map/gradient_exchange/all_to_all | solution.py:40
  45.7 42.9 %all-gather.3.cloned.1.call-start = ((), (), s32[]{:S(2)}) async-start(), calls=%async_computation.4 | async-start | bytes 1474560 | tf_op jit(solution)/shard_map/weight_over_x_and_core/all_gather | solution.py:468
  50.7 38.0 %copy-start.11 = (bf16[128,128]{1,0:T(8,128)(2,1)S(1)}, bf16[128,128]{1,0:T(8,128)(2,1)}, u32[]{:S(2)}) copy-start(bf16[128,128]{1,0:T(8,128)(2,1)} %cot_ref.3) | copy-start | bytes 98308
  50.7 38.0 %copy-start.13 = (f32[5120]{0:T(1024)S(1)}, f32[5120]{0:T(1024)}, u32[]{:S(2)}) copy-start(f32[5120]{0:T(1024)} %param.7) | copy-start | bytes 61444
  50.7 3.1 %collective-permute-start.1 = (f32[40,128]{1,0:T(8,128)S(1)}, f32[40,128]{1,0:T(8,128)S(1)}, u32[]{:S(2)}, u32[]{:S(2)}) collective-permute-start(f32[40,128]{1,0:T(8,128)S(1)} %pick.1), channel_id=1, source_target_pairs={{0,16},{16,0},{2,18},{18,2},{4,20},{20,4},{6,22},{22,6},{8,24},{24... | collective-permute-start | bytes 61448 | tf_op jit(solution)/shard_map/coefficients/ppermute | solution.py:36
  53.8 5.7 %collective-permute-start.2 = (f32[40,128]{1,0:T(8,128)S(1)}, f32[40,128]{1,0:T(8,128)S(1)}, u32[]{:S(2)}, u32[]{:S(2)}) collective-permute-start(f32[40,128]{1,0:T(8,128)S(1)} %add.76), channel_id=1, source_target_pairs={{0,32},{16,48},{2,34},{18,50},{4,36},{20,52},{6,38},{22,54},{8,40}... | collective-permute-start | bytes 61448 | tf_op jit(solution)/shard_map/coefficients/ppermute | solution.py:36
  59.5 6.9 %collective-permute-start.3 = (f32[40,128]{1,0:T(8,128)S(1)}, f32[40,128]{1,0:T(8,128)S(1)}, u32[]{:S(2)}, u32[]{:S(2)}) collective-permute-start(f32[40,128]{1,0:T(8,128)S(1)} %add.77), channel_id=1, source_target_pairs={{0,97},{16,113},{2,99},{18,115},{4,101},{20,117},{6,103},{22,119},... | collective-permute-start | bytes 61448 | tf_op jit(solution)/shard_map/coefficients/ppermute | solution.py:36
  66.3 7.5 %collective-permute-start.4 = (f32[40,128]{1,0:T(8,128)S(1)}, f32[40,128]{1,0:T(8,128)S(1)}, u32[]{:S(2)}, u32[]{:S(2)}) collective-permute-start(f32[40,128]{1,0:T(8,128)S(1)} %add.78), channel_id=1, source_target_pairs={{0,96},{16,112},{2,98},{18,114},{4,100},{20,116},{6,102},{22,118},... | collective-permute-start | bytes 61448 | tf_op jit(solution)/shard_map/coefficients/ppermute | solution.py:36
  81.2 13.5 %all-to-all-start.2 = ((f32[8,40,128]{2,1,0:T(8,128)}), f32[8,40,128]{2,1,0:T(8,128)S(1)}, u32[]{:S(2)}, u32[]{:S(2)}) async-start(f32[8,40,128]{2,1,0:T(8,128)} %get-tuple-element.16), calls=%async_computation.2 | async-start | bytes 327680 | tf_op jit(solution)/shard_map/coefficients_over_z/all_to_all | solution.py:40
  84.6 17.1 %collective-permute-start.5 = (s16[336,128]{1,0:T(8,128)(2,1)}, s16[336,128]{1,0:T(8,128)(2,1)S(1)}, u32[]{:S(2)}, u32[]{:S(2)}) collective-permute-start(s16[336,128]{1,0:T(8,128)(2,1)} %get-tuple-element.18), channel_id=1, source_target_pairs={{0,1},{16,17},{2,3},{18,19},{4,5},{20,21},{6,7},{22,23},{8,9},{24,... | collective-permute-start | bytes 258056 | tf_op jit(solution)/shard_map/gradient_over_y/ppermute | solution.py:36
  88.7 1.3 %copy-start.2 = (bf16[64,80,128]{2,1,0:T(8,128)(2,1)S(1)}, bf16[64,80,128]{2,1,0:T(8,128)(2,1)}, u32[]{:S(2)}) copy-start(bf16[64,80,128]{2,1,0:T(8,128)(2,1)} %all-gather.3.cloned.1.call-done) | copy-start | bytes 3932164
  90.0 11.7 %copy-start.7 = (f32[3,128,128]{2,1,0:T(8,128)S(1)}, f32[3,128,128]{2,1,0:T(8,128)}, u32[]{:S(2)}) copy-start(f32[3,128,128]{2,1,0:T(8,128)} %get-tuple-element.20.col_waves_ref) | copy-start | bytes 589828
  92.4 9.3 %copy-start.5 = (f32[1,320,128]{2,1,0:T(8,128)S(1)}, f32[1,320,128]{2,1,0:T(8,128)}, u32[]{:S(2)}) copy-start(f32[1,320,128]{2,1,0:T(8,128)} %param.10) | copy-start | bytes 491524
  92.4 9.3 %copy-start.6 = (f32[3,128,128]{2,1,0:T(8,128)S(1)}, f32[3,128,128]{2,1,0:T(8,128)}, u32[]{:S(2)}) copy-start(f32[3,128,128]{2,1,0:T(8,128)} %get-tuple-element.19.row_waves_ref) | copy-start | bytes 589828
  92.4 13.0 %copy-start.3 = (bf16[64,80,128]{2,1,0:T(8,128)(2,1)S(1)}, bf16[64,80,128]{2,1,0:T(8,128)(2,1)}, u32[]{:S(2)}) copy-start(bf16[64,80,128]{2,1,0:T(8,128)(2,1)} %all-gather.3.cloned.1.call-done) | copy-start | bytes 3932164
  97.0 8.4 %all-to-all-start.3 = ((f32[4,40,128]{2,1,0:T(8,128)}), f32[4,40,128]{2,1,0:T(8,128)S(1)}, u32[]{:S(2)}, u32[]{:S(2)}) async-start(f32[4,40,128]{2,1,0:T(8,128)} %fold.1), calls=%async_computation.3 | async-start | bytes 163840 | tf_op jit(solution)/shard_map/coefficients_over_x/all_to_all | solution.py:472
  (4 other events, 2.6 us)
Sparse Core Ops, SparseCore 0:
  48.7 25.7 all-gather.2

commit v4 on v3

--- a/solution.py
+++ b/solution.py
@@ -14,11 +14,10 @@
 pair = 128
 f32 = jnp.float32
 bf16 = jnp.bfloat16
-kernel_room = pltpu.CompilerParams(vmem_limit_bytes=24 * 2**20)
+kernel_room = pltpu.CompilerParams(vmem_limit_bytes=12 * 2**20)
 small = pl.CostEstimate(flops=1, bytes_accessed=1, transcendentals=0)
 
 z_groups = [[2 * z + h for z in range(8)] for h in range(2)]
-x_groups = [[8 * x + r for x in range(4)] for r in range(8)]
 x_core_groups = [[8 * x + 2 * r + c for x in range(4) for c in range(2)] for r in range(4)]
 
 
@@ -104,25 +103,66 @@
     return whole.astype(jnp.int32).astype(f32) * jnp.exp2(power.astype(jnp.int32)[0:1, :].astype(f32))
 
 
+def picked_from(tile, row_high, row_low, col_waves):
+    high, low = split2(tile)
+    half = dot(jnp.concatenate([high, low], axis=0), jnp.concatenate([row_high, row_high], axis=0), ((0,), (0,)))
+    half += dot(high, row_low, ((0,), (0,)))
+    return jnp.sum(half * col_waves, axis=0, keepdims=True)
+
+
+def field_from(picked, row_high, row_low, col_waves):
+    high, low = split2(picked * col_waves)
+    field = dot(jnp.concatenate([row_high, row_low], axis=1), jnp.concatenate([high, high], axis=1), ((1,), (1,)))
+    return field + dot(row_high, low, ((1,), (1,)))
+
+
 def front_kernel(
-    hidden_ref, gain_ref, cot_ref, message_out_ref, high_out_ref, low_out_ref,
-    message_ref, high_ref, low_ref, message_done, high_done, low_done,
+    table_ref, spots_ref, hidden_in_ref, gain_in_ref, cot_in_ref, momentum_in_ref,
+    message_out_ref, high_out_ref, low_out_ref, picked_ref,
+    hidden_ref, gain_ref, cot_ref, momentum_ref, message_ref, high_ref, low_ref,
+    read, hidden_read, message_done, high_done, low_done,
 ):
-    wide = hidden_ref[...].astype(f32)
-    features = wide.shape[1]
     lines, _, tall, _ = message_ref.shape
     rows = tall - 16
-    scale = lax.rsqrt(jnp.sum(wide * wide, axis=1, keepdims=True) * (1.0 / features) + epsilon)
+    features = hidden_ref.shape[1]
+    spans = [slice(line * 2 * rows, (line + 1) * 2 * rows) for line in range(lines)]
+    reads = [
+        pltpu.make_async_copy(source, target, read.at[at])
+        for at, (source, target) in enumerate(
+            [(momentum_in_ref, momentum_ref), (cot_in_ref, cot_ref), (gain_in_ref, gain_ref)]
+        )
+    ]
+    hidden_reads = [
+        pltpu.make_async_copy(hidden_in_ref.at[:, at], hidden_ref.at[:, at], hidden_read.at[line])
+        for line, at in enumerate(spans)
+    ]
+    for copy in reads + hidden_reads:
+        copy.start()
+    own = waves(table_ref[...], spots_ref[...])
+    reads[0].wait()
+    for q in range(picked_ref.shape[0]):
+        tile = decay_rate * momentum_ref[q * pair : min((q + 1) * pair, rows), :]
+        short = pair - tile.shape[0]
+        if short:
+            tile = jnp.concatenate([tile, jnp.zeros((short, pair), f32)], axis=0)
+        picked_ref[q : q + 1, :] = picked_from(tile, *[part[:, q * pair : (q + 1) * pair] for part in own])
+    square = jnp.zeros((hidden_ref.shape[0], 1), f32)
+    for line, at in enumerate(spans):
+        hidden_reads[line].wait()
+        wide = hidden_ref[:, at].astype(f32)
+        square += jnp.sum(wide * wide, axis=1, keepdims=True)
+    scale = lax.rsqrt(square * (1.0 / features) + epsilon)
+    reads[1].wait()
+    reads[2].wait()
     cot = cot_ref[...]
     copies = []
-    for line in range(lines):
-        at = slice(line * 2 * rows, (line + 1) * 2 * rows)
+    for line, at in enumerate(spans):
         normed = (hidden_ref[:, at].astype(f32) * scale * gain_ref[:, at]).astype(bf16)
         term = dot(normed, cot, ((0,), (0,)))
-        high_ref[line], low_ref[line] = split2(dot(cot, normed, ((0,), (0,))))
         for half in range(2):
             own = term[half * rows : (half + 1) * rows]
             message_ref[line, half, 0:rows, :], message_ref[line, half, rows:tall, :] = coded(own)
+        high_ref[line], low_ref[line] = split2(dot(cot, normed, ((0,), (0,))))
         for source, target, done in (
             (message_ref, message_out_ref, message_done),
             (high_ref, high_out_ref, high_done),
@@ -134,9 +174,10 @@
         copy.wait()
 
 
-def front(hidden, gain, cot, owners):
+def front(table, spots, hidden, gain, cot, momentum, owners):
     tokens, features = hidden.shape
     lines, rows = owners // 2, features // owners
+    ins = (hidden, gain, cot, momentum)
     outs = (
         pltpu.HBM((lines, 2, rows + 16, pair), jnp.int16),
         pltpu.HBM((lines, pair, 2 * rows), bf16),
@@ -144,71 +185,15 @@
     )
     return pl.pallas_call(
         front_kernel,
-        out_shape=outs,
-        in_specs=[in_vmem] * 3,
-        out_specs=(in_hbm,) * 3,
-        scratch_shapes=[pltpu.VMEM(out.shape, out.dtype) for out in outs]
-        + [pltpu.SemaphoreType.DMA((lines,))] * 3,
+        out_shape=outs + (jax.ShapeDtypeStruct((spots.shape[0] // 2, pair), f32),),
+        in_specs=[in_vmem, in_vmem] + [in_hbm] * 4,
+        out_specs=(in_hbm,) * 3 + (in_vmem,),
+        scratch_shapes=[pltpu.VMEM(value.shape, value.dtype) for value in ins + outs]
+        + [pltpu.SemaphoreType.DMA((count,)) for count in (3, lines, lines, lines, lines)],
         compiler_params=kernel_room,
         cost_estimate=small,
         name="front",
-    )(hidden, gain, cot)
-
-
-def own_kernel(table_ref, spots_ref, momentum_ref, row_waves_ref, col_waves_ref, picked_ref):
-    row_high, row_low, col_waves = waves(table_ref[...], spots_ref[...])
-    row_waves = row_high.astype(f32) + row_low.astype(f32)
-    for q in range(picked_ref.shape[0]):
-        at = slice(q * pair, (q + 1) * pair)
-        row_waves_ref[q] = row_waves[:, at]
-        col_waves_ref[q] = col_waves[:, at]
-        tile = decay_rate * momentum_ref[q * pair : min((q + 1) * pair, momentum_ref.shape[0]), :]
-        short = pair - tile.shape[0]
-        if short:
-            tile = jnp.concatenate([tile, jnp.zeros((short, pair), f32)], axis=0)
-        half = lax.dot_general(
-            tile,
-            row_waves[:, at],
-            (((0,), (0,)), ((), ())),
-            precision=lax.Precision.HIGHEST,
-            preferred_element_type=f32,
-        )
-        picked_ref[q : q + 1, :] = jnp.sum(half * col_waves[:, at], axis=0, keepdims=True)
-
-
-def own_waves(table, spots, momentum):
-    tiles = spots.shape[0] // 2
-    return pl.pallas_call(
-        own_kernel,
-        out_shape=(
-            jax.ShapeDtypeStruct((tiles, pair, pair), f32),
-            jax.ShapeDtypeStruct((tiles, pair, pair), f32),
-            jax.ShapeDtypeStruct((tiles, pair), f32),
-        ),
-        cost_estimate=small,
-        name="own_waves",
-    )(table, spots, momentum)
-
-
-def pack_kernel(upper_ref, mine_ref, other_ref, _, out_ref):
-    eighth = mine_ref.shape[0] - 16
-    mine, other = mine_ref[...].astype(f32), other_ref[...].astype(f32)
-    first = upper_ref[0] == 0
-    low = jnp.where(first, mine[:eighth], other[:eighth])
-    high = jnp.where(first, other[:eighth], mine[:eighth])
-    packed = jnp.concatenate([low, high, mine[eighth:] + other[eighth:]], axis=0).astype(bf16)
-    for target in range(out_ref.shape[0]):
-        out_ref[target] = packed
-
-
-def pack(upper, mine, other, after):
-    return pl.pallas_call(
-        pack_kernel,
-        out_shape=jax.ShapeDtypeStruct((8, 2 * mine.shape[0] - 16, pair), bf16),
-        in_specs=[in_smem, in_vmem, in_vmem, pl.BlockSpec(memory_space=pl.ANY)],
-        cost_estimate=small,
-        name="pack",
-    )(upper[None], mine, other, after)
+    )(table, spots, *[from_hbm(value) for value in ins])
 
 
 def line_spots(spots_ref, line, tiles):
@@ -296,34 +281,33 @@
     )(upper[None], message, total)
 
 
-def momentum_kernel(sum_ref, rest_ref, momentum_ref, row_waves_ref, col_waves_ref, out_ref, mid_ref):
+def momentum_kernel(table_ref, spots_ref, sum_ref, rest_ref, momentum_ref, out_ref, mid_ref):
     rows = out_ref.shape[0]
+    row_high, row_low, col_waves = waves(table_ref[...], spots_ref[...])
     total = decay_rate * momentum_ref[...] + sum_ref[...]
     mid_ref[0:rows, :] = total + decoded(rest_ref[0:rows, :], rest_ref[rows:, :])
     mid_ref[rows:, :] = jnp.zeros((mid_ref.shape[0] - rows, pair), f32)
-    highest = functools.partial(lax.dot_general, precision=lax.Precision.HIGHEST, preferred_element_type=f32)
-    for q in range(row_waves_ref.shape[0]):
-        tile = mid_ref[q * pair : (q + 1) * pair, :]
-        half = highest(tile, row_waves_ref[q], (((0,), (0,)), ((), ())))
-        picked = jnp.sum(half * col_waves_ref[q], axis=0, keepdims=True)
-        sent = highest(row_waves_ref[q], picked * col_waves_ref[q], (((1,), (1,)), ((), ())))
+    for q in range(mid_ref.shape[0] // pair):
+        at = slice(q * pair, (q + 1) * pair)
+        own = row_high[:, at], row_low[:, at], col_waves[:, at]
+        tile = mid_ref[at, :]
+        sent = field_from(picked_from(tile, *own), *own)
         left = min(pair, rows - q * pair)
         out_ref[q * pair : q * pair + left, :] = (tile - sent)[:left]
 
 
-def new_momentum_of(own_sum, rest, momentum, row_waves, col_waves):
-    tiles = row_waves.shape[0]
+def new_momentum_of(table, spots, own_sum, rest, momentum):
     return pl.pallas_call(
         momentum_kernel,
         out_shape=jax.ShapeDtypeStruct(momentum.shape, f32),
-        scratch_shapes=[pltpu.VMEM((tiles * pair, pair), f32)],
+        scratch_shapes=[pltpu.VMEM((spots.shape[0] // 2 * pair, pair), f32)],
         compiler_params=kernel_room,
         cost_estimate=small,
         name="momentum_step",
-    )(own_sum, rest, momentum, row_waves, col_waves)
-
-
-def fold_kernel(parts_ref, _, out_ref):
+    )(table, spots, own_sum, rest, momentum)
+
+
+def fold_kernel(parts_ref, _, __, out_ref):
     total = parts_ref[0]
     for part in range(1, parts_ref.shape[0]):
         total += parts_ref[part]
@@ -331,14 +315,15 @@
         out_ref[target] = total
 
 
-def fold(parts, after):
+def fold(parts, *after):
     return pl.pallas_call(
         fold_kernel,
-        out_shape=jax.ShapeDtypeStruct((4,) + parts.shape[1:], f32),
-        in_specs=[in_vmem, pl.BlockSpec(memory_space=pl.ANY)],
+        out_shape=jax.ShapeDtypeStruct((8,) + parts.shape[1:], f32),
+        in_specs=[in_vmem, in_hbm, in_hbm],
+        compiler_params=kernel_room,
         cost_estimate=small,
         name="fold",
-    )(parts, after)
+    )(parts, *[from_hbm(value) for value in after])
 
 
 def weight_rows(parts_ref, line):
@@ -359,16 +344,10 @@
         weight = weight_rows(parts_ref, line)
         row_high, row_low, col_waves = waves(table, line_spots(spots_ref, line, each))
         mean = jnp.concatenate([total[line * each + tile : line * each + tile + 1] for tile in range(each)], axis=1)
-        high, low = split2(mean * col_waves)
         for tile in range(each):
             q = line * each + tile
             at = slice(tile * pair, (tile + 1) * pair)
-            field = dot(
-                jnp.concatenate([row_high[:, at], row_low[:, at]], axis=1),
-                jnp.concatenate([high[:, at], high[:, at]], axis=1),
-                ((1,), (1,)),
-            )
-            field += dot(row_high[:, at], low[:, at], ((1,), (1,)))
+            field = field_from(mean[:, at], row_high[:, at], row_low[:, at], col_waves[:, at])
             fresh = weight[at] - learn_rate * jnp.tanh(field)
             out_ref[q * pair : (q + 1) * pair, :] = fresh.astype(bf16)
 
@@ -383,35 +362,52 @@
     )(table, spots, total, parts)
 
 
-def input_kernel(hidden_ref, gain_ref, cot_ref, parts_ref, out_ref, gained_ref):
+def input_kernel(
+    hidden_ref, gain_in_ref, cot_in_ref, parts_in_ref, out_ref, gain_ref, cot_ref, parts_ref, gained_ref, read
+):
+    lines = parts_ref.shape[1]
     features = hidden_ref.shape[1]
-    wide = hidden_ref[...].astype(f32)
-    scale = lax.rsqrt(jnp.sum(wide * wide, axis=1, keepdims=True) * (1.0 / features) + epsilon)
+    step = features // lines
+    spans = [slice(line * step, (line + 1) * step) for line in range(lines)]
+    reads = [
+        pltpu.make_async_copy(source, target, read.at[at])
+        for at, (source, target) in enumerate(
+            [(parts_in_ref, parts_ref), (cot_in_ref, cot_ref), (gain_in_ref, gain_ref)]
+        )
+    ]
+    for copy in reads:
+        copy.start()
+    square = jnp.zeros((hidden_ref.shape[0], 1), f32)
+    for at in spans:
+        wide = hidden_ref[:, at].astype(f32)
+        square += jnp.sum(wide * wide, axis=1, keepdims=True)
+    scale = lax.rsqrt(square * (1.0 / features) + epsilon)
+    for copy in reads:
+        copy.wait()
     cot = cot_ref[...]
-    lines = parts_ref.shape[1]
-    step = features // lines
     along = jnp.zeros(scale.shape, f32)
-    for piece in range(lines):
-        at = slice(piece * step, (piece + 1) * step)
-        weight = weight_rows(parts_ref, piece).astype(bf16)
+    for line, at in enumerate(spans):
+        weight = weight_rows(parts_ref, line).astype(bf16)
         gained = gain_ref[:, at] * dot(cot, weight, ((1,), (1,)))
         gained_ref[:, at] = gained
         along += jnp.sum(hidden_ref[:, at].astype(f32) * gained, axis=1, keepdims=True)
     factor = scale**3 * (along * (1.0 / features))
-    for piece in range(lines):
-        at = slice(piece * step, (piece + 1) * step)
+    for at in spans:
         out_ref[:, at] = (scale * gained_ref[:, at] - hidden_ref[:, at].astype(f32) * factor).astype(bf16)
 
 
 def input_grad_of(hidden, gain, cot, parts):
+    ins = (gain, cot, parts)
     return pl.pallas_call(
         input_kernel,
         out_shape=jax.ShapeDtypeStruct(hidden.shape, bf16),
-        scratch_shapes=[pltpu.VMEM(hidden.shape, f32)],
+        in_specs=[in_vmem] + [in_hbm] * 3,
+        scratch_shapes=[pltpu.VMEM(value.shape, value.dtype) for value in ins]
+        + [pltpu.VMEM(hidden.shape, f32), pltpu.SemaphoreType.DMA((3,))],
         compiler_params=kernel_room,
         cost_estimate=small,
         name="input_gradient",
-    )(hidden, gain, cot, parts)
+    )(hidden, *[from_hbm(value) for value in ins])
 
 
 def on_device(hidden, gain, cotangent, weight, momentum, indices):
@@ -421,7 +417,7 @@
     own_rows, head = weight.shape
     table = wave_table()
     blocks = indices.size
-    row_of, col_of = indices // side, indices % side
+    row_of, col_of = indices >> 6, indices & (side - 1)
 
     upper = local % 2
     eighth = own_rows // 8
@@ -432,29 +428,33 @@
             jnp.zeros((8 * pair,), jnp.int32), spots.reshape(-1), (upper * blocks,)
         ).reshape(8, pair)
         piece = jnp.concatenate([piece, at_half(row_of).astype(bf16), at_half(col_of).astype(bf16)], axis=0)
-    with jax.named_scope("weight_over_y"):
-        other = hop(piece, lambda x, y, z, c: (x, (y + (2 if y in (2, 3, 6, 7) else 6)) % 8, z, c))
+    with jax.named_scope("weight_over_z"):
+        gathered = over_z(jnp.broadcast_to(piece[None], (8,) + piece.shape))
 
     spare = (-blocks) % pair
     tiles = (blocks + spare) // pair
     own_spots = jnp.stack([row_of.reshape(-1), col_of.reshape(-1)])
     own_spots = jnp.pad(own_spots, ((0, 0), (0, spare))).reshape(2 * tiles, pair)
     own_momentum = momentum[0]
-    row_waves, col_waves, decayed = own_waves(table, own_spots, own_momentum)
+    message, high, low, decayed = front(
+        table, own_spots, hidden, gain[None, :], cotangent, own_momentum, owners
+    )
     decayed = lax.dynamic_update_slice(
         jnp.zeros((owners * blocks,), f32), decayed.reshape(-1)[:blocks], (local * blocks,)
     ).reshape(-1, pair)
 
-    with jax.named_scope("weight_over_z"):
-        gathered = over_z(pack(upper, piece, other, decayed))
-
-    message, high, low = front(hidden, gain[None, :], cotangent, owners)
     with jax.named_scope("gradient_exchange"):
         arrived = over_z(message)
 
-    total = pick(table, gathered, high, low, decayed)
+    with jax.named_scope("weight_over_y"):
+        other = hop(gathered, lambda x, y, z, c: (x, (y + (2 if y in (2, 3, 6, 7) else 6)) % 8, z, c))
+        spots = gathered[:, eighth:] + other[:, eighth:]
+        mine, other = gathered[:, None, :eighth], other[:, None, :eighth]
+        pieces = jnp.where(upper == 0, jnp.concatenate([mine, other], 1), jnp.concatenate([other, mine], 1))
+        pieces = pieces.reshape(8, 2 * eighth, head)
+
+    total = pick(table, spots, high, low, decayed)
     with jax.named_scope("coefficients"):
-        total = total + hop(total, lambda x, y, z, c: (x, y, z, 1 - c))
         total = total + hop(total, lambda x, y, z, c: (x, y ^ 1, z, c))
         total = total + hop(total, lambda x, y, z, c: (x, ((y + 1) ^ 1) - 1, z, c))
         total = total + hop(total, lambda x, y, z, c: (x, y ^ 3 if y in (0, 3, 4, 7) else 7 - y, z, c))
@@ -465,13 +465,13 @@
         rest = hop(rest, lambda x, y, z, c: (x, (y + 4) % 8, z, c))
 
     with jax.named_scope("weight_over_x_and_core"):
-        parts = lax.all_gather(gathered[:, : 2 * eighth, :], "node", axis_index_groups=x_core_groups)
+        parts = lax.all_gather(pieces, "node", axis_index_groups=x_core_groups)
 
     input_grad = input_grad_of(hidden, gain[None, :], cotangent, parts)
-    with jax.named_scope("coefficients_over_x"):
-        totals = lax.all_to_all(fold(totals, input_grad), "node", 0, 0, axis_index_groups=x_groups)
-    new_momentum = new_momentum_of(own_sum, rest, own_momentum, row_waves, col_waves)[None]
-    new_weight = new_weight_of(table, gathered, totals, parts, nodes)
+    with jax.named_scope("coefficients_over_x_and_core"):
+        totals = lax.all_to_all(fold(totals, rest, input_grad), "node", 0, 0, axis_index_groups=x_core_groups)
+    new_momentum = new_momentum_of(table, own_spots, own_sum, rest, own_momentum)[None]
+    new_weight = new_weight_of(table, spots, totals, parts, nodes)
     return (new_weight, new_momentum, input_grad)
 
 

time: 119 us -> 112 us (0.941)
  the two profiles are of different devices: /device:TPU:6 before, /device:TPU:48 now
where the time goes in v4:
time: 112 us
  starting transfers between devices  39.2 us (35%)
  waiting for transfers between devices  31.7 us (28%)
  Pallas kernels  21.5 us (19%)
  between operations  14.3 us (13%)
  local copies, waits for them, and re-layouts  3.81 us (3%)
    ppermute x5, waiting for transfers between devices, hop(): return lax.ppermute(value, ('node', 'local'), whole_mesh(move))  24.5 us
    all_to_all x3, starting transfers between devices, over_z(): return lax.all_to_all(value, 'local', 0, 0, axis_index_groups=z_groups)  21.1 us
    ppermute x5, starting transfers between devices, hop(): return lax.ppermute(value, ('node', 'local'), whole_mesh(move))  13.8 us
    pallas_call x1, Pallas kernels, front(): pl.pallas_call(front_kernel, out_shape=outs + (jax.ShapeDtypeStruct((spot...  5.02 us
    pallas_call x1, Pallas kernels, new_weight_of(): pl.pallas_call(functools.partial(weight_kernel, nodes), out_shape=jax.Sha...  4.35 us
    all_to_all x1, starting transfers between devices, on_device(): lax.all_to_all(fold(totals, rest, input_grad), 'node', 0, 0, axis_index_g...  4.3 us
    pallas_call x1, Pallas kernels, pick(): pl.pallas_call(pick_kernel, out_shape=jax.ShapeDtypeStruct(decayed.shape,...  4.21 us
    all_to_all x1, waiting for transfers between devices, on_device(): lax.all_to_all(fold(totals, rest, input_grad), 'node', 0, 0, axis_index_g...  3.87 us
  transfers between devices with their start and end apart: 10, of which 7 were waited for; matrix products, arithmetic and copies ran while one was open for 1% of the time, Pallas kernels for 15%

profile of v4, /device:TPU:48, one launch (start us, length us, event | category | flops | bytes accessed | tf_op | source)
XLA Modules:
  0.0 111.5 jit_solution(1125352442164678077)
XLA Ops:
  7.2 0.7 broadcast_shift-right-arithmetic_fusion
  9.2 10.3 %all-to-all-start = ((bf16[8,56,128]{2,1,0:T(8,128)(2,1)}), bf16[8,56,128]{2,1,0:T(8,128)(2,1)S(1)}, u32[]{:S(2)}, u32[]{:S(2)}) async-start(bf16[8,56,128]{2,1,0:T(8,128)(2,1)} %broadcast_in_dim.38), calls=%async_computation | async-start | bytes 229376 | tf_op jit(solution)/shard_map/weight_over_z/all_to_all | solution.py:39
  20.0 5.0 %front.1 = (s16[8,2,336,128]{3,2,1,0:T(8,128)(2,1)}, bf16[8,128,640]{2,1,0:T(8,128)(2,1)}, bf16[8,128,640]{2,1,0:T(8,128)(2,1)}, f32[3,128]{1,0:T(4,128)S(1)}) custom-call(bf16[256,128]{1,0:T(8,128)(2,1)S(1)} %fusion.7.table_ref, s32[6,128]{1,0:T(8,128)S(1)} %reshape.64.spots_ref, bf16[128,5120]{1,0:T(8,128)(2,1)} %hidden_ref.1, f32[1,5120]{1,0:T(1,128)} %bitcast.21, ...), custom_call_target="tpu_custom_call" | custom-call | flops 1 | bytes 1 | tf_op jit(solution)/shard_map/front/pallas_call | solution.py:186
  25.1 3.4 %all-to-all-done = bf16[8,56,128]{2,1,0:T(8,128)(2,1)S(1)} async-done(((bf16[8,56,128]{2,1,0:T(8,128)(2,1)}), bf16[8,56,128]{2,1,0:T(8,128)(2,1)S(1)}, u32[]{:S(2)}, u32[]{:S(2)}) %all-to-all-start) | async-done | bytes 114720 | tf_op jit(solution)/shard_map/weight_over_z/all_to_all | solution.py:39
  28.4 3.9 %all-to-all-start.1 = ((s16[8,2,336,128]{3,2,1,0:T(8,128)(2,1)}), s16[8,2,336,128]{3,2,1,0:T(8,128)(2,1)S(1)}, u32[]{:S(2)}, u32[]{:S(2)}) async-start(s16[8,2,336,128]{3,2,1,0:T(8,128)(2,1)} %get-tuple-element.10), calls=%async_computation.1 | async-start | bytes 2752512 | tf_op jit(solution)/shard_map/gradient_exchange/all_to_all | solution.py:39
  32.3 1.9 %collective-permute-start = (bf16[8,56,128]{2,1,0:T(8,128)(2,1)S(1)}, bf16[8,56,128]{2,1,0:T(8,128)(2,1)S(1)}, u32[]{:S(2)}, u32[]{:S(2)}) collective-permute-start(bf16[8,56,128]{2,1,0:T(8,128)(2,1)S(1)} %all-to-all-done), channel_id=1, source_target_pairs={{0,65},{16,81},{2,67},{18,83},{4,69},{20,85},{6,71},{22,87},{8,73}... | collective-permute-start | bytes 344072 | tf_op jit(solution)/shard_map/weight_over_y/ppermute | solution.py:35
  34.3 8.6 %collective-permute-done = bf16[8,56,128]{2,1,0:T(8,128)(2,1)S(1)} collective-permute-done((bf16[8,56,128]{2,1,0:T(8,128)(2,1)S(1)}, bf16[8,56,128]{2,1,0:T(8,128)(2,1)S(1)}, u32[]{:S(2)}, u32[]{:S(2)}) %collective-permute-start) | collective-permute-done | bytes 114720 | tf_op jit(solution)/shard_map/weight_over_y/ppermute | solution.py:35
  43.7 4.2 %pick.1 = f32[40,128]{1,0:T(8,128)S(1)} custom-call(bf16[256,128]{1,0:T(8,128)(2,1)S(1)} %fusion.7.table_ref, bf16[8,16,128]{2,1,0:T(8,128)(2,1)S(1)} %slice_add_fusion.spots_ref, bf16[8,128,640]{2,1,0:T(8,128)(2,1)} %get-tuple-element.11.high_in_ref, bf16[8,128,640]{2,1,0:T(8,128)(2,1)} %get-tuple-element.12.low_in_ref, f32[40,128]{1,0:T(8,128)S(1)} %bitcast.17), custom_call_target="tpu_custom_call" | custom-call | flops 1 | bytes 1 | tf_op jit(solution)/shard_map/pick/pallas_call | solution.py:236
  48.0 2.1 %collective-permute-start.1 = (f32[40,128]{1,0:T(8,128)S(1)}, f32[40,128]{1,0:T(8,128)S(1)}, u32[]{:S(2)}, u32[]{:S(2)}) collective-permute-start(f32[40,128]{1,0:T(8,128)S(1)} %pick.1), channel_id=1, source_target_pairs={{0,32},{16,48},{2,34},{18,50},{4,36},{20,52},{6,38},{22,54},{8,40}... | collective-permute-start | bytes 61448 | tf_op jit(solution)/shard_map/coefficients/ppermute | solution.py:35
  50.0 3.7 %collective-permute-done.1 = f32[40,128]{1,0:T(8,128)S(1)} collective-permute-done((f32[40,128]{1,0:T(8,128)S(1)}, f32[40,128]{1,0:T(8,128)S(1)}, u32[]{:S(2)}, u32[]{:S(2)}) %collective-permute-start.1) | collective-permute-done | bytes 20512 | tf_op jit(solution)/shard_map/coefficients/ppermute | solution.py:35
  53.8 3.2 %collective-permute-start.2 = (f32[40,128]{1,0:T(8,128)S(1)}, f32[40,128]{1,0:T(8,128)S(1)}, u32[]{:S(2)}, u32[]{:S(2)}) collective-permute-start(f32[40,128]{1,0:T(8,128)S(1)} %add.69), channel_id=1, source_target_pairs={{0,97},{16,113},{2,99},{18,115},{4,101},{20,117},{6,103},{22,119},... | collective-permute-start | bytes 61448 | tf_op jit(solution)/shard_map/coefficients/ppermute | solution.py:35
  57.0 2.4 %collective-permute-done.2 = f32[40,128]{1,0:T(8,128)S(1)} collective-permute-done((f32[40,128]{1,0:T(8,128)S(1)}, f32[40,128]{1,0:T(8,128)S(1)}, u32[]{:S(2)}, u32[]{:S(2)}) %collective-permute-start.2) | collective-permute-done | bytes 20512 | tf_op jit(solution)/shard_map/coefficients/ppermute | solution.py:35
  59.5 2.8 %collective-permute-start.3 = (f32[40,128]{1,0:T(8,128)S(1)}, f32[40,128]{1,0:T(8,128)S(1)}, u32[]{:S(2)}, u32[]{:S(2)}) collective-permute-start(f32[40,128]{1,0:T(8,128)S(1)} %add.70), channel_id=1, source_target_pairs={{0,96},{16,112},{2,98},{18,114},{4,100},{20,116},{6,102},{22,118},... | collective-permute-start | bytes 61448 | tf_op jit(solution)/shard_map/coefficients/ppermute | solution.py:35
  62.3 5.9 %collective-permute-done.3 = f32[40,128]{1,0:T(8,128)S(1)} collective-permute-done((f32[40,128]{1,0:T(8,128)S(1)}, f32[40,128]{1,0:T(8,128)S(1)}, u32[]{:S(2)}, u32[]{:S(2)}) %collective-permute-start.3) | collective-permute-done | bytes 20512 | tf_op jit(solution)/shard_map/coefficients/ppermute | solution.py:35
  68.1 1.8 %middle.1 = (f32[320,128]{1,0:T(8,128)S(1)}, s16[336,128]{1,0:T(8,128)(2,1)}, f32[8,40,128]{2,1,0:T(8,128)}) custom-call(s32[1]{0:T(128)} %bitcast.2.upper_ref, s16[8,2,336,128]{3,2,1,0:T(8,128)(2,1)S(1)} %all-to-all-done.1.message_ref, f32[40,128]{1,0:T(8,128)S(1)} %add.71.total_ref), custom_call_target="tpu_custom_call" | custom-call | flops 1 | bytes 1 | tf_op jit(solution)/shard_map/middle/pallas_call | solution.py:268
  69.9 6.9 %all-to-all-start.2 = ((f32[8,40,128]{2,1,0:T(8,128)}), f32[8,40,128]{2,1,0:T(8,128)S(1)}, u32[]{:S(2)}, u32[]{:S(2)}) async-start(f32[8,40,128]{2,1,0:T(8,128)} %get-tuple-element.14), calls=%async_computation.2 | async-start | bytes 327680 | tf_op jit(solution)/shard_map/coefficients_over_z/all_to_all | solution.py:39
  76.8 3.8 %collective-permute-start.4 = (s16[336,128]{1,0:T(8,128)(2,1)}, s16[336,128]{1,0:T(8,128)(2,1)S(1)}, u32[]{:S(2)}, u32[]{:S(2)}) collective-permute-start(s16[336,128]{1,0:T(8,128)(2,1)} %get-tuple-element.15), channel_id=1, source_target_pairs={{0,1},{16,17},{2,3},{18,19},{4,5},{20,21},{6,7},{22,23},{8,9},{24,... | collective-permute-start | bytes 258056 | tf_op jit(solution)/shard_map/gradient_over_y/ppermute | solution.py:35
  80.7 3.7 %input_gradient.1.__ = bf16[128,5120]{1,0:T(8,128)(2,1)} custom-call(bf16[128,5120]{1,0:T(8,128)(2,1)S(1)} %copy-done.1, f32[1,5120]{1,0:T(1,128)} %bitcast.22, bf16[128,128]{1,0:T(8,128)(2,1)} %cot_in_ref.3, bf16[8,8,80,128]{3,2,1,0:T(8,128)(2,1)} %all-gather.2.cloned.1.call-done.parts_in_ref.parts_ref), custom_call_target="tpu_custom_call" | custom-call | flops 1 | bytes 1 | tf_op jit(solution)/shard_map/input_gradient/pallas_call | solution.py:401
  84.4 3.8 %collective-permute-done.4._.rest_ref = s16[336,128]{1,0:T(8,128)(2,1)S(1)} collective-permute-done((s16[336,128]{1,0:T(8,128)(2,1)}, s16[336,128]{1,0:T(8,128)(2,1)S(1)}, u32[]{:S(2)}, u32[]{:S(2)}) %collective-permute-start.4) | collective-permute-done | bytes 86048 | tf_op jit(solution)/shard_map/gradient_over_y/ppermute | solution.py:35
  89.5 4.3 %all-to-all-start.3 = ((f32[8,40,128]{2,1,0:T(8,128)}), f32[8,40,128]{2,1,0:T(8,128)S(1)}, u32[]{:S(2)}, u32[]{:S(2)}) async-start(f32[8,40,128]{2,1,0:T(8,128)} %fold.1), calls=%async_computation.3 | async-start | bytes 327680 | tf_op jit(solution)/shard_map/coefficients_over_x_and_core/all_to_all | solution.py:472
  93.8 0.9 copy-done.5
  94.7 1.7 %momentum_step.1 = f32[320,128]{1,0:T(8,128)} custom-call(bf16[256,128]{1,0:T(8,128)(2,1)S(1)} %fusion.7.table_ref, s32[6,128]{1,0:T(8,128)S(1)} %reshape.64.spots_ref, f32[320,128]{1,0:T(8,128)S(1)} %get-tuple-element.16.sum_ref, s16[336,128]{1,0:T(8,128)(2,1)S(1)} %copy-done.5, f32[320,128]{1,0:T(8,128)S(1)} %bitcast.16), custom_call_target="tpu_custom_call" | custom-call | flops 1 | bytes 1 | tf_op jit(solution)/shard_map/momentum_step/pallas_call | solution.py:300
  96.5 3.9 %all-to-all-done.3.total_ref = f32[8,40,128]{2,1,0:T(8,128)S(1)} async-done(((f32[8,40,128]{2,1,0:T(8,128)}), f32[8,40,128]{2,1,0:T(8,128)S(1)}, u32[]{:S(2)}, u32[]{:S(2)}) %all-to-all-start.3) | async-done | bytes 163872 | tf_op jit(solution)/shard_map/coefficients_over_x_and_core/all_to_all | solution.py:472
  100.3 4.4 %weight_step.1 = bf16[5120,128]{1,0:T(8,128)(2,1)} custom-call(bf16[256,128]{1,0:T(8,128)(2,1)S(1)} %fusion.7.table_ref, bf16[8,16,128]{2,1,0:T(8,128)(2,1)S(1)} %slice_add_fusion.spots_ref, f32[8,40,128]{2,1,0:T(8,128)S(1)} %all-to-all-done.3.total_ref, bf16[8,8,80,128]{3,2,1,0:T(8,128)(2,1)S(1)} %copy-done.2), custom_call_target="tpu_custom_call" | custom-call | flops 1 | bytes 1 | tf_op jit(solution)/shard_map/weight_step/pallas_call | solution.py:356
  (45 shorter events, 4.0 us)
Async XLA Ops:
  7.2 0.9 copy-start
  9.2 19.2 %all-to-all-start = ((bf16[8,56,128]{2,1,0:T(8,128)(2,1)}), bf16[8,56,128]{2,1,0:T(8,128)(2,1)S(1)}, u32[]{:S(2)}, u32[]{:S(2)}) async-start(bf16[8,56,128]{2,1,0:T(8,128)(2,1)} %broadcast_in_dim.38), calls=%async_computation | async-start | bytes 229376 | tf_op jit(solution)/shard_map/weight_over_z/all_to_all | solution.py:39
  28.4 39.7 %all-to-all-start.1 = ((s16[8,2,336,128]{3,2,1,0:T(8,128)(2,1)}), s16[8,2,336,128]{3,2,1,0:T(8,128)(2,1)S(1)}, u32[]{:S(2)}, u32[]{:S(2)}) async-start(s16[8,2,336,128]{3,2,1,0:T(8,128)(2,1)} %get-tuple-element.10), calls=%async_computation.1 | async-start | bytes 2752512 | tf_op jit(solution)/shard_map/gradient_exchange/all_to_all | solution.py:39
  32.3 48.4 %all-gather.2.cloned.1.call-start = ((), (), s32[]{:S(2)}) async-start(), calls=%async_computation.4 | async-start | bytes 1474560 | tf_op jit(solution)/shard_map/weight_over_x_and_core/all_gather | solution.py:468
  32.3 10.5 %collective-permute-start = (bf16[8,56,128]{2,1,0:T(8,128)(2,1)S(1)}, bf16[8,56,128]{2,1,0:T(8,128)(2,1)S(1)}, u32[]{:S(2)}, u32[]{:S(2)}) collective-permute-start(bf16[8,56,128]{2,1,0:T(8,128)(2,1)S(1)} %all-to-all-done), channel_id=1, source_target_pairs={{0,65},{16,81},{2,67},{18,83},{4,69},{20,85},{6,71},{22,87},{8,73}... | collective-permute-start | bytes 344072 | tf_op jit(solution)/shard_map/weight_over_y/ppermute | solution.py:35
  48.0 32.7 %copy-start.1 = (bf16[128,5120]{1,0:T(8,128)(2,1)S(1)}, bf16[128,5120]{1,0:T(8,128)(2,1)}, u32[]{:S(2)}) copy-start(bf16[128,5120]{1,0:T(8,128)(2,1)} %hidden_ref.1) | copy-start | bytes 3932164
  48.0 5.8 %collective-permute-start.1 = (f32[40,128]{1,0:T(8,128)S(1)}, f32[40,128]{1,0:T(8,128)S(1)}, u32[]{:S(2)}, u32[]{:S(2)}) collective-permute-start(f32[40,128]{1,0:T(8,128)S(1)} %pick.1), channel_id=1, source_target_pairs={{0,32},{16,48},{2,34},{18,50},{4,36},{20,52},{6,38},{22,54},{8,40}... | collective-permute-start | bytes 61448 | tf_op jit(solution)/shard_map/coefficients/ppermute | solution.py:35
  53.8 5.7 %collective-permute-start.2 = (f32[40,128]{1,0:T(8,128)S(1)}, f32[40,128]{1,0:T(8,128)S(1)}, u32[]{:S(2)}, u32[]{:S(2)}) collective-permute-start(f32[40,128]{1,0:T(8,128)S(1)} %add.69), channel_id=1, source_target_pairs={{0,97},{16,113},{2,99},{18,115},{4,101},{20,117},{6,103},{22,119},... | collective-permute-start | bytes 61448 | tf_op jit(solution)/shard_map/coefficients/ppermute | solution.py:35
  59.5 8.7 %collective-permute-start.3 = (f32[40,128]{1,0:T(8,128)S(1)}, f32[40,128]{1,0:T(8,128)S(1)}, u32[]{:S(2)}, u32[]{:S(2)}) collective-permute-start(f32[40,128]{1,0:T(8,128)S(1)} %add.70), channel_id=1, source_target_pairs={{0,96},{16,112},{2,98},{18,114},{4,100},{20,116},{6,102},{22,118},... | collective-permute-start | bytes 61448 | tf_op jit(solution)/shard_map/coefficients/ppermute | solution.py:35
  69.9 18.3 %all-to-all-start.2 = ((f32[8,40,128]{2,1,0:T(8,128)}), f32[8,40,128]{2,1,0:T(8,128)S(1)}, u32[]{:S(2)}, u32[]{:S(2)}) async-start(f32[8,40,128]{2,1,0:T(8,128)} %get-tuple-element.14), calls=%async_computation.2 | async-start | bytes 327680 | tf_op jit(solution)/shard_map/coefficients_over_z/all_to_all | solution.py:39
  76.8 11.4 %collective-permute-start.4 = (s16[336,128]{1,0:T(8,128)(2,1)}, s16[336,128]{1,0:T(8,128)(2,1)S(1)}, u32[]{:S(2)}, u32[]{:S(2)}) collective-permute-start(s16[336,128]{1,0:T(8,128)(2,1)} %get-tuple-element.15), channel_id=1, source_target_pairs={{0,1},{16,17},{2,3},{18,19},{4,5},{20,21},{6,7},{22,23},{8,9},{24,... | collective-permute-start | bytes 258056 | tf_op jit(solution)/shard_map/gradient_over_y/ppermute | solution.py:35
  84.4 9.5 %copy-start.3 = (f32[1,320,128]{2,1,0:T(8,128)S(1)}, f32[1,320,128]{2,1,0:T(8,128)}, u32[]{:S(2)}) copy-start(f32[1,320,128]{2,1,0:T(8,128)} %param.10) | copy-start | bytes 491524
  84.4 15.9 %copy-start.2 = (bf16[8,8,80,128]{3,2,1,0:T(8,128)(2,1)S(1)}, bf16[8,8,80,128]{3,2,1,0:T(8,128)(2,1)}, u32[]{:S(2)}) copy-start(bf16[8,8,80,128]{3,2,1,0:T(8,128)(2,1)} %all-gather.2.cloned.1.call-done.parts_in_ref.parts_ref) | copy-start | bytes 3932164
  88.2 0.6 copy-start.4
  89.5 10.8 %all-to-all-start.3 = ((f32[8,40,128]{2,1,0:T(8,128)}), f32[8,40,128]{2,1,0:T(8,128)S(1)}, u32[]{:S(2)}, u32[]{:S(2)}) async-start(f32[8,40,128]{2,1,0:T(8,128)} %fold.1), calls=%async_computation.3 | async-start | bytes 327680 | tf_op jit(solution)/shard_map/coefficients_over_x_and_core/all_to_all | solution.py:472
  93.8 0.9 copy-start.5
Sparse Core Ops, SparseCore 0:
  43.7 29.0 all-gather.1

commit v5 on v4

--- a/solution.py
+++ b/solution.py
@@ -18,6 +18,7 @@
 small = pl.CostEstimate(flops=1, bytes_accessed=1, transcendentals=0)
 
 z_groups = [[2 * z + h for z in range(8)] for h in range(2)]
+core_groups = [[2 * i, 2 * i + 1] for i in range(16)]
 x_core_groups = [[8 * x + 2 * r + c for x in range(4) for c in range(2)] for r in range(4)]
 
 
@@ -95,12 +96,17 @@
 def coded(value):
     top = jnp.max(jnp.abs(value), axis=0, keepdims=True)
     power = jnp.clip(jnp.ceil(jnp.log2(top * (1.0 / 32000.0))), -120.0, 120.0)
-    whole = jnp.round(value * jnp.exp2(-power)).astype(jnp.int32).astype(jnp.int16)
-    return whole, jnp.broadcast_to(power.astype(jnp.int32), (16, pair)).astype(jnp.int16)
-
-
-def decoded(whole, power):
-    return whole.astype(jnp.int32).astype(f32) * jnp.exp2(power.astype(jnp.int32)[0:1, :].astype(f32))
+    whole = jnp.round(value * jnp.exp2(-power)).astype(jnp.int32)
+    place = lax.broadcasted_iota(jnp.int32, (8, pair), 0)
+    bits = ((power.astype(jnp.int32) + 128) >> place) & 1
+    return jnp.concatenate([(whole[:8] & -2) | bits, whole[8:]], axis=0).astype(jnp.int16)
+
+
+def decoded(message):
+    whole = message.astype(jnp.int32)
+    place = lax.broadcasted_iota(jnp.int32, (8, pair), 0)
+    power = jnp.sum(((whole[:8] & 1) << place).astype(f32), axis=0, keepdims=True) - 128.0
+    return whole.astype(f32) * jnp.exp2(power)
 
 
 def picked_from(tile, row_high, row_low, col_waves):
@@ -122,8 +128,7 @@
     hidden_ref, gain_ref, cot_ref, momentum_ref, message_ref, high_ref, low_ref,
     read, hidden_read, message_done, high_done, low_done,
 ):
-    lines, _, tall, _ = message_ref.shape
-    rows = tall - 16
+    lines, _, rows, _ = message_ref.shape
     features = hidden_ref.shape[1]
     spans = [slice(line * 2 * rows, (line + 1) * 2 * rows) for line in range(lines)]
     reads = [
@@ -161,7 +166,7 @@
         term = dot(normed, cot, ((0,), (0,)))
         for half in range(2):
             own = term[half * rows : (half + 1) * rows]
-            message_ref[line, half, 0:rows, :], message_ref[line, half, rows:tall, :] = coded(own)
+            message_ref[line, half] = coded(own)
         high_ref[line], low_ref[line] = split2(dot(cot, normed, ((0,), (0,))))
         for source, target, done in (
             (message_ref, message_out_ref, message_done),
@@ -179,7 +184,7 @@
     lines, rows = owners // 2, features // owners
     ins = (hidden, gain, cot, momentum)
     outs = (
-        pltpu.HBM((lines, 2, rows + 16, pair), jnp.int16),
+        pltpu.HBM((lines, 2, rows, pair), jnp.int16),
         pltpu.HBM((lines, pair, 2 * rows), bf16),
         pltpu.HBM((lines, pair, 2 * rows), bf16),
     )
@@ -194,6 +199,28 @@
         cost_estimate=small,
         name="front",
     )(table, spots, *[from_hbm(value) for value in ins])
+
+
+def pack_kernel(upper_ref, mine_ref, other_ref, out_ref):
+    eighth = mine_ref.shape[0] - 16
+    mine, other = mine_ref[...].astype(f32), other_ref[...].astype(f32)
+    first = upper_ref[0] == 0
+    low = jnp.where(first, mine[:eighth], other[:eighth])
+    high = jnp.where(first, other[:eighth], mine[:eighth])
+    packed = jnp.concatenate([low, high, mine[eighth:] + other[eighth:]], axis=0).astype(bf16)
+    for target in range(out_ref.shape[0]):
+        out_ref[target] = packed
+
+
+def pack(upper, mine, other):
+    return pl.pallas_call(
+        pack_kernel,
+        out_shape=jax.ShapeDtypeStruct((8, 2 * mine.shape[0] - 16, pair), bf16),
+        in_specs=[in_smem, in_vmem, in_vmem],
+        compiler_params=kernel_room,
+        cost_estimate=small,
+        name="pack",
+    )(upper[None], mine, other)
 
 
 def line_spots(spots_ref, line, tiles):
@@ -245,17 +272,16 @@
 
 
 def middle_kernel(upper_ref, message_ref, total_ref, own_ref, rest_out_ref, spread_ref, rest_ref, rest_done):
-    sources, halves, tall, _ = message_ref.shape
-    rows = own_ref.shape[0]
+    sources, halves, _, _ = message_ref.shape
     sums = []
     for half in range(halves):
         term = jnp.zeros(own_ref.shape, f32)
         for source in range(sources):
-            term += decoded(message_ref[source, half, 0:rows, :], message_ref[source, half, rows:tall, :])
+            term += decoded(message_ref[source, half])
         sums.append(term)
     first = upper_ref[0] == 0
     own_ref[...] = jnp.where(first, sums[0], sums[1])
-    rest_ref[0:rows, :], rest_ref[rows:tall, :] = coded(jnp.where(first, sums[1], sums[0]))
+    rest_ref[...] = coded(jnp.where(first, sums[1], sums[0]))
     copy = pltpu.make_async_copy(rest_ref, rest_out_ref, rest_done)
     copy.start()
     for source in range(sources):
@@ -264,16 +290,16 @@
 
 
 def middle(message, upper, total):
-    sources, _, tall, _ = message.shape
+    sources, _, rows, _ = message.shape
     return pl.pallas_call(
         middle_kernel,
         out_shape=(
-            jax.ShapeDtypeStruct((tall - 16, pair), f32),
-            pltpu.HBM((tall, pair), jnp.int16),
+            jax.ShapeDtypeStruct((rows, pair), f32),
+            pltpu.HBM((rows, pair), jnp.int16),
             jax.ShapeDtypeStruct((sources,) + total.shape, f32),
         ),
         out_specs=(in_vmem, in_hbm, in_vmem),
-        scratch_shapes=[pltpu.VMEM((tall, pair), jnp.int16), pltpu.SemaphoreType.DMA],
+        scratch_shapes=[pltpu.VMEM((rows, pair), jnp.int16), pltpu.SemaphoreType.DMA],
         in_specs=[in_smem, in_vmem, in_vmem],
         compiler_params=kernel_room,
         cost_estimate=small,
@@ -285,7 +311,7 @@
     rows = out_ref.shape[0]
     row_high, row_low, col_waves = waves(table_ref[...], spots_ref[...])
     total = decay_rate * momentum_ref[...] + sum_ref[...]
-    mid_ref[0:rows, :] = total + decoded(rest_ref[0:rows, :], rest_ref[rows:, :])
+    mid_ref[0:rows, :] = total + decoded(rest_ref[...])
     mid_ref[rows:, :] = jnp.zeros((mid_ref.shape[0] - rows, pair), f32)
     for q in range(mid_ref.shape[0] // pair):
         at = slice(q * pair, (q + 1) * pair)
@@ -307,37 +333,33 @@
     )(table, spots, own_sum, rest, momentum)
 
 
-def fold_kernel(parts_ref, _, __, out_ref):
+def fold_kernel(parts_ref, _, out_ref):
     total = parts_ref[0]
     for part in range(1, parts_ref.shape[0]):
         total += parts_ref[part]
-    for target in range(out_ref.shape[0]):
-        out_ref[target] = total
-
-
-def fold(parts, *after):
+    out_ref[...] = total
+
+
+def fold(parts, after):
     return pl.pallas_call(
         fold_kernel,
-        out_shape=jax.ShapeDtypeStruct((8,) + parts.shape[1:], f32),
-        in_specs=[in_vmem, in_hbm, in_hbm],
+        out_shape=jax.ShapeDtypeStruct(parts.shape[1:], f32),
+        in_specs=[in_vmem, in_hbm],
         compiler_params=kernel_room,
         cost_estimate=small,
         name="fold",
-    )(parts, *[from_hbm(value) for value in after])
+    )(parts, from_hbm(after))
 
 
 def weight_rows(parts_ref, line):
     parts = [parts_ref[part, line].astype(f32) for part in range(parts_ref.shape[0])]
-    eighth = parts[0].shape[0] // 2
-    return jnp.concatenate([p[:eighth] for p in parts] + [p[eighth:] for p in parts], axis=0)
-
-
-def weight_kernel(nodes, table_ref, spots_ref, total_ref, parts_ref, out_ref):
+    eighth = (parts[0].shape[0] - 16) // 2
+    return jnp.concatenate([p[:eighth] for p in parts] + [p[eighth : 2 * eighth] for p in parts], axis=0)
+
+
+def weight_kernel(nodes, table_ref, spots_ref, total_ref, other_ref, parts_ref, out_ref):
     lines = spots_ref.shape[0]
-    total = total_ref[0]
-    for part in range(1, total_ref.shape[0]):
-        total += total_ref[part]
-    total = total / nodes
+    total = (total_ref[...] + other_ref[...]) / nodes
     each = total.shape[0] // lines
     table = table_ref[...]
     for line in range(lines):
@@ -352,14 +374,14 @@
             out_ref[q * pair : (q + 1) * pair, :] = fresh.astype(bf16)
 
 
-def new_weight_of(table, spots, total, parts, nodes):
+def new_weight_of(table, spots, total, other, parts, nodes):
     return pl.pallas_call(
         functools.partial(weight_kernel, nodes),
-        out_shape=jax.ShapeDtypeStruct((total.shape[1] * pair, pair), bf16),
+        out_shape=jax.ShapeDtypeStruct((total.shape[0] * pair, pair), bf16),
         compiler_params=kernel_room,
         cost_estimate=small,
         name="weight_step",
-    )(table, spots, total, parts)
+    )(table, spots, total, other, parts)
 
 
 def input_kernel(
@@ -428,36 +450,31 @@
             jnp.zeros((8 * pair,), jnp.int32), spots.reshape(-1), (upper * blocks,)
         ).reshape(8, pair)
         piece = jnp.concatenate([piece, at_half(row_of).astype(bf16), at_half(col_of).astype(bf16)], axis=0)
-    with jax.named_scope("weight_over_z"):
-        gathered = over_z(jnp.broadcast_to(piece[None], (8,) + piece.shape))
+    with jax.named_scope("weight_over_y"):
+        other = hop(piece, lambda x, y, z, c: (x, (y + (2 if y in (2, 3, 6, 7) else 6)) % 8, z, c))
 
     spare = (-blocks) % pair
     tiles = (blocks + spare) // pair
     own_spots = jnp.stack([row_of.reshape(-1), col_of.reshape(-1)])
     own_spots = jnp.pad(own_spots, ((0, 0), (0, spare))).reshape(2 * tiles, pair)
     own_momentum = momentum[0]
-    message, high, low, decayed = front(
-        table, own_spots, hidden, gain[None, :], cotangent, own_momentum, owners
-    )
+    with jax.named_scope("weight_over_z"):
+        gathered = over_z(pack(upper, piece, other))
+
+    message, high, low, decayed = front(table, own_spots, hidden, gain[None, :], cotangent, own_momentum, owners)
     decayed = lax.dynamic_update_slice(
         jnp.zeros((owners * blocks,), f32), decayed.reshape(-1)[:blocks], (local * blocks,)
     ).reshape(-1, pair)
-
     with jax.named_scope("gradient_exchange"):
         arrived = over_z(message)
 
-    with jax.named_scope("weight_over_y"):
-        other = hop(gathered, lambda x, y, z, c: (x, (y + (2 if y in (2, 3, 6, 7) else 6)) % 8, z, c))
-        spots = gathered[:, eighth:] + other[:, eighth:]
-        mine, other = gathered[:, None, :eighth], other[:, None, :eighth]
-        pieces = jnp.where(upper == 0, jnp.concatenate([mine, other], 1), jnp.concatenate([other, mine], 1))
-        pieces = pieces.reshape(8, 2 * eighth, head)
-
-    total = pick(table, spots, high, low, decayed)
+    total = pick(table, gathered, high, low, decayed)
     with jax.named_scope("coefficients"):
+        total = jnp.sum(lax.all_gather(total, "node", axis_index_groups=core_groups), axis=0)
         total = total + hop(total, lambda x, y, z, c: (x, y ^ 1, z, c))
         total = total + hop(total, lambda x, y, z, c: (x, ((y + 1) ^ 1) - 1, z, c))
         total = total + hop(total, lambda x, y, z, c: (x, y ^ 3 if y in (0, 3, 4, 7) else 7 - y, z, c))
+        total = total + hop(total, lambda x, y, z, c: (x ^ 1, y, z, c))
     own_sum, rest, spread = middle(arrived, upper, total)
     with jax.named_scope("coefficients_over_z"):
         totals = over_z(spread)
@@ -465,13 +482,14 @@
         rest = hop(rest, lambda x, y, z, c: (x, (y + 4) % 8, z, c))
 
     with jax.named_scope("weight_over_x_and_core"):
-        parts = lax.all_gather(pieces, "node", axis_index_groups=x_core_groups)
+        parts = lax.all_gather(gathered, "node", axis_index_groups=x_core_groups)
 
     input_grad = input_grad_of(hidden, gain[None, :], cotangent, parts)
-    with jax.named_scope("coefficients_over_x_and_core"):
-        totals = lax.all_to_all(fold(totals, rest, input_grad), "node", 0, 0, axis_index_groups=x_core_groups)
+    with jax.named_scope("coefficients_over_x"):
+        totals = fold(totals, input_grad)
+        others = hop(totals, lambda x, y, z, c: (((x + 1) ^ 1) - 1, y, z, c))
     new_momentum = new_momentum_of(table, own_spots, own_sum, rest, own_momentum)[None]
-    new_weight = new_weight_of(table, spots, totals, parts, nodes)
+    new_weight = new_weight_of(table, gathered, totals, others, parts, nodes)
     return (new_weight, new_momentum, input_grad)
 
 

time: 112 us -> 118 us (1.054)
  the two profiles are of different devices: /device:TPU:48 before, /device:TPU:6 now
where the time goes in v5:
time: 118 us; the launch traced here: 117 us
  starting transfers between devices  53.8 us (46%)
  waiting for transfers between devices  23.1 us (20%)
  Pallas kernels  21.6 us (18%)
  between operations  14.3 us (12%)
  blocking collectives  1.97 us (2%)
  local copies, waits for them, and re-layouts  1.62 us (1%)
    ppermute x7, starting transfers between devices, hop(): return lax.ppermute(value, ('node', 'local'), whole_mesh(move))  32.8 us
    all_to_all x3, starting transfers between devices, over_z(): return lax.all_to_all(value, 'local', 0, 0, axis_index_groups=z_groups)  21 us
    ppermute x7, waiting for transfers between devices, hop(): return lax.ppermute(value, ('node', 'local'), whole_mesh(move))  13.5 us
    all_to_all x3, waiting for transfers between devices, over_z(): return lax.all_to_all(value, 'local', 0, 0, axis_index_groups=z_groups)  9.55 us
    pallas_call x1, Pallas kernels, front(): pl.pallas_call(front_kernel, out_shape=outs + (jax.ShapeDtypeStruct((spot...  5.01 us
    pallas_call x1, Pallas kernels, new_weight_of(): pl.pallas_call(functools.partial(weight_kernel, nodes), out_shape=jax.Sha...  4.34 us
    pallas_call x1, Pallas kernels, pick(): pl.pallas_call(pick_kernel, out_shape=jax.ShapeDtypeStruct(decayed.shape,...  4.22 us
    pallas_call x1, Pallas kernels, input_grad_of(): pl.pallas_call(input_kernel, out_shape=jax.ShapeDtypeStruct(hidden.shape,...  3.82 us
  transfers between devices with their start and end apart: 11, of which 8 were waited for; matrix products, arithmetic and copies ran while one was open for 1% of the time, Pallas kernels for 14%

profile of v5, /device:TPU:6, one launch (start us, length us, event | category | flops | bytes accessed | tf_op | source)
XLA Modules:
  0.0 117.4 jit_solution(1683886698417296620)
XLA Ops:
  8.6 6.2 %collective-permute-start = (bf16[56,128]{1,0:T(8,128)(2,1)S(1)}, bf16[56,128]{1,0:T(8,128)(2,1)S(1)}, u32[]{:S(2)}, u32[]{:S(2)}) collective-permute-start(bf16[56,128]{1,0:T(8,128)(2,1)S(1)} %pad_maximum_fusion.mine_ref), channel_id=1, source_target_pairs={{0,65},{16,81},{2,67},{18,83},{4,69},{20,85},{6,71},{22,87},{8,73}... | collective-permute-start | bytes 43016 | tf_op jit(solution)/shard_map/weight_over_y/ppermute | solution.py:36
  14.7 1.8 %collective-permute-done.other_ref = bf16[56,128]{1,0:T(8,128)(2,1)S(1)} collective-permute-done((bf16[56,128]{1,0:T(8,128)(2,1)S(1)}, bf16[56,128]{1,0:T(8,128)(2,1)S(1)}, u32[]{:S(2)}, u32[]{:S(2)}) %collective-permute-start) | collective-permute-done | bytes 14368 | tf_op jit(solution)/shard_map/weight_over_y/ppermute | solution.py:36
  17.2 10.3 %all-to-all-start = ((bf16[8,96,128]{2,1,0:T(8,128)(2,1)}), bf16[8,96,128]{2,1,0:T(8,128)(2,1)S(1)}, u32[]{:S(2)}, u32[]{:S(2)}) async-start(bf16[8,96,128]{2,1,0:T(8,128)(2,1)} %pack.1), calls=%async_computation | async-start | bytes 393216 | tf_op jit(solution)/shard_map/weight_over_z/all_to_all | solution.py:40
  27.9 9.4 %all-to-all-done.spots_ref = bf16[8,96,128]{2,1,0:T(8,128)(2,1)S(1)} async-done(((bf16[8,96,128]{2,1,0:T(8,128)(2,1)}), bf16[8,96,128]{2,1,0:T(8,128)(2,1)S(1)}, u32[]{:S(2)}, u32[]{:S(2)}) %all-to-all-start) | async-done | bytes 196640 | tf_op jit(solution)/shard_map/weight_over_z/all_to_all | solution.py:40
  38.1 5.0 %front.1 = (s16[8,2,320,128]{3,2,1,0:T(8,128)(2,1)}, bf16[8,128,640]{2,1,0:T(8,128)(2,1)}, bf16[8,128,640]{2,1,0:T(8,128)(2,1)}, f32[3,128]{1,0:T(4,128)S(1)}) custom-call(bf16[256,128]{1,0:T(8,128)(2,1)S(1)} %fusion.7.table_ref, s32[6,128]{1,0:T(8,128)S(1)} %reshape.43.spots_ref, bf16[128,5120]{1,0:T(8,128)(2,1)} %hidden_ref.1, f32[1,5120]{1,0:T(1,128)} %bitcast.20, ...), custom_call_target="tpu_custom_call" | custom-call | flops 1 | bytes 1 | tf_op jit(solution)/shard_map/front/pallas_call | solution.py:191
  43.2 3.7 %all-to-all-start.1 = ((s16[8,2,320,128]{3,2,1,0:T(8,128)(2,1)}), s16[8,2,320,128]{3,2,1,0:T(8,128)(2,1)S(1)}, u32[]{:S(2)}, u32[]{:S(2)}) async-start(s16[8,2,320,128]{3,2,1,0:T(8,128)(2,1)} %get-tuple-element.10), calls=%async_computation.1 | async-start | bytes 2621440 | tf_op jit(solution)/shard_map/gradient_exchange/all_to_all | solution.py:40
  47.0 4.2 %pick.1 = f32[40,128]{1,0:T(8,128)S(1)} custom-call(bf16[256,128]{1,0:T(8,128)(2,1)S(1)} %fusion.7.table_ref, bf16[8,96,128]{2,1,0:T(8,128)(2,1)S(1)} %copy-done.4, bf16[8,128,640]{2,1,0:T(8,128)(2,1)} %get-tuple-element.11.high_in_ref, bf16[8,128,640]{2,1,0:T(8,128)(2,1)} %get-tuple-element.12.low_in_ref, f32[40,128]{1,0:T(8,128)S(1)} %bitcast.16), custom_call_target="tpu_custom_call" | custom-call | flops 1 | bytes 1 | tf_op jit(solution)/shard_map/pick/pallas_call | solution.py:263
  51.3 2.0 %all-gather = f32[80,128]{1,0:T(8,128)S(1)} all-gather(f32[40,128]{1,0:T(8,128)S(1)} %pick.1), channel_id=2, replica_groups={{0,16},{32,48},{64,80},{96,112},{128,144},{160,176},{192,208},{224,240}..., dimensions={0}, use_global_device_ids=true | all-gather | bytes 61440 | tf_op jit(solution)/shard_map/coefficients/all_gather | solution.py:473
  53.2 3.4 %collective-permute-start.1 = (f32[40,128]{1,0:T(8,128)S(1)}, f32[40,128]{1,0:T(8,128)S(1)}, u32[]{:S(2)}, u32[]{:S(2)}) collective-permute-start(f32[40,128]{1,0:T(8,128)S(1)} %reduce_sum.9), channel_id=1, source_target_pairs={{0,32},{16,48},{2,34},{18,50},{4,36},{20,52},{6,38},{22,54},{8,40}... | collective-permute-start | bytes 61448 | tf_op jit(solution)/shard_map/coefficients/ppermute | solution.py:36
  56.6 2.3 %collective-permute-done.1 = f32[40,128]{1,0:T(8,128)S(1)} collective-permute-done((f32[40,128]{1,0:T(8,128)S(1)}, f32[40,128]{1,0:T(8,128)S(1)}, u32[]{:S(2)}, u32[]{:S(2)}) %collective-permute-start.1) | collective-permute-done | bytes 20512 | tf_op jit(solution)/shard_map/coefficients/ppermute | solution.py:36
  58.9 5.1 %collective-permute-start.2 = (f32[40,128]{1,0:T(8,128)S(1)}, f32[40,128]{1,0:T(8,128)S(1)}, u32[]{:S(2)}, u32[]{:S(2)}) collective-permute-start(f32[40,128]{1,0:T(8,128)S(1)} %add.68), channel_id=1, source_target_pairs={{0,97},{16,113},{2,99},{18,115},{4,101},{20,117},{6,103},{22,119},... | collective-permute-start | bytes 61448 | tf_op jit(solution)/shard_map/coefficients/ppermute | solution.py:36
  64.1 1.7 %collective-permute-done.2 = f32[40,128]{1,0:T(8,128)S(1)} collective-permute-done((f32[40,128]{1,0:T(8,128)S(1)}, f32[40,128]{1,0:T(8,128)S(1)}, u32[]{:S(2)}, u32[]{:S(2)}) %collective-permute-start.2) | collective-permute-done | bytes 20512 | tf_op jit(solution)/shard_map/coefficients/ppermute | solution.py:36
  65.8 5.2 %collective-permute-start.3 = (f32[40,128]{1,0:T(8,128)S(1)}, f32[40,128]{1,0:T(8,128)S(1)}, u32[]{:S(2)}, u32[]{:S(2)}) collective-permute-start(f32[40,128]{1,0:T(8,128)S(1)} %add.69), channel_id=1, source_target_pairs={{0,96},{16,112},{2,98},{18,114},{4,100},{20,116},{6,102},{22,118},... | collective-permute-start | bytes 61448 | tf_op jit(solution)/shard_map/coefficients/ppermute | solution.py:36
  71.1 2.2 %collective-permute-done.3 = f32[40,128]{1,0:T(8,128)S(1)} collective-permute-done((f32[40,128]{1,0:T(8,128)S(1)}, f32[40,128]{1,0:T(8,128)S(1)}, u32[]{:S(2)}, u32[]{:S(2)}) %collective-permute-start.3) | collective-permute-done | bytes 20512 | tf_op jit(solution)/shard_map/coefficients/ppermute | solution.py:36
  73.3 2.7 %collective-permute-start.4 = (f32[40,128]{1,0:T(8,128)S(1)}, f32[40,128]{1,0:T(8,128)S(1)}, u32[]{:S(2)}, u32[]{:S(2)}) collective-permute-start(f32[40,128]{1,0:T(8,128)S(1)} %add.70), channel_id=1, source_target_pairs={{0,128},{16,144},{2,130},{18,146},{4,132},{20,148},{6,134},{22,150... | collective-permute-start | bytes 61448 | tf_op jit(solution)/shard_map/coefficients/ppermute | solution.py:36
  76.0 2.9 %collective-permute-done.4 = f32[40,128]{1,0:T(8,128)S(1)} collective-permute-done((f32[40,128]{1,0:T(8,128)S(1)}, f32[40,128]{1,0:T(8,128)S(1)}, u32[]{:S(2)}, u32[]{:S(2)}) %collective-permute-start.4) | collective-permute-done | bytes 20512 | tf_op jit(solution)/shard_map/coefficients/ppermute | solution.py:36
  79.1 1.8 %middle.1 = (f32[320,128]{1,0:T(8,128)S(1)}, s16[320,128]{1,0:T(8,128)(2,1)}, f32[8,40,128]{2,1,0:T(8,128)}) custom-call(s32[1]{0:T(128)} %bitcast.upper_ref, s16[8,2,320,128]{3,2,1,0:T(8,128)(2,1)S(1)} %all-to-all-done.1.message_ref, f32[40,128]{1,0:T(8,128)S(1)} %add.71.total_ref), custom_call_target="tpu_custom_call" | custom-call | flops 1 | bytes 1 | tf_op jit(solution)/shard_map/middle/pallas_call | solution.py:294
  80.9 6.9 %all-to-all-start.2 = ((f32[8,40,128]{2,1,0:T(8,128)}), f32[8,40,128]{2,1,0:T(8,128)S(1)}, u32[]{:S(2)}, u32[]{:S(2)}) async-start(f32[8,40,128]{2,1,0:T(8,128)} %get-tuple-element.14), calls=%async_computation.2 | async-start | bytes 327680 | tf_op jit(solution)/shard_map/coefficients_over_z/all_to_all | solution.py:40
  87.8 7.4 %collective-permute-start.6 = (s16[320,128]{1,0:T(8,128)(2,1)}, s16[320,128]{1,0:T(8,128)(2,1)S(1)}, u32[]{:S(2)}, u32[]{:S(2)}) collective-permute-start(s16[320,128]{1,0:T(8,128)(2,1)} %get-tuple-element.16), channel_id=1, source_target_pairs={{0,1},{16,17},{2,3},{18,19},{4,5},{20,21},{6,7},{22,23},{8,9},{24,... | collective-permute-start | bytes 245768 | tf_op jit(solution)/shard_map/gradient_over_y/ppermute | solution.py:36
  95.4 3.8 %input_gradient.1._ = bf16[128,5120]{1,0:T(8,128)(2,1)} custom-call(bf16[128,5120]{1,0:T(8,128)(2,1)S(1)} %copy-done.2, f32[1,5120]{1,0:T(1,128)} %bitcast.21, bf16[128,128]{1,0:T(8,128)(2,1)} %cot_in_ref.3, bf16[8,8,96,128]{3,2,1,0:T(8,128)(2,1)} %bitcast.12), custom_call_target="tpu_custom_call" | custom-call | flops 1 | bytes 1 | tf_op jit(solution)/shard_map/input_gradient/pallas_call | solution.py:423
  99.2 2.7 %collective-permute-start.5 = (f32[40,128]{1,0:T(8,128)S(1)}, f32[40,128]{1,0:T(8,128)S(1)}, u32[]{:S(2)}, u32[]{:S(2)}) collective-permute-start(f32[40,128]{1,0:T(8,128)S(1)} %fold.1.total_ref), channel_id=1, source_target_pairs={{0,384},{16,400},{2,386},{18,402},{4,388},{20,404},{6,390},{22,406... | collective-permute-start | bytes 61448 | tf_op jit(solution)/shard_map/coefficients_over_x/ppermute | solution.py:36
  102.0 1.7 %momentum_step.1 = f32[320,128]{1,0:T(8,128)} custom-call(bf16[256,128]{1,0:T(8,128)(2,1)S(1)} %fusion.7.table_ref, s32[6,128]{1,0:T(8,128)S(1)} %reshape.43.spots_ref, f32[320,128]{1,0:T(8,128)S(1)} %get-tuple-element.15.sum_ref, s16[320,128]{1,0:T(8,128)(2,1)S(1)} %collective-permute-done.6.rest_ref, f32[320,128]{1,0:T(8,128)S(1)} %bitcast.15), custom_call_target="tpu_custom_call" | custom-call | flops 1 | bytes 1 | tf_op jit(solution)/shard_map/momentum_step/pallas_call | solution.py:326
  103.7 2.5 %collective-permute-done.5.other_ref = f32[40,128]{1,0:T(8,128)S(1)} collective-permute-done((f32[40,128]{1,0:T(8,128)S(1)}, f32[40,128]{1,0:T(8,128)S(1)}, u32[]{:S(2)}, u32[]{:S(2)}) %collective-permute-start.5) | collective-permute-done | bytes 20512 | tf_op jit(solution)/shard_map/coefficients_over_x/ppermute | solution.py:36
  106.2 4.3 %weight_step.1 = bf16[5120,128]{1,0:T(8,128)(2,1)} custom-call(bf16[256,128]{1,0:T(8,128)(2,1)S(1)} %fusion.7.table_ref, bf16[8,96,128]{2,1,0:T(8,128)(2,1)S(1)} %copy-done.4, f32[40,128]{1,0:T(8,128)S(1)} %fold.1.total_ref, f32[40,128]{1,0:T(8,128)S(1)} %collective-permute-done.5.other_ref, bf16[8,8,96,128]{3,2,1,0:T(8,128)(2,1)S(1)} %bitcast.13), custom_call_target="tpu_custom_call" | custom-call | flops 1 | bytes 1 | tf_op jit(solution)/shard_map/weight_step/pallas_call | solution.py:378
  (45 shorter events, 3.6 us)
Async XLA Ops:
  7.2 0.9 copy-start
  8.6 8.0 %collective-permute-start = (bf16[56,128]{1,0:T(8,128)(2,1)S(1)}, bf16[56,128]{1,0:T(8,128)(2,1)S(1)}, u32[]{:S(2)}, u32[]{:S(2)}) collective-permute-start(bf16[56,128]{1,0:T(8,128)(2,1)S(1)} %pad_maximum_fusion.mine_ref), channel_id=1, source_target_pairs={{0,65},{16,81},{2,67},{18,83},{4,69},{20,85},{6,71},{22,87},{8,73}... | collective-permute-start | bytes 43016 | tf_op jit(solution)/shard_map/weight_over_y/ppermute | solution.py:36
  17.2 20.1 %all-to-all-start = ((bf16[8,96,128]{2,1,0:T(8,128)(2,1)}), bf16[8,96,128]{2,1,0:T(8,128)(2,1)S(1)}, u32[]{:S(2)}, u32[]{:S(2)}) async-start(bf16[8,96,128]{2,1,0:T(8,128)(2,1)} %pack.1), calls=%async_computation | async-start | bytes 393216 | tf_op jit(solution)/shard_map/weight_over_z/all_to_all | solution.py:40
  27.5 67.8 %all-gather.4.cloned.1.call-start = ((), (), s32[]{:S(2)}) async-start(), calls=%async_computation.3 | async-start | bytes 1769472 | tf_op jit(solution)/shard_map/weight_over_x_and_core/all_gather | solution.py:485
  37.3 0.7 copy-start.3
  43.2 3.9 %copy-start.4 = (bf16[8,96,128]{2,1,0:T(8,128)(2,1)S(1)}, bf16[8,96,128]{2,1,0:T(8,128)(2,1)}, u32[]{:S(2)}) copy-start(bf16[8,96,128]{2,1,0:T(8,128)(2,1)} %copy-done.3) | copy-start | bytes 589828
  43.2 36.0 %all-to-all-start.1 = ((s16[8,2,320,128]{3,2,1,0:T(8,128)(2,1)}), s16[8,2,320,128]{3,2,1,0:T(8,128)(2,1)S(1)}, u32[]{:S(2)}, u32[]{:S(2)}) async-start(s16[8,2,320,128]{3,2,1,0:T(8,128)(2,1)} %get-tuple-element.10), calls=%async_computation.1 | async-start | bytes 2621440 | tf_op jit(solution)/shard_map/gradient_exchange/all_to_all | solution.py:40
  51.2 44.1 %copy-start.2 = (bf16[128,5120]{1,0:T(8,128)(2,1)S(1)}, bf16[128,5120]{1,0:T(8,128)(2,1)}, u32[]{:S(2)}) copy-start(bf16[128,5120]{1,0:T(8,128)(2,1)} %hidden_ref.1) | copy-start | bytes 3932164
  53.2 5.7 %collective-permute-start.1 = (f32[40,128]{1,0:T(8,128)S(1)}, f32[40,128]{1,0:T(8,128)S(1)}, u32[]{:S(2)}, u32[]{:S(2)}) collective-permute-start(f32[40,128]{1,0:T(8,128)S(1)} %reduce_sum.9), channel_id=1, source_target_pairs={{0,32},{16,48},{2,34},{18,50},{4,36},{20,52},{6,38},{22,54},{8,40}... | collective-permute-start | bytes 61448 | tf_op jit(solution)/shard_map/coefficients/ppermute | solution.py:36
  58.9 6.9 %collective-permute-start.2 = (f32[40,128]{1,0:T(8,128)S(1)}, f32[40,128]{1,0:T(8,128)S(1)}, u32[]{:S(2)}, u32[]{:S(2)}) collective-permute-start(f32[40,128]{1,0:T(8,128)S(1)} %add.68), channel_id=1, source_target_pairs={{0,97},{16,113},{2,99},{18,115},{4,101},{20,117},{6,103},{22,119},... | collective-permute-start | bytes 61448 | tf_op jit(solution)/shard_map/coefficients/ppermute | solution.py:36
  65.8 7.5 %collective-permute-start.3 = (f32[40,128]{1,0:T(8,128)S(1)}, f32[40,128]{1,0:T(8,128)S(1)}, u32[]{:S(2)}, u32[]{:S(2)}) collective-permute-start(f32[40,128]{1,0:T(8,128)S(1)} %add.69), channel_id=1, source_target_pairs={{0,96},{16,112},{2,98},{18,114},{4,100},{20,116},{6,102},{22,118},... | collective-permute-start | bytes 61448 | tf_op jit(solution)/shard_map/coefficients/ppermute | solution.py:36
  73.3 5.7 %collective-permute-start.4 = (f32[40,128]{1,0:T(8,128)S(1)}, f32[40,128]{1,0:T(8,128)S(1)}, u32[]{:S(2)}, u32[]{:S(2)}) collective-permute-start(f32[40,128]{1,0:T(8,128)S(1)} %add.70), channel_id=1, source_target_pairs={{0,128},{16,144},{2,130},{18,146},{4,132},{20,148},{6,134},{22,150... | collective-permute-start | bytes 61448 | tf_op jit(solution)/shard_map/coefficients/ppermute | solution.py:36
  80.9 18.3 %all-to-all-start.2 = ((f32[8,40,128]{2,1,0:T(8,128)}), f32[8,40,128]{2,1,0:T(8,128)S(1)}, u32[]{:S(2)}, u32[]{:S(2)}) async-start(f32[8,40,128]{2,1,0:T(8,128)} %get-tuple-element.14), calls=%async_computation.2 | async-start | bytes 327680 | tf_op jit(solution)/shard_map/coefficients_over_z/all_to_all | solution.py:40
  87.8 14.1 %collective-permute-start.6 = (s16[320,128]{1,0:T(8,128)(2,1)}, s16[320,128]{1,0:T(8,128)(2,1)S(1)}, u32[]{:S(2)}, u32[]{:S(2)}) collective-permute-start(s16[320,128]{1,0:T(8,128)(2,1)} %get-tuple-element.16), channel_id=1, source_target_pairs={{0,1},{16,17},{2,3},{18,19},{4,5},{20,21},{6,7},{22,23},{8,9},{24,... | collective-permute-start | bytes 245768 | tf_op jit(solution)/shard_map/gradient_over_y/ppermute | solution.py:36
  95.3 6.6 %copy-start.5 = (f32[1,320,128]{2,1,0:T(8,128)S(1)}, f32[1,320,128]{2,1,0:T(8,128)}, u32[]{:S(2)}) copy-start(f32[1,320,128]{2,1,0:T(8,128)} %param.10) | copy-start | bytes 491524
  99.2 7.1 %copy-start.1 = (bf16[64,96,128]{2,1,0:T(8,128)(2,1)S(1)}, bf16[64,96,128]{2,1,0:T(8,128)(2,1)}, u32[]{:S(2)}) copy-start(bf16[64,96,128]{2,1,0:T(8,128)(2,1)} %all-gather.4.cloned.1.call-done) | copy-start | bytes 4718596
  99.2 7.0 %collective-permute-start.5 = (f32[40,128]{1,0:T(8,128)S(1)}, f32[40,128]{1,0:T(8,128)S(1)}, u32[]{:S(2)}, u32[]{:S(2)}) collective-permute-start(f32[40,128]{1,0:T(8,128)S(1)} %fold.1.total_ref), channel_id=1, source_target_pairs={{0,384},{16,400},{2,386},{18,402},{4,388},{20,404},{6,390},{22,406... | collective-permute-start | bytes 61448 | tf_op jit(solution)/shard_map/coefficients_over_x/ppermute | solution.py:36
Sparse Core Ops, SparseCore 0:
  38.1 24.1 all-gather.3

commit v6 on v5

--- a/solution.py
+++ b/solution.py
@@ -353,8 +353,8 @@
 
 def weight_rows(parts_ref, line):
     parts = [parts_ref[part, line].astype(f32) for part in range(parts_ref.shape[0])]
-    eighth = (parts[0].shape[0] - 16) // 2
-    return jnp.concatenate([p[:eighth] for p in parts] + [p[eighth : 2 * eighth] for p in parts], axis=0)
+    eighth = parts[0].shape[0] // 2
+    return jnp.concatenate([p[:eighth] for p in parts] + [p[eighth:] for p in parts], axis=0)
 
 
 def weight_kernel(nodes, table_ref, spots_ref, total_ref, other_ref, parts_ref, out_ref):
@@ -482,7 +482,7 @@
         rest = hop(rest, lambda x, y, z, c: (x, (y + 4) % 8, z, c))
 
     with jax.named_scope("weight_over_x_and_core"):
-        parts = lax.all_gather(gathered, "node", axis_index_groups=x_core_groups)
+        parts = lax.all_gather(gathered[:, : 2 * eighth, :], "node", axis_index_groups=x_core_groups)
 
     input_grad = input_grad_of(hidden, gain[None, :], cotangent, parts)
     with jax.named_scope("coefficients_over_x"):

time: 118 us -> 113 us (0.958)
  waiting for transfers between devices: 23.1 us -> 17.8 us
    all_to_all x3, waiting for transfers between devices: 9.55 us -> 4.44 us  [over_z(): return lax.all_to_all(value, 'local', 0, 0, axis_index_groups=z_groups)]
  transfers between devices with their start and end apart: 11 -> 11, of which waited for: 8 -> 7; matrix products, arithmetic and copies ran while one was open for 1% -> 1% of each run, Pallas kernels for 14% -> 15%
where the time goes in v6:
time: 113 us; the launch traced here: 112 us
  starting transfers between devices  53.9 us (48%)
  Pallas kernels  21.5 us (19%)
  waiting for transfers between devices  17.8 us (16%)
  between operations  14.3 us (13%)
  blocking collectives  1.97 us (2%)
  local copies, waits for them, and re-layouts  1.63 us (1%)
    ppermute x7, starting transfers between devices, hop(): return lax.ppermute(value, ('node', 'local'), whole_mesh(move))  32.8 us
    all_to_all x3, starting transfers between devices, over_z(): return lax.all_to_all(value, 'local', 0, 0, axis_index_groups=z_groups)  21 us
    ppermute x7, waiting for transfers between devices, hop(): return lax.ppermute(value, ('node', 'local'), whole_mesh(move))  13.3 us
    pallas_call x1, Pallas kernels, front(): pl.pallas_call(front_kernel, out_shape=outs + (jax.ShapeDtypeStruct((spot...  5.01 us
    all_to_all x3, waiting for transfers between devices, over_z(): return lax.all_to_all(value, 'local', 0, 0, axis_index_groups=z_groups)  4.44 us
    pallas_call x1, Pallas kernels, new_weight_of(): pl.pallas_call(functools.partial(weight_kernel, nodes), out_shape=jax.Sha...  4.38 us
    pallas_call x1, Pallas kernels, pick(): pl.pallas_call(pick_kernel, out_shape=jax.ShapeDtypeStruct(decayed.shape,...  4.19 us
    pallas_call x1, Pallas kernels, input_grad_of(): pl.pallas_call(input_kernel, out_shape=jax.ShapeDtypeStruct(hidden.shape,...  3.68 us
  transfers between devices with their start and end apart: 11, of which 7 were waited for; matrix products, arithmetic and copies ran while one was open for 1% of the time, Pallas kernels for 15%

profile of v6, /device:TPU:6, one launch (start us, length us, event | category | flops | bytes accessed | tf_op | source)
XLA Modules:
  0.0 112.1 jit_solution(2159905487950780522)
XLA Ops:
  8.6 6.2 %collective-permute-start = (bf16[56,128]{1,0:T(8,128)(2,1)S(1)}, bf16[56,128]{1,0:T(8,128)(2,1)S(1)}, u32[]{:S(2)}, u32[]{:S(2)}) collective-permute-start(bf16[56,128]{1,0:T(8,128)(2,1)S(1)} %pad_maximum_fusion.mine_ref), channel_id=1, source_target_pairs={{0,65},{16,81},{2,67},{18,83},{4,69},{20,85},{6,71},{22,87},{8,73}... | collective-permute-start | bytes 43016 | tf_op jit(solution)/shard_map/weight_over_y/ppermute | solution.py:36
  14.9 1.6 %collective-permute-done.other_ref = bf16[56,128]{1,0:T(8,128)(2,1)S(1)} collective-permute-done((bf16[56,128]{1,0:T(8,128)(2,1)S(1)}, bf16[56,128]{1,0:T(8,128)(2,1)S(1)}, u32[]{:S(2)}, u32[]{:S(2)}) %collective-permute-start) | collective-permute-done | bytes 14368 | tf_op jit(solution)/shard_map/weight_over_y/ppermute | solution.py:36
  17.2 10.3 %all-to-all-start = ((bf16[8,96,128]{2,1,0:T(8,128)(2,1)}), bf16[8,96,128]{2,1,0:T(8,128)(2,1)S(1)}, u32[]{:S(2)}, u32[]{:S(2)}) async-start(bf16[8,96,128]{2,1,0:T(8,128)(2,1)} %pack.1), calls=%async_computation | async-start | bytes 393216 | tf_op jit(solution)/shard_map/weight_over_z/all_to_all | solution.py:40
  27.8 5.0 %front.1 = (s16[8,2,320,128]{3,2,1,0:T(8,128)(2,1)}, bf16[8,128,640]{2,1,0:T(8,128)(2,1)}, bf16[8,128,640]{2,1,0:T(8,128)(2,1)}, f32[3,128]{1,0:T(4,128)S(1)}) custom-call(bf16[256,128]{1,0:T(8,128)(2,1)S(1)} %fusion.7.table_ref, s32[6,128]{1,0:T(8,128)S(1)} %reshape.43.spots_ref, bf16[128,5120]{1,0:T(8,128)(2,1)} %hidden_ref.1, f32[1,5120]{1,0:T(1,128)} %bitcast.20, ...), custom_call_target="tpu_custom_call" | custom-call | flops 1 | bytes 1 | tf_op jit(solution)/shard_map/front/pallas_call | solution.py:191
  32.9 4.4 %all-to-all-done.spots_ref = bf16[8,96,128]{2,1,0:T(8,128)(2,1)S(1)} async-done(((bf16[8,96,128]{2,1,0:T(8,128)(2,1)}), bf16[8,96,128]{2,1,0:T(8,128)(2,1)S(1)}, u32[]{:S(2)}, u32[]{:S(2)}) %all-to-all-start) | async-done | bytes 196640 | tf_op jit(solution)/shard_map/weight_over_z/all_to_all | solution.py:40
  37.3 3.6 %all-to-all-start.1 = ((s16[8,2,320,128]{3,2,1,0:T(8,128)(2,1)}), s16[8,2,320,128]{3,2,1,0:T(8,128)(2,1)S(1)}, u32[]{:S(2)}, u32[]{:S(2)}) async-start(s16[8,2,320,128]{3,2,1,0:T(8,128)(2,1)} %get-tuple-element.10), calls=%async_computation.1 | async-start | bytes 2621440 | tf_op jit(solution)/shard_map/gradient_exchange/all_to_all | solution.py:40
  41.8 4.2 %pick.1 = f32[40,128]{1,0:T(8,128)S(1)} custom-call(bf16[256,128]{1,0:T(8,128)(2,1)S(1)} %fusion.7.table_ref, bf16[8,96,128]{2,1,0:T(8,128)(2,1)S(1)} %all-to-all-done.spots_ref, bf16[8,128,640]{2,1,0:T(8,128)(2,1)} %get-tuple-element.11.high_in_ref, bf16[8,128,640]{2,1,0:T(8,128)(2,1)} %get-tuple-element.12.low_in_ref, f32[40,128]{1,0:T(8,128)S(1)} %bitcast.16), custom_call_target="tpu_custom_call" | custom-call | flops 1 | bytes 1 | tf_op jit(solution)/shard_map/pick/pallas_call | solution.py:263
  46.0 2.0 %all-gather = f32[80,128]{1,0:T(8,128)S(1)} all-gather(f32[40,128]{1,0:T(8,128)S(1)} %pick.1), channel_id=2, replica_groups={{0,16},{32,48},{64,80},{96,112},{128,144},{160,176},{192,208},{224,240}..., dimensions={0}, use_global_device_ids=true | all-gather | bytes 61440 | tf_op jit(solution)/shard_map/coefficients/all_gather | solution.py:473
  48.0 3.4 %collective-permute-start.1 = (f32[40,128]{1,0:T(8,128)S(1)}, f32[40,128]{1,0:T(8,128)S(1)}, u32[]{:S(2)}, u32[]{:S(2)}) collective-permute-start(f32[40,128]{1,0:T(8,128)S(1)} %reduce_sum.9), channel_id=1, source_target_pairs={{0,32},{16,48},{2,34},{18,50},{4,36},{20,52},{6,38},{22,54},{8,40}... | collective-permute-start | bytes 61448 | tf_op jit(solution)/shard_map/coefficients/ppermute | solution.py:36
  51.4 2.2 %collective-permute-done.1 = f32[40,128]{1,0:T(8,128)S(1)} collective-permute-done((f32[40,128]{1,0:T(8,128)S(1)}, f32[40,128]{1,0:T(8,128)S(1)}, u32[]{:S(2)}, u32[]{:S(2)}) %collective-permute-start.1) | collective-permute-done | bytes 20512 | tf_op jit(solution)/shard_map/coefficients/ppermute | solution.py:36
  53.6 5.2 %collective-permute-start.2 = (f32[40,128]{1,0:T(8,128)S(1)}, f32[40,128]{1,0:T(8,128)S(1)}, u32[]{:S(2)}, u32[]{:S(2)}) collective-permute-start(f32[40,128]{1,0:T(8,128)S(1)} %add.68), channel_id=1, source_target_pairs={{0,97},{16,113},{2,99},{18,115},{4,101},{20,117},{6,103},{22,119},... | collective-permute-start | bytes 61448 | tf_op jit(solution)/shard_map/coefficients/ppermute | solution.py:36
  58.8 1.7 %collective-permute-done.2 = f32[40,128]{1,0:T(8,128)S(1)} collective-permute-done((f32[40,128]{1,0:T(8,128)S(1)}, f32[40,128]{1,0:T(8,128)S(1)}, u32[]{:S(2)}, u32[]{:S(2)}) %collective-permute-start.2) | collective-permute-done | bytes 20512 | tf_op jit(solution)/shard_map/coefficients/ppermute | solution.py:36
  60.5 5.2 %collective-permute-start.3 = (f32[40,128]{1,0:T(8,128)S(1)}, f32[40,128]{1,0:T(8,128)S(1)}, u32[]{:S(2)}, u32[]{:S(2)}) collective-permute-start(f32[40,128]{1,0:T(8,128)S(1)} %add.69), channel_id=1, source_target_pairs={{0,96},{16,112},{2,98},{18,114},{4,100},{20,116},{6,102},{22,118},... | collective-permute-start | bytes 61448 | tf_op jit(solution)/shard_map/coefficients/ppermute | solution.py:36
  65.8 2.2 %collective-permute-done.3 = f32[40,128]{1,0:T(8,128)S(1)} collective-permute-done((f32[40,128]{1,0:T(8,128)S(1)}, f32[40,128]{1,0:T(8,128)S(1)}, u32[]{:S(2)}, u32[]{:S(2)}) %collective-permute-start.3) | collective-permute-done | bytes 20512 | tf_op jit(solution)/shard_map/coefficients/ppermute | solution.py:36
  68.0 2.7 %collective-permute-start.4 = (f32[40,128]{1,0:T(8,128)S(1)}, f32[40,128]{1,0:T(8,128)S(1)}, u32[]{:S(2)}, u32[]{:S(2)}) collective-permute-start(f32[40,128]{1,0:T(8,128)S(1)} %add.70), channel_id=1, source_target_pairs={{0,128},{16,144},{2,130},{18,146},{4,132},{20,148},{6,134},{22,150... | collective-permute-start | bytes 61448 | tf_op jit(solution)/shard_map/coefficients/ppermute | solution.py:36
  70.7 2.9 %collective-permute-done.4 = f32[40,128]{1,0:T(8,128)S(1)} collective-permute-done((f32[40,128]{1,0:T(8,128)S(1)}, f32[40,128]{1,0:T(8,128)S(1)}, u32[]{:S(2)}, u32[]{:S(2)}) %collective-permute-start.4) | collective-permute-done | bytes 20512 | tf_op jit(solution)/shard_map/coefficients/ppermute | solution.py:36
  73.7 1.8 %middle.1 = (f32[320,128]{1,0:T(8,128)S(1)}, s16[320,128]{1,0:T(8,128)(2,1)}, f32[8,40,128]{2,1,0:T(8,128)}) custom-call(s32[1]{0:T(128)} %bitcast.upper_ref, s16[8,2,320,128]{3,2,1,0:T(8,128)(2,1)S(1)} %all-to-all-done.1.message_ref, f32[40,128]{1,0:T(8,128)S(1)} %add.71.total_ref), custom_call_target="tpu_custom_call" | custom-call | flops 1 | bytes 1 | tf_op jit(solution)/shard_map/middle/pallas_call | solution.py:294
  75.5 7.1 %all-to-all-start.2 = ((f32[8,40,128]{2,1,0:T(8,128)}), f32[8,40,128]{2,1,0:T(8,128)S(1)}, u32[]{:S(2)}, u32[]{:S(2)}) async-start(f32[8,40,128]{2,1,0:T(8,128)} %get-tuple-element.14), calls=%async_computation.2 | async-start | bytes 327680 | tf_op jit(solution)/shard_map/coefficients_over_z/all_to_all | solution.py:40
  82.6 7.5 %collective-permute-start.6 = (s16[320,128]{1,0:T(8,128)(2,1)}, s16[320,128]{1,0:T(8,128)(2,1)S(1)}, u32[]{:S(2)}, u32[]{:S(2)}) collective-permute-start(s16[320,128]{1,0:T(8,128)(2,1)} %get-tuple-element.16), channel_id=1, source_target_pairs={{0,1},{16,17},{2,3},{18,19},{4,5},{20,21},{6,7},{22,23},{8,9},{24,... | collective-permute-start | bytes 245768 | tf_op jit(solution)/shard_map/gradient_over_y/ppermute | solution.py:36
  90.1 3.7 %input_gradient.1._ = bf16[128,5120]{1,0:T(8,128)(2,1)} custom-call(bf16[128,5120]{1,0:T(8,128)(2,1)S(1)} %copy-done.1, f32[1,5120]{1,0:T(1,128)} %bitcast.21, bf16[128,128]{1,0:T(8,128)(2,1)} %cot_in_ref.3, bf16[8,8,80,128]{3,2,1,0:T(8,128)(2,1)} %bitcast.12), custom_call_target="tpu_custom_call" | custom-call | flops 1 | bytes 1 | tf_op jit(solution)/shard_map/input_gradient/pallas_call | solution.py:423
  93.8 2.7 %collective-permute-start.5 = (f32[40,128]{1,0:T(8,128)S(1)}, f32[40,128]{1,0:T(8,128)S(1)}, u32[]{:S(2)}, u32[]{:S(2)}) collective-permute-start(f32[40,128]{1,0:T(8,128)S(1)} %fold.1.total_ref), channel_id=1, source_target_pairs={{0,384},{16,400},{2,386},{18,402},{4,388},{20,404},{6,390},{22,406... | collective-permute-start | bytes 61448 | tf_op jit(solution)/shard_map/coefficients_over_x/ppermute | solution.py:36
  96.6 1.7 %momentum_step.1 = f32[320,128]{1,0:T(8,128)} custom-call(bf16[256,128]{1,0:T(8,128)(2,1)S(1)} %fusion.7.table_ref, s32[6,128]{1,0:T(8,128)S(1)} %reshape.43.spots_ref, f32[320,128]{1,0:T(8,128)S(1)} %get-tuple-element.15.sum_ref, s16[320,128]{1,0:T(8,128)(2,1)S(1)} %collective-permute-done.6.rest_ref, f32[320,128]{1,0:T(8,128)S(1)} %bitcast.15), custom_call_target="tpu_custom_call" | custom-call | flops 1 | bytes 1 | tf_op jit(solution)/shard_map/momentum_step/pallas_call | solution.py:326
  98.3 2.6 %collective-permute-done.5.other_ref = f32[40,128]{1,0:T(8,128)S(1)} collective-permute-done((f32[40,128]{1,0:T(8,128)S(1)}, f32[40,128]{1,0:T(8,128)S(1)}, u32[]{:S(2)}, u32[]{:S(2)}) %collective-permute-start.5) | collective-permute-done | bytes 20512 | tf_op jit(solution)/shard_map/coefficients_over_x/ppermute | solution.py:36
  100.9 4.4 %weight_step.1 = bf16[5120,128]{1,0:T(8,128)(2,1)} custom-call(bf16[256,128]{1,0:T(8,128)(2,1)S(1)} %fusion.7.table_ref, bf16[8,96,128]{2,1,0:T(8,128)(2,1)S(1)} %all-to-all-done.spots_ref, f32[40,128]{1,0:T(8,128)S(1)} %fold.1.total_ref, f32[40,128]{1,0:T(8,128)S(1)} %collective-permute-done.5.other_ref, bf16[8,8,80,128]{3,2,1,0:T(8,128)(2,1)S(1)} %bitcast.13), custom_call_target="tpu_custom_call" | custom-call | flops 1 | bytes 1 | tf_op jit(solution)/shard_map/weight_step/pallas_call | solution.py:378
  (42 shorter events, 3.4 us)
Async XLA Ops:
  7.2 0.9 copy-start
  8.6 8.0 %collective-permute-start = (bf16[56,128]{1,0:T(8,128)(2,1)S(1)}, bf16[56,128]{1,0:T(8,128)(2,1)S(1)}, u32[]{:S(2)}, u32[]{:S(2)}) collective-permute-start(bf16[56,128]{1,0:T(8,128)(2,1)S(1)} %pad_maximum_fusion.mine_ref), channel_id=1, source_target_pairs={{0,65},{16,81},{2,67},{18,83},{4,69},{20,85},{6,71},{22,87},{8,73}... | collective-permute-start | bytes 43016 | tf_op jit(solution)/shard_map/weight_over_y/ppermute | solution.py:36
  17.2 20.1 %all-to-all-start = ((bf16[8,96,128]{2,1,0:T(8,128)(2,1)}), bf16[8,96,128]{2,1,0:T(8,128)(2,1)S(1)}, u32[]{:S(2)}, u32[]{:S(2)}) async-start(bf16[8,96,128]{2,1,0:T(8,128)(2,1)} %pack.1), calls=%async_computation | async-start | bytes 393216 | tf_op jit(solution)/shard_map/weight_over_z/all_to_all | solution.py:40
  37.3 36.4 %all-to-all-start.1 = ((s16[8,2,320,128]{3,2,1,0:T(8,128)(2,1)}), s16[8,2,320,128]{3,2,1,0:T(8,128)(2,1)S(1)}, u32[]{:S(2)}, u32[]{:S(2)}) async-start(s16[8,2,320,128]{3,2,1,0:T(8,128)(2,1)} %get-tuple-element.10), calls=%async_computation.1 | async-start | bytes 2621440 | tf_op jit(solution)/shard_map/gradient_exchange/all_to_all | solution.py:40
  40.9 49.2 %all-gather.4.cloned.1.call-start = ((), (), s32[]{:S(2)}) async-start(), calls=%async_computation.3 | async-start | bytes 1474560 | tf_op jit(solution)/shard_map/weight_over_x_and_core/all_gather | solution.py:485
  46.0 44.1 %copy-start.1 = (bf16[128,5120]{1,0:T(8,128)(2,1)S(1)}, bf16[128,5120]{1,0:T(8,128)(2,1)}, u32[]{:S(2)}) copy-start(bf16[128,5120]{1,0:T(8,128)(2,1)} %hidden_ref.1) | copy-start | bytes 3932164
  48.0 5.7 %collective-permute-start.1 = (f32[40,128]{1,0:T(8,128)S(1)}, f32[40,128]{1,0:T(8,128)S(1)}, u32[]{:S(2)}, u32[]{:S(2)}) collective-permute-start(f32[40,128]{1,0:T(8,128)S(1)} %reduce_sum.9), channel_id=1, source_target_pairs={{0,32},{16,48},{2,34},{18,50},{4,36},{20,52},{6,38},{22,54},{8,40}... | collective-permute-start | bytes 61448 | tf_op jit(solution)/shard_map/coefficients/ppermute | solution.py:36
  53.6 6.9 %collective-permute-start.2 = (f32[40,128]{1,0:T(8,128)S(1)}, f32[40,128]{1,0:T(8,128)S(1)}, u32[]{:S(2)}, u32[]{:S(2)}) collective-permute-start(f32[40,128]{1,0:T(8,128)S(1)} %add.68), channel_id=1, source_target_pairs={{0,97},{16,113},{2,99},{18,115},{4,101},{20,117},{6,103},{22,119},... | collective-permute-start | bytes 61448 | tf_op jit(solution)/shard_map/coefficients/ppermute | solution.py:36
  60.5 7.5 %collective-permute-start.3 = (f32[40,128]{1,0:T(8,128)S(1)}, f32[40,128]{1,0:T(8,128)S(1)}, u32[]{:S(2)}, u32[]{:S(2)}) collective-permute-start(f32[40,128]{1,0:T(8,128)S(1)} %add.69), channel_id=1, source_target_pairs={{0,96},{16,112},{2,98},{18,114},{4,100},{20,116},{6,102},{22,118},... | collective-permute-start | bytes 61448 | tf_op jit(solution)/shard_map/coefficients/ppermute | solution.py:36
  68.0 5.7 %collective-permute-start.4 = (f32[40,128]{1,0:T(8,128)S(1)}, f32[40,128]{1,0:T(8,128)S(1)}, u32[]{:S(2)}, u32[]{:S(2)}) collective-permute-start(f32[40,128]{1,0:T(8,128)S(1)} %add.70), channel_id=1, source_target_pairs={{0,128},{16,144},{2,130},{18,146},{4,132},{20,148},{6,134},{22,150... | collective-permute-start | bytes 61448 | tf_op jit(solution)/shard_map/coefficients/ppermute | solution.py:36
  75.5 18.3 %all-to-all-start.2 = ((f32[8,40,128]{2,1,0:T(8,128)}), f32[8,40,128]{2,1,0:T(8,128)S(1)}, u32[]{:S(2)}, u32[]{:S(2)}) async-start(f32[8,40,128]{2,1,0:T(8,128)} %get-tuple-element.14), calls=%async_computation.2 | async-start | bytes 327680 | tf_op jit(solution)/shard_map/coefficients_over_z/all_to_all | solution.py:40
  82.6 14.0 %collective-permute-start.6 = (s16[320,128]{1,0:T(8,128)(2,1)}, s16[320,128]{1,0:T(8,128)(2,1)S(1)}, u32[]{:S(2)}, u32[]{:S(2)}) collective-permute-start(s16[320,128]{1,0:T(8,128)(2,1)} %get-tuple-element.16), channel_id=1, source_target_pairs={{0,1},{16,17},{2,3},{18,19},{4,5},{20,21},{6,7},{22,23},{8,9},{24,... | collective-permute-start | bytes 245768 | tf_op jit(solution)/shard_map/gradient_over_y/ppermute | solution.py:36
  93.8 2.8 %copy-start.3 = (f32[1,320,128]{2,1,0:T(8,128)S(1)}, f32[1,320,128]{2,1,0:T(8,128)}, u32[]{:S(2)}) copy-start(f32[1,320,128]{2,1,0:T(8,128)} %param.10) | copy-start | bytes 491524
  93.8 7.1 %copy-start.2 = (bf16[64,80,128]{2,1,0:T(8,128)(2,1)S(1)}, bf16[64,80,128]{2,1,0:T(8,128)(2,1)}, u32[]{:S(2)}) copy-start(bf16[64,80,128]{2,1,0:T(8,128)(2,1)} %all-gather.4.cloned.1.call-done) | copy-start | bytes 3932164
  93.8 7.0 %collective-permute-start.5 = (f32[40,128]{1,0:T(8,128)S(1)}, f32[40,128]{1,0:T(8,128)S(1)}, u32[]{:S(2)}, u32[]{:S(2)}) collective-permute-start(f32[40,128]{1,0:T(8,128)S(1)} %fold.1.total_ref), channel_id=1, source_target_pairs={{0,384},{16,400},{2,386},{18,402},{4,388},{20,404},{6,390},{22,406... | collective-permute-start | bytes 61448 | tf_op jit(solution)/shard_map/coefficients_over_x/ppermute | solution.py:36
Sparse Core Ops, SparseCore 0:
  43.8 28.9 all-gather.3
